TPU v7x, 32 devices: a whole 2x2x4 slice. The times are simulated.
32 devices in a mesh: parts: 2 (over y), expert: 8 (over z, x), tile: 2 (over core).
Axes of the slice: x: 2, y: 2, z: 4, core: 2. Of those that a mesh axis runs over, the one named last changes fastest.
Arguments:
- tokens: bfloat16 [512, 3072], P(('parts', 'expert', 'tile')), parts along dimension 0, may hold values from -6 to 6
- routes: int32 [512, 2], P(('parts', 'expert', 'tile')), parts along dimension 0, may hold values from 0 to 3, all different within a row; in each aligned block of 16 rows (0 to 15, 16 to 31, ...) at most 8 rows name the same one
- route_weights: bfloat16 [512, 2], P(('parts', 'expert', 'tile')), parts along dimension 0, may hold values from 0.099609375 to 1
- gate_proj: bfloat16 [8, 3072, 4096], P('expert', None, 'tile'), may hold values from -0.109375 to 0.109375
- up_proj: bfloat16 [8, 3072, 4096], P('expert', None, 'tile'), may hold values from -0.109375 to 0.109375
- down_proj: bfloat16 [8, 4096, 3072], P('expert', 'tile'), may hold values from -0.0625 to 0.0625
Outputs:
- mixed_out: bfloat16 [512, 3072], P(('parts', 'expert', 'tile')), parts along dimension 0
There are 2 independent parts, one for each index of `parts`. A program takes and returns all parts, laid end to end along the dimension named above; an argument that names none is the same for every part. Nothing has to cross between parts.
Inputs may be any that keep to these rules, and one draw needn't show every extreme that they name: `routes`: each row names two different experts; in each aligned block of 16 rows (the rows of one device) no expert is named by more than 8 rows, a bound that some block reaches.
All inputs are finite; a program needn't handle non-finite values.
Results may differ from a plain program's by a relative error of at most 0.009.
Values may be sent and summed in bfloat16 or wider, within the bound.
No kernel may reach another device: no remote copies, remote signals or barrier semaphores. Data moves between devices by JAX's collectives and lax.ppermute only.
A program may use at most 128 MiB of HBM per device.

v0:
```python
import jax
import jax.numpy as jnp
from jax import lax
from jax.sharding import PartitionSpec as P


def slot_tables(route_blocks, group_count, capacity):
    blocks = route_blocks.shape[0]
    entries = route_blocks.shape[1] * route_blocks.shape[2]
    flattened = route_blocks.reshape(blocks, entries)
    equal_ids = flattened[:, :, None] == flattened[:, None, :]
    earlier = lax.broadcasted_iota(jnp.int32, (entries, entries), 0) < lax.broadcasted_iota(
        jnp.int32, (entries, entries), 1
    )
    positions = jnp.sum((equal_ids & earlier[None]).astype(jnp.int32), axis=1).reshape(
        route_blocks.shape
    )
    owners = lax.broadcasted_iota(jnp.int32, (group_count,), 0) // 2
    matches = (route_blocks[..., None] == owners).astype(jnp.float32)
    slot_ids = lax.broadcasted_iota(jnp.int32, (capacity,), 0)
    placed = (positions[..., None] == slot_ids).astype(jnp.float32)
    return (matches, placed)


def shards(tokens, routes, route_weights, gate_proj, up_proj, down_proj):
    group_count = lax.axis_size("expert")
    expert_count = group_count // 2
    row_count = tokens.shape[0]
    feature = tokens.shape[1]
    capacity = max(2, 2 * row_count // expert_count)
    gate_local = gate_proj[0]
    up_local = up_proj[0]
    down_local = down_proj[0]
    matches, placed = slot_tables(routes[None], group_count, capacity)
    selector = jnp.einsum("brkg,brkc->bgcr", matches, placed)[0].astype(jnp.bfloat16)
    outgoing = jnp.einsum(
        "gcr,rd->gcd", selector, tokens, preferred_element_type=jnp.float32
    ).astype(jnp.bfloat16)
    received = lax.all_to_all(outgoing, "expert", split_axis=0, concat_axis=0, tiled=True)
    flattened = received.reshape(group_count * capacity, feature)
    block_rows = lax.all_gather(flattened, "tile", axis=0, tiled=True)
    gate_pre = jnp.dot(block_rows, gate_local, preferred_element_type=jnp.float32)
    up_pre = jnp.dot(block_rows, up_local, preferred_element_type=jnp.float32)
    hidden = (jax.nn.silu(gate_pre) * up_pre).astype(jnp.bfloat16)
    slot_sums = lax.psum_scatter(
        jnp.dot(hidden, down_local, preferred_element_type=jnp.float32).astype(jnp.bfloat16),
        "tile",
        scatter_dimension=0,
        tiled=True,
    ).astype(jnp.float32)
    returned = lax.all_to_all(
        slot_sums.reshape(group_count, capacity, feature).astype(jnp.bfloat16),
        "expert",
        split_axis=0,
        concat_axis=0,
        tiled=True,
    ).astype(jnp.float32)
    weighting = route_weights.astype(jnp.float32)
    combiner = jnp.einsum("brkg,brkc,brk->brgc", matches, placed, weighting[None])[0]
    mixed_out = jnp.einsum("rgc,gcd->rd", combiner, returned, precision=lax.Precision.HIGHEST)
    return mixed_out.astype(jnp.bfloat16)


def solution(mesh):
    placed = (
        P(("parts", "expert", "tile"), None),
        P(("parts", "expert", "tile"), None),
        P(("parts", "expert", "tile"), None),
        P("expert", None, "tile"),
        P("expert", None, "tile"),
        P("expert", "tile", None),
    )
    return jax.shard_map(
        shards,
        mesh=mesh,
        in_specs=placed,
        out_specs=P(("parts", "expert", "tile"), None),
        check_vma=False,
    )
```

profile of v0, /device:TPU:0, one launch (start us, length us, event | category | flops | bytes accessed | tf_op | source)
XLA Modules:
  0.0 82.4 jit_solution(8247440108377973562)
XLA Ops:
  6.5 0.0 copy-start
  6.5 0.0 reduce-scatter.2.cloned.1.call-start
  6.5 0.8 copy.23
  7.3 0.1 eq.62
  7.4 0.1 convert_reduce_fusion
  7.5 0.1 eq.66
  7.6 0.3 fusion.16
  7.9 0.1 copy.26
  8.0 0.0 copy-done
  8.0 0.2 convolution_convert_fusion
  8.3 19.2 %all_to_all.10 = bf16[8,8,3072]{2,1,0:T(8,128)(2,1)S(1)} all-to-all(bf16[8,8,3072]{2,1,0:T(8,128)(2,1)S(1)} %convolution_convert_fusion), channel_id=1, replica_groups=mesh['parts'=2,'expert'=8,'tile'=2] {'expert'}, dimensions={0} | all-to-all | bytes 786432 | tf_op jit(solution)/shard_map/all_to_all | solution.py:39
  27.4 2.4 %all_gather.3 = bf16[128,3072]{1,0:T(8,128)(2,1)S(1)} all-gather(bf16[64,3072]{1,0:T(8,128)(2,1)S(1)} %bitcast.36), channel_id=1, replica_groups=mesh['parts'=2,'expert'=8,'tile'=2] {'tile'}, dimensions={0}, use_global_device_ids=true | all-gather | bytes 1179648 | tf_op jit(solution)/shard_map/all_gather | solution.py:41
  29.8 6.4 %fusion.4 = f32[128,2048]{1,0:T(8,128)S(1)} fusion(bf16[128,3072]{1,0:T(8,128)(2,1)S(1)} %all_gather.3, bf16[1,3072,2048]{2,1,0:T(8,128)(2,1)} %param.9), kind=kOutput, calls=%fused_computation.4 | convolution fusion | flops 1610612736 | bytes 14417920 | tf_op jit(solution)/shard_map/dot_general | solution.py:42
  36.2 0.0 copy-start.1
  36.2 12.9 %fusion.6 = bf16[128,3072]{1,0:T(8,128)(2,1)} fusion(bf16[1,2048,3072]{2,1,0:T(8,128)(2,1)} %param.11, bf16[128,3072]{1,0:T(8,128)(2,1)S(1)} %all_gather.3, bf16[1,3072,2048]{2,1,0:T(8,128)(2,1)} %param.10, f32[128,2048]{1,0:T(8,128)S(1)} %fusion.4), kind=kOutput, calls=%fused_computation.6 | convolution fusion | flops 3223191552 | bytes 27787264 | tf_op jit(solution)/shard_map/dot_general | solution.py:46
  49.1 0.0 reduce-scatter.2.cloned.1.call-update
  49.1 7.1 %reduce-scatter.2.cloned.1.call-done = bf16[64,3072]{1,0:T(8,128)(2,1)} async-done(((bf16[128,3072]{1,0:T(8,128)(2,1)}), bf16[64,3072]{1,0:T(8,128)(2,1)}) %reduce-scatter.2.cloned.1.call-update) | async-done | bytes 393232 | tf_op jit(solution)/shard_map/reduce_scatter | solution.py:45
  56.1 5.8 %all-to-all-start.1 = ((bf16[8,8,3072]{2,1,0:T(8,128)(2,1)}), bf16[8,8,3072]{2,1,0:T(8,128)(2,1)S(1)}, u32[]{:S(2)}, u32[]{:S(2)}) async-start(bf16[8,8,3072]{2,1,0:T(8,128)(2,1)} %bitcast.37), calls=%async_computation.2 | async-start | bytes 786432 | tf_op jit(solution)/shard_map/all_to_all | solution.py:51
  61.9 0.0 copy-done.1
  61.9 0.1 copy.25
  62.0 0.3 fusion.23
  62.3 11.7 %all-to-all-done.1 = bf16[8,8,3072]{2,1,0:T(8,128)(2,1)S(1)} async-done(((bf16[8,8,3072]{2,1,0:T(8,128)(2,1)}), bf16[8,8,3072]{2,1,0:T(8,128)(2,1)S(1)}, u32[]{:S(2)}, u32[]{:S(2)}) %all-to-all-start.1) | async-done | bytes 393248 | tf_op jit(solution)/shard_map/all_to_all | solution.py:51
  74.1 1.5 %fusion.9 = bf16[16,3072]{1,0:T(8,128)(2,1)} fusion(bf16[8,8,3072]{2,1,0:T(8,128)(2,1)S(1)} %all-to-all-done.1, f32[16,8,8]{2,1,0:T(8,128)S(1)} %fusion.23), kind=kOutput, calls=%fused_computation.9 | convolution fusion | flops 37797888 | bytes 495616 | tf_op jit(solution)/shard_map/rgc,gcd->rd/dot_general | solution.py:60
  (1 shorter events, 0.0 us)
Async XLA Ops:
  6.5 1.5 %copy-start = (bf16[16,3072]{1,0:T(8,128)(2,1)S(1)}, bf16[16,3072]{1,0:T(8,128)(2,1)}, u32[]{:S(2)}) copy-start(bf16[16,3072]{1,0:T(8,128)(2,1)} %param.6) | copy-start | bytes 294916
  6.5 49.6 %reduce-scatter.2.cloned.1.call-start = ((), (), s32[]{:S(2)}) async-start(), calls=%async_computation.3 | async-start | bytes 1179648 | tf_op jit(solution)/shard_map/reduce_scatter | solution.py:45
  36.2 25.7 %copy-start.1 = (bf16[16,2]{0,1:T(2,128)(2,1)S(1)}, bf16[16,2]{0,1:T(2,128)(2,1)}, u32[]{:S(2)}) copy-start(bf16[16,2]{0,1:T(2,128)(2,1)} %param.8) | copy-start | bytes 196
  56.1 17.9 %all-to-all-start.1 = ((bf16[8,8,3072]{2,1,0:T(8,128)(2,1)}), bf16[8,8,3072]{2,1,0:T(8,128)(2,1)S(1)}, u32[]{:S(2)}, u32[]{:S(2)}) async-start(bf16[8,8,3072]{2,1,0:T(8,128)(2,1)} %bitcast.37), calls=%async_computation.2 | async-start | bytes 786432 | tf_op jit(solution)/shard_map/all_to_all | solution.py:51
Sparse Core Ops, SparseCore 0:
  49.2 6.8 reduce-scatter.1
where the time goes:
time: 82.7 us; the launch traced here: 82.4 us
  matrix products  21.7 us (26%)
  blocking collectives  21.5 us (26%)
  waiting for transfers between devices  18.8 us (23%)
  between operations  13.4 us (16%)
  starting transfers between devices  5.77 us (7%)
  local copies, waits for them, and re-layouts  1.17 us (1%)
    all_to_all x1, blocking collectives, shards(): lax.all_to_all(outgoing, 'expert', split_axis=0, concat_axis=0, tiled=True)  19.2 us
    dot_general x1, matrix products, shards(): jnp.dot(hidden, down_local, preferred_element_type=jnp.float32)  12.9 us
    all_to_all x1, waiting for transfers between devices, shards(): lax.all_to_all(slot_sums.reshape(group_count, capacity, feature).astype(j...  11.7 us
    reduce_scatter x1, waiting for transfers between devices, shards(): lax.psum_scatter(jnp.dot(hidden, down_local, preferred_element_type=jnp.f...  7.05 us
    dot_general x1, matrix products, shards(): jnp.dot(block_rows, gate_local, preferred_element_type=jnp.float32)  6.41 us
    all_to_all x1, starting transfers between devices, shards(): lax.all_to_all(slot_sums.reshape(group_count, capacity, feature).astype(j...  5.76 us
    all_gather x1, blocking collectives, shards(): block_rows = lax.all_gather(flattened, 'tile', axis=0, tiled=True)  2.36 us
  transfers between devices with their start and end apart: 2, of which 2 were waited for; matrix products, arithmetic and copies ran while one was open for 1% of the time, Pallas kernels for 0%

commit v1 on v0

v1 whole, which is shorter than its diff:
```python
import functools

import jax
import jax.numpy as jnp
from jax import lax
from jax.experimental import pallas as pl
from jax.experimental.pallas import tpu as pltpu
from jax.sharding import PartitionSpec as P

F32 = jnp.float32
BF16 = jnp.bfloat16
MIB = 2**20


def partner(expert, step, experts):
    if experts & (experts - 1) == 0:
        return expert ^ step
    return (step - expert + experts) % experts


def route_kernel(experts, capacity, me_ref, routes_ref, weights_ref, tokens_ref, out_ref, comb_ref):
    slots = experts * capacity
    rows = tokens_ref.shape[0]
    slot = lax.broadcasted_iota(jnp.int32, (slots, rows), 0)
    step = slot // capacity
    place = slot - step * capacity
    expert = jnp.zeros_like(slot)
    for s in range(experts):
        expert = jnp.where(step == s, me_ref[s], expert)
    match = [routes_ref[k : k + 1, :] == expert for k in range(2)]
    named = jnp.where(match[0] | match[1], 1.0, 0.0)
    before = jnp.where(
        lax.broadcasted_iota(jnp.int32, (rows, rows), 0)
        < lax.broadcasted_iota(jnp.int32, (rows, rows), 1),
        1.0,
        0.0,
    )
    ahead = jnp.dot(named.astype(BF16), before.astype(BF16), preferred_element_type=F32)
    chosen = jnp.where(ahead == place.astype(F32), named, 0.0)
    weights = weights_ref[...].astype(F32)
    weight = jnp.where(match[0], weights[0:1, :], weights[1:2, :])
    comb_ref[...] = (chosen * weight).astype(BF16)
    out_ref[...] = jnp.dot(
        chosen.astype(BF16), tokens_ref[...], preferred_element_type=F32
    ).astype(BF16)


def fetch_kernel(from_ref, to_ref, sem):
    copy = pltpu.make_async_copy(from_ref, to_ref, sem)
    copy.start()
    copy.wait()


def fetch(array, limit):
    return pl.pallas_call(
        fetch_kernel,
        out_shape=pltpu.VMEM(array.shape, array.dtype),
        in_specs=[pl.BlockSpec(memory_space=pltpu.HBM)],
        out_specs=pl.BlockSpec(memory_space=pltpu.VMEM),
        scratch_shapes=[pltpu.SemaphoreType.DMA],
        compiler_params=pltpu.CompilerParams(vmem_limit_bytes=limit * MIB),
        cost_estimate=pl.CostEstimate(
            flops=0, bytes_accessed=4 * array.size, transcendentals=0
        ),
        name="fetch",
    )(pltpu.with_memory_space_constraint(array, pltpu.HBM))


def ffn_kernel(width, rows_ref, gate_ref, up_ref, down_hbm, out_ref, hidden_ref, down_ref, sems):
    blocks = [slice(at, at + 256) for at in range(0, down_ref.shape[1], 256)]
    copies = [
        pltpu.make_async_copy(down_hbm.at[:, part], down_ref.at[:, part], sems.at[i])
        for i, part in enumerate(blocks)
    ]
    for copy in copies:
        copy.start()
    for at in range(0, gate_ref.shape[1], width):
        part = slice(at, at + width)
        gate = jnp.dot(rows_ref[...], gate_ref[:, part], preferred_element_type=F32)
        up = jnp.dot(rows_ref[...], up_ref[:, part], preferred_element_type=F32)
        hidden_ref[:, part] = (gate / (1.0 + jnp.exp(-gate)) * up).astype(BF16)
    for copy, part in zip(copies, blocks):
        copy.wait()
        out_ref[:, part] = jnp.dot(
            hidden_ref[...], down_ref[:, part], preferred_element_type=F32
        ).astype(BF16)


def combine_kernel(comb_ref, results_ref, out_ref):
    out_ref[...] = lax.dot_general(
        comb_ref[...],
        results_ref[...],
        (((0,), (0,)), ((), ())),
        preferred_element_type=F32,
    ).astype(BF16)


def add(a, b):
    return (a.astype(F32) + b.astype(F32)).astype(BF16)


def shards(tokens, routes, route_weights, gate_proj, up_proj, down_proj):
    groups = lax.axis_size("expert")
    tiles = lax.axis_size("tile")
    experts = groups // 2
    rows, width = tokens.shape
    capacity = max(2, 2 * rows // experts)
    slots = experts * capacity
    vmem = pl.BlockSpec(memory_space=pltpu.VMEM)
    me = lax.axis_index("expert") // 2
    targets = jnp.stack([partner(me, s, experts) for s in range(experts)]).astype(jnp.int32)
    outgoing, comb = pl.pallas_call(
        functools.partial(route_kernel, experts, capacity),
        out_shape=(
            jax.ShapeDtypeStruct((slots, width), BF16),
            jax.ShapeDtypeStruct((slots, rows), BF16),
        ),
        in_specs=[pl.BlockSpec(memory_space=pltpu.SMEM), vmem, vmem, vmem],
        out_specs=(vmem, vmem),
        name="route",
    )(targets, routes.T, route_weights.T, tokens)

    def trade(x, step):
        pairs = [
            (g, 2 * partner(g // 2, step, experts) + g % 2)
            for g in range(groups)
            if partner(g // 2, step, experts) != g // 2
        ]
        if len(pairs) == groups:
            return lax.ppermute(x, "expert", pairs)
        moved = lax.ppermute(x, "expert", pairs)
        return jnp.where(partner(me, step, experts) == me, x, moved)

    def swap(x, axis):
        return lax.ppermute(x, axis, [(i, i ^ 1) for i in range(lax.axis_size(axis))])

    def trade_all(x):
        blocks = x.reshape(experts, capacity, width)
        return jnp.concatenate(
            [blocks[0]] + [trade(blocks[s], s) for s in range(1, experts)]
        )

    gate, up, down = gate_proj[0], up_proj[0], down_proj[0]
    mine, gate = lax.optimization_barrier((trade_all(outgoing), fetch(gate, 8)))
    both = jnp.concatenate([mine, swap(mine, "expert")])
    both, up = lax.optimization_barrier((both, fetch(up, 8)))
    if tiles == 2:
        received = jnp.concatenate([both, swap(both, "tile")])
    else:
        received = lax.all_gather(both, "tile", axis=0, tiled=True)
    count, hidden = received.shape[0], gate.shape[1]
    block = min(256, hidden)
    partials = pl.pallas_call(
        functools.partial(ffn_kernel, block),
        out_shape=jax.ShapeDtypeStruct((count, width), BF16),
        in_specs=[vmem, vmem, vmem, pl.BlockSpec(memory_space=pltpu.HBM)],
        out_specs=vmem,
        scratch_shapes=[
            pltpu.VMEM((count, hidden), BF16),
            pltpu.VMEM((hidden, width), BF16),
            pltpu.SemaphoreType.DMA((width // 256,)),
        ],
        compiler_params=pltpu.CompilerParams(vmem_limit_bytes=20 * MIB),
        cost_estimate=pl.CostEstimate(
            flops=6 * count * width * hidden,
            bytes_accessed=6 * width * hidden,
            transcendentals=count * hidden,
        ),
        name="ffn",
    )(received, gate, up, pltpu.with_memory_space_constraint(down, pltpu.HBM))
    if tiles == 2:
        half = count // 2
        both = add(partials[:half], swap(partials[half:], "tile"))
    else:
        pieces = lax.all_to_all(
            partials.reshape(tiles, 2 * slots, width), "tile", 0, 0, tiled=True
        )
        both = jnp.sum(pieces.astype(F32), axis=0).astype(BF16)
    mine = add(both[:slots], swap(both[slots:], "expert"))
    results = trade_all(mine)
    return pl.pallas_call(
        combine_kernel,
        out_shape=jax.ShapeDtypeStruct((rows, width), BF16),
        in_specs=[vmem, vmem],
        out_specs=vmem,
        name="combine",
    )(comb, results)


def solution(mesh):
    placed = (
        P(("parts", "expert", "tile"), None),
        P(("parts", "expert", "tile"), None),
        P(("parts", "expert", "tile"), None),
        P("expert", None, "tile"),
        P("expert", None, "tile"),
        P("expert", "tile", None),
    )
    return jax.shard_map(
        shards,
        mesh=mesh,
        in_specs=placed,
        out_specs=P(("parts", "expert", "tile"), None),
        check_vma=False,
    )
```

time: 82.7 us -> 52.4 us (0.63)
  Pallas kernels: 0 us -> 22.7 us
  matrix products: 21.7 us -> 0 us
  blocking collectives: 21.5 us -> 0 us
  between operations: 13.4 us -> 0.13 us
  starting transfers between devices: 5.77 us -> 13.6 us
  waiting for transfers between devices: 18.8 us -> 13.1 us
  other arithmetic: 0.09 us -> 1.61 us
    pallas_call x0 -> x5, Pallas kernels: none -> 22.7 us  [the longest x1 9.83 us: shards(): pl.pallas_call(functools.partial(ffn_kernel, block), out_shape=jax.ShapeD...]
    dot_general x6 -> x0, matrix products: 21.7 us -> none  [the longest x1 12.9 us: shards(): jnp.dot(hidden, down_local, preferred_element_type=jnp.float32)]
    all_to_all x1 -> x0, blocking collectives: 19.2 us -> none  [shards(): lax.all_to_all(outgoing, 'expert', split_axis=0, concat_axis=0, tiled=True)]
    ppermute x0 -> x10, starting transfers between devices: none -> 13.6 us  [the longest x6 10.2 us: trade(): return lax.ppermute(x, 'expert', pairs)]
    ppermute x0 -> x10, waiting for transfers between devices: none -> 13.1 us  [the longest x4 8.92 us: swap(): lax.ppermute(x, axis, [(i, i ^ 1) for i in range(lax.axis_size(axis))])]
    all_to_all x1 -> x0, waiting for transfers between devices: 11.7 us -> none  [shards(): lax.all_to_all(slot_sums.reshape(group_count, capacity, feature).astype(j...]
    reduce_scatter x1 -> x0, waiting for transfers between devices: 7.05 us -> none  [shards(): lax.psum_scatter(jnp.dot(hidden, down_local, preferred_element_type=jnp.f...]
    all_to_all x1 -> x0, starting transfers between devices: 5.76 us -> none  [shards(): lax.all_to_all(slot_sums.reshape(group_count, capacity, feature).astype(j...]
  transfers between devices with their start and end apart: 2 -> 10, of which waited for: 2 -> 5; matrix products, arithmetic and copies ran while one was open for 1% -> 0% of each run, Pallas kernels for 0% -> 18%
where the time goes in v1:
time: 52.4 us; the launch traced here: 52.1 us
  Pallas kernels  22.7 us (43%)
  starting transfers between devices  13.6 us (26%)
  waiting for transfers between devices  13.1 us (25%)
  other arithmetic  1.61 us (3%)
  local copies, waits for them, and re-layouts  0.94 us (2%)
    ppermute x6, starting transfers between devices, trade(): return lax.ppermute(x, 'expert', pairs)  10.2 us
    pallas_call x1, Pallas kernels, shards(): pl.pallas_call(functools.partial(ffn_kernel, block), out_shape=jax.ShapeD...  9.83 us
    pallas_call x2, Pallas kernels, fetch(): pl.pallas_call(fetch_kernel, out_shape=pltpu.VMEM(array.shape, array.dtyp...  9.17 us
    ppermute x4, waiting for transfers between devices, swap(): lax.ppermute(x, axis, [(i, i ^ 1) for i in range(lax.axis_size(axis))])  8.92 us
    ppermute x6, waiting for transfers between devices, trade(): return lax.ppermute(x, 'expert', pairs)  4.21 us
    ppermute x4, starting transfers between devices, swap(): lax.ppermute(x, axis, [(i, i ^ 1) for i in range(lax.axis_size(axis))])  3.37 us
    pallas_call x1, Pallas kernels, shards(): pl.pallas_call(functools.partial(route_kernel, experts, capacity), out_sh...  1.92 us
    pallas_call x1, Pallas kernels, shards(): pl.pallas_call(combine_kernel, out_shape=jax.ShapeDtypeStruct((rows, widt...  1.79 us
  transfers between devices with their start and end apart: 10, of which 5 were waited for; matrix products, arithmetic and copies ran while one was open for 0% of the time, Pallas kernels for 18%

profile of v1, /device:TPU:0, one launch (start us, length us, event | category | flops | bytes accessed | tf_op | source)
XLA Modules:
  0.0 52.1 jit_solution(17194476577132220155)
XLA Ops:
  0.0 0.7 %pad_add_fusion.me_ref = s32[4]{0:T(128)} fusion(s32[1]{0:T(128)} %bitcast.3, s32[1]{0:T(128)} %bitcast.2, s32[1]{0:T(128)} %bitcast.1, s32[1]{0:T(128)} %bitcast), kind=kLoop, calls=%fused_computation.6 | loop fusion | flops 12 | bytes 32 | tf_op jit(solution)/shard_map/stack | solution.py:111
  0.7 1.9 %route.1 = (bf16[32,3072]{1,0:T(8,128)(2,1)}, bf16[32,16]{1,0:T(8,128)(2,1)}) custom-call(s32[4]{0:T(128)} %pad_add_fusion.me_ref, s32[2,16]{1,0:T(2,128)} %bitcast.12, bf16[2,16]{1,0:T(2,128)(2,1)} %bitcast.13, bf16[16,3072]{1,0:T(8,128)(2,1)} %tokens_ref.1), custom_call_target="tpu_custom_call" | custom-call | tf_op jit(solution)/shard_map/route/pallas_call | solution.py:112
  2.6 0.9 %fusion.1 = (bf16[8,3072]{1,0:T(8,128)(2,1)S(1)}, bf16[8,3072]{1,0:T(8,128)(2,1)S(1)}, bf16[8,3072]{1,0:T(8,128)(2,1)S(1)}, bf16[8,3072]{1,0:T(8,128)(2,1)S(1)}) fusion(bf16[32,3072]{1,0:T(8,128)(2,1)} %get-tuple-element.12), kind=kLoop, calls=%fused_computation.8 | loop fusion | bytes 393216 | tf_op jit(solution)/shard_map/slice | solution.py:140
  3.5 5.1 %collective-permute-start.2 = (bf16[8,3072]{1,0:T(8,128)(2,1)S(1)}, bf16[8,3072]{1,0:T(8,128)(2,1)S(1)}, u32[]{:S(2)}, u32[]{:S(2)}) collective-permute-start(bf16[8,3072]{1,0:T(8,128)(2,1)S(1)} %get-tuple-element.22), channel_id=1, source_target_pairs={{0,12},{2,14},{4,8},{6,10},{8,4},{10,6},{12,0},{14,2},{1,13},{3,15... | collective-permute-start | bytes 147464 | tf_op jit(solution)/shard_map/ppermute | solution.py:130
  8.6 0.6 %collective-permute-start = (bf16[8,3072]{1,0:T(8,128)(2,1)S(1)}, bf16[8,3072]{1,0:T(8,128)(2,1)S(1)}, u32[]{:S(2)}, u32[]{:S(2)}) collective-permute-start(bf16[8,3072]{1,0:T(8,128)(2,1)S(1)} %get-tuple-element.24), channel_id=1, source_target_pairs={{0,4},{2,6},{4,0},{6,2},{8,12},{10,14},{12,8},{14,10},{1,5},{3,7},... | collective-permute-start | bytes 147464 | tf_op jit(solution)/shard_map/ppermute | solution.py:130
  9.2 4.6 %fetch.2.gate_ref = bf16[3072,2048]{1,0:T(8,128)(2,1)S(1)} custom-call(bf16[3072,2048]{1,0:T(8,128)(2,1)} %bitcast.9), custom_call_target="tpu_custom_call" | custom-call | bytes 25165824 | tf_op jit(solution)/shard_map/fetch/pallas_call | solution.py:55
  13.8 0.0 collective-permute-done.2
  13.9 1.7 %collective-permute-start.3 = (bf16[32,3072]{1,0:T(8,128)(2,1)S(1)}, bf16[32,3072]{1,0:T(8,128)(2,1)S(1)}, u32[]{:S(2)}, u32[]{:S(2)}) collective-permute-start(bf16[32,3072]{1,0:T(8,128)(2,1)S(1)} %pad_maximum_fusion.2), channel_id=1, source_target_pairs={{0,2},{2,0},{4,6},{6,4},{8,10},{10,8},{12,14},{14,12},{1,3},{3,1},... | collective-permute-start | bytes 589832 | tf_op jit(solution)/shard_map/ppermute | solution.py:135
  15.6 4.6 %fetch.3.up_ref = bf16[3072,2048]{1,0:T(8,128)(2,1)S(1)} custom-call(bf16[3072,2048]{1,0:T(8,128)(2,1)} %bitcast.10), custom_call_target="tpu_custom_call" | custom-call | bytes 25165824 | tf_op jit(solution)/shard_map/fetch/pallas_call | solution.py:55
  20.2 0.1 collective-permute-start.4
  20.3 1.7 %collective-permute-done.4 = bf16[64,3072]{1,0:T(8,128)(2,1)S(1)} collective-permute-done((bf16[64,3072]{1,0:T(8,128)(2,1)S(1)}, bf16[64,3072]{1,0:T(8,128)(2,1)S(1)}, u32[]{:S(2)}, u32[]{:S(2)}) %collective-permute-start.4) | collective-permute-done | bytes 393248 | tf_op jit(solution)/shard_map/ppermute | solution.py:135
  22.0 0.1 pad_maximum_fusion.rows_ref
  22.1 9.8 %ffn.1 = bf16[128,3072]{1,0:T(8,128)(2,1)S(1)} custom-call(bf16[128,3072]{1,0:T(8,128)(2,1)S(1)} %pad_maximum_fusion.rows_ref, bf16[3072,2048]{1,0:T(8,128)(2,1)S(1)} %fetch.2.gate_ref, bf16[3072,2048]{1,0:T(8,128)(2,1)S(1)} %fetch.3.up_ref, bf16[2048,3072]{1,0:T(8,128)(2,1)} %bitcast.11), custom_call_target="tpu_custom_call" | custom-call | flops 4831838208 | bytes 37748736 | tf_op jit(solution)/shard_map/ffn/pallas_call | solution.py:153
  31.9 0.2 collective-permute-start.5
  32.1 1.6 %collective-permute-done.5 = bf16[64,3072]{1,0:T(8,128)(2,1)S(1)} collective-permute-done((bf16[64,3072]{1,0:T(8,128)(2,1)S(1)}, bf16[64,3072]{1,0:T(8,128)(2,1)S(1)}, u32[]{:S(2)}, u32[]{:S(2)}) %collective-permute-start.5) | collective-permute-done | bytes 393248 | tf_op jit(solution)/shard_map/ppermute | solution.py:135
  33.7 0.1 add_convert_fusion
  33.9 1.4 %collective-permute-start.6 = (bf16[32,3072]{1,0:T(8,128)(2,1)S(1)}, bf16[32,3072]{1,0:T(8,128)(2,1)S(1)}, u32[]{:S(2)}, u32[]{:S(2)}) collective-permute-start(bf16[32,3072]{1,0:T(8,128)(2,1)S(1)} %slice.59), channel_id=1, source_target_pairs={{0,2},{2,0},{4,6},{6,4},{8,10},{10,8},{12,14},{14,12},{1,3},{3,1},... | collective-permute-start | bytes 589832 | tf_op jit(solution)/shard_map/ppermute | solution.py:135
  35.2 5.6 %collective-permute-done.6 = bf16[32,3072]{1,0:T(8,128)(2,1)S(1)} collective-permute-done((bf16[32,3072]{1,0:T(8,128)(2,1)S(1)}, bf16[32,3072]{1,0:T(8,128)(2,1)S(1)}, u32[]{:S(2)}, u32[]{:S(2)}) %collective-permute-start.6) | collective-permute-done | bytes 196640 | tf_op jit(solution)/shard_map/ppermute | solution.py:135
  40.9 3.7 %collective-permute-start.9 = (bf16[8,3072]{1,0:T(8,128)(2,1)S(1)}, bf16[8,3072]{1,0:T(8,128)(2,1)S(1)}, u32[]{:S(2)}, u32[]{:S(2)}) collective-permute-start(bf16[8,3072]{1,0:T(8,128)(2,1)S(1)} %get-tuple-element.18), channel_id=1, source_target_pairs={{0,12},{2,14},{4,8},{6,10},{8,4},{10,6},{12,0},{14,2},{1,13},{3,15... | collective-permute-start | bytes 147464 | tf_op jit(solution)/shard_map/ppermute | solution.py:130
  44.6 0.8 %collective-permute-start.7 = (bf16[8,3072]{1,0:T(8,128)(2,1)S(1)}, bf16[8,3072]{1,0:T(8,128)(2,1)S(1)}, u32[]{:S(2)}, u32[]{:S(2)}) collective-permute-start(bf16[8,3072]{1,0:T(8,128)(2,1)S(1)} %get-tuple-element.20), channel_id=1, source_target_pairs={{0,4},{2,6},{4,0},{6,2},{8,12},{10,14},{12,8},{14,10},{1,5},{3,7},... | collective-permute-start | bytes 147464 | tf_op jit(solution)/shard_map/ppermute | solution.py:130
  45.4 1.6 %collective-permute-done.9 = bf16[8,3072]{1,0:T(8,128)(2,1)S(1)} collective-permute-done((bf16[8,3072]{1,0:T(8,128)(2,1)S(1)}, bf16[8,3072]{1,0:T(8,128)(2,1)S(1)}, u32[]{:S(2)}, u32[]{:S(2)}) %collective-permute-start.9) | collective-permute-done | bytes 49184 | tf_op jit(solution)/shard_map/ppermute | solution.py:130
  47.0 2.6 %collective-permute-done.8 = bf16[8,3072]{1,0:T(8,128)(2,1)S(1)} collective-permute-done((bf16[8,3072]{1,0:T(8,128)(2,1)S(1)}, bf16[8,3072]{1,0:T(8,128)(2,1)S(1)}, u32[]{:S(2)}, u32[]{:S(2)}) %collective-permute-start.8) | collective-permute-done | bytes 49184 | tf_op jit(solution)/shard_map/ppermute | solution.py:130
  49.6 0.7 %pad_maximum_fusion.3.results_ref = bf16[32,3072]{1,0:T(8,128)(2,1)} fusion(bf16[8,3072]{1,0:T(8,128)(2,1)S(1)} %collective-permute-done.9, bf16[8,3072]{1,0:T(8,128)(2,1)S(1)} %collective-permute-done.8, bf16[8,3072]{1,0:T(8,128)(2,1)S(1)} %collective-permute-done.7, bf16[8,3072]{1,0:T(8,128)(2,1)S(1)} %get-tuple-element.17), kind=kLoop, calls=%fused_computation.5 | loop fusion | flops 786432 | bytes 393216 | tf_op jit(solution)/shard_map/concatenate | solution.py:139
  50.3 1.8 %combine.1 = bf16[16,3072]{1,0:T(8,128)(2,1)} custom-call(bf16[32,16]{1,0:T(8,128)(2,1)} %get-tuple-element.11.comb_ref, bf16[32,3072]{1,0:T(8,128)(2,1)} %pad_maximum_fusion.3.results_ref), custom_call_target="tpu_custom_call" | custom-call | tf_op jit(solution)/shard_map/combine/pallas_call | solution.py:181
  (12 shorter events, 0.2 us)
Async XLA Ops:
  3.5 10.3 %collective-permute-start.2 = (bf16[8,3072]{1,0:T(8,128)(2,1)S(1)}, bf16[8,3072]{1,0:T(8,128)(2,1)S(1)}, u32[]{:S(2)}, u32[]{:S(2)}) collective-permute-start(bf16[8,3072]{1,0:T(8,128)(2,1)S(1)} %get-tuple-element.22), channel_id=1, source_target_pairs={{0,12},{2,14},{4,8},{6,10},{8,4},{10,6},{12,0},{14,2},{1,13},{3,15... | collective-permute-start | bytes 147464 | tf_op jit(solution)/shard_map/ppermute | solution.py:130
  8.6 5.2 %collective-permute-start.1 = (bf16[8,3072]{1,0:T(8,128)(2,1)S(1)}, bf16[8,3072]{1,0:T(8,128)(2,1)S(1)}, u32[]{:S(2)}, u32[]{:S(2)}) collective-permute-start(bf16[8,3072]{1,0:T(8,128)(2,1)S(1)} %get-tuple-element.23), channel_id=1, source_target_pairs={{0,8},{2,10},{4,12},{6,14},{8,0},{10,2},{12,4},{14,6},{1,9},{3,11}... | collective-permute-start | bytes 147464 | tf_op jit(solution)/shard_map/ppermute | solution.py:130
  8.6 5.3 %collective-permute-start = (bf16[8,3072]{1,0:T(8,128)(2,1)S(1)}, bf16[8,3072]{1,0:T(8,128)(2,1)S(1)}, u32[]{:S(2)}, u32[]{:S(2)}) collective-permute-start(bf16[8,3072]{1,0:T(8,128)(2,1)S(1)} %get-tuple-element.24), channel_id=1, source_target_pairs={{0,4},{2,6},{4,0},{6,2},{8,12},{10,14},{12,8},{14,10},{1,5},{3,7},... | collective-permute-start | bytes 147464 | tf_op jit(solution)/shard_map/ppermute | solution.py:130
  13.9 6.3 %collective-permute-start.3 = (bf16[32,3072]{1,0:T(8,128)(2,1)S(1)}, bf16[32,3072]{1,0:T(8,128)(2,1)S(1)}, u32[]{:S(2)}, u32[]{:S(2)}) collective-permute-start(bf16[32,3072]{1,0:T(8,128)(2,1)S(1)} %pad_maximum_fusion.2), channel_id=1, source_target_pairs={{0,2},{2,0},{4,6},{6,4},{8,10},{10,8},{12,14},{14,12},{1,3},{3,1},... | collective-permute-start | bytes 589832 | tf_op jit(solution)/shard_map/ppermute | solution.py:135
  20.2 1.8 %collective-permute-start.4 = (bf16[64,3072]{1,0:T(8,128)(2,1)S(1)}, bf16[64,3072]{1,0:T(8,128)(2,1)S(1)}, u32[]{:S(2)}, u32[]{:S(2)}) collective-permute-start(bf16[64,3072]{1,0:T(8,128)(2,1)S(1)} %pad_maximum_fusion.1), channel_id=1, source_target_pairs={{0,1},{1,0},{2,3},{3,2},{4,5},{5,4},{6,7},{7,6},{8,9},{9,8},{10,11... | collective-permute-start | bytes 1179656 | tf_op jit(solution)/shard_map/ppermute | solution.py:135
  31.9 1.8 %collective-permute-start.5 = (bf16[64,3072]{1,0:T(8,128)(2,1)S(1)}, bf16[64,3072]{1,0:T(8,128)(2,1)S(1)}, u32[]{:S(2)}, u32[]{:S(2)}) collective-permute-start(bf16[64,3072]{1,0:T(8,128)(2,1)S(1)} %slice.57), channel_id=1, source_target_pairs={{0,1},{1,0},{2,3},{3,2},{4,5},{5,4},{6,7},{7,6},{8,9},{9,8},{10,11... | collective-permute-start | bytes 1179656 | tf_op jit(solution)/shard_map/ppermute | solution.py:135
  33.9 7.0 %collective-permute-start.6 = (bf16[32,3072]{1,0:T(8,128)(2,1)S(1)}, bf16[32,3072]{1,0:T(8,128)(2,1)S(1)}, u32[]{:S(2)}, u32[]{:S(2)}) collective-permute-start(bf16[32,3072]{1,0:T(8,128)(2,1)S(1)} %slice.59), channel_id=1, source_target_pairs={{0,2},{2,0},{4,6},{6,4},{8,10},{10,8},{12,14},{14,12},{1,3},{3,1},... | collective-permute-start | bytes 589832 | tf_op jit(solution)/shard_map/ppermute | solution.py:135
  40.9 6.1 %collective-permute-start.9 = (bf16[8,3072]{1,0:T(8,128)(2,1)S(1)}, bf16[8,3072]{1,0:T(8,128)(2,1)S(1)}, u32[]{:S(2)}, u32[]{:S(2)}) collective-permute-start(bf16[8,3072]{1,0:T(8,128)(2,1)S(1)} %get-tuple-element.18), channel_id=1, source_target_pairs={{0,12},{2,14},{4,8},{6,10},{8,4},{10,6},{12,0},{14,2},{1,13},{3,15... | collective-permute-start | bytes 147464 | tf_op jit(solution)/shard_map/ppermute | solution.py:130
  44.6 5.0 %collective-permute-start.8 = (bf16[8,3072]{1,0:T(8,128)(2,1)S(1)}, bf16[8,3072]{1,0:T(8,128)(2,1)S(1)}, u32[]{:S(2)}, u32[]{:S(2)}) collective-permute-start(bf16[8,3072]{1,0:T(8,128)(2,1)S(1)} %get-tuple-element.19), channel_id=1, source_target_pairs={{0,8},{2,10},{4,12},{6,14},{8,0},{10,2},{12,4},{14,6},{1,9},{3,11}... | collective-permute-start | bytes 147464 | tf_op jit(solution)/shard_map/ppermute | solution.py:130
  44.6 5.0 %collective-permute-start.7 = (bf16[8,3072]{1,0:T(8,128)(2,1)S(1)}, bf16[8,3072]{1,0:T(8,128)(2,1)S(1)}, u32[]{:S(2)}, u32[]{:S(2)}) collective-permute-start(bf16[8,3072]{1,0:T(8,128)(2,1)S(1)} %get-tuple-element.20), channel_id=1, source_target_pairs={{0,4},{2,6},{4,0},{6,2},{8,12},{10,14},{12,8},{14,10},{1,5},{3,7},... | collective-permute-start | bytes 147464 | tf_op jit(solution)/shard_map/ppermute | solution.py:130

commit v2 on v1

--- a/solution.py
+++ b/solution.py
@@ -18,7 +18,8 @@
     return (step - expert + experts) % experts
 
 
-def route_kernel(experts, capacity, me_ref, routes_ref, weights_ref, tokens_ref, out_ref, comb_ref):
+def route_kernel(experts, capacity, routes_ref, weights_ref, tokens_ref, out_ref, comb_ref):
+    me = lax.axis_index("expert") // 2
     slots = experts * capacity
     rows = tokens_ref.shape[0]
     slot = lax.broadcasted_iota(jnp.int32, (slots, rows), 0)
@@ -26,7 +27,7 @@
     place = slot - step * capacity
     expert = jnp.zeros_like(slot)
     for s in range(experts):
-        expert = jnp.where(step == s, me_ref[s], expert)
+        expert = jnp.where(step == s, partner(me, s, experts), expert)
     match = [routes_ref[k : k + 1, :] == expert for k in range(2)]
     named = jnp.where(match[0] | match[1], 1.0, 0.0)
     before = jnp.where(
@@ -45,42 +46,14 @@
     ).astype(BF16)
 
 
-def fetch_kernel(from_ref, to_ref, sem):
-    copy = pltpu.make_async_copy(from_ref, to_ref, sem)
-    copy.start()
-    copy.wait()
-
-
-def fetch(array, limit):
-    return pl.pallas_call(
-        fetch_kernel,
-        out_shape=pltpu.VMEM(array.shape, array.dtype),
-        in_specs=[pl.BlockSpec(memory_space=pltpu.HBM)],
-        out_specs=pl.BlockSpec(memory_space=pltpu.VMEM),
-        scratch_shapes=[pltpu.SemaphoreType.DMA],
-        compiler_params=pltpu.CompilerParams(vmem_limit_bytes=limit * MIB),
-        cost_estimate=pl.CostEstimate(
-            flops=0, bytes_accessed=4 * array.size, transcendentals=0
-        ),
-        name="fetch",
-    )(pltpu.with_memory_space_constraint(array, pltpu.HBM))
-
-
-def ffn_kernel(width, rows_ref, gate_ref, up_ref, down_hbm, out_ref, hidden_ref, down_ref, sems):
-    blocks = [slice(at, at + 256) for at in range(0, down_ref.shape[1], 256)]
-    copies = [
-        pltpu.make_async_copy(down_hbm.at[:, part], down_ref.at[:, part], sems.at[i])
-        for i, part in enumerate(blocks)
-    ]
-    for copy in copies:
-        copy.start()
+def ffn_kernel(width, rows_ref, gate_ref, up_ref, down_ref, out_ref, hidden_ref):
     for at in range(0, gate_ref.shape[1], width):
         part = slice(at, at + width)
         gate = jnp.dot(rows_ref[...], gate_ref[:, part], preferred_element_type=F32)
         up = jnp.dot(rows_ref[...], up_ref[:, part], preferred_element_type=F32)
         hidden_ref[:, part] = (gate / (1.0 + jnp.exp(-gate)) * up).astype(BF16)
-    for copy, part in zip(copies, blocks):
-        copy.wait()
+    for at in range(0, down_ref.shape[1], 256):
+        part = slice(at, at + 256)
         out_ref[:, part] = jnp.dot(
             hidden_ref[...], down_ref[:, part], preferred_element_type=F32
         ).astype(BF16)
@@ -108,17 +81,20 @@
     slots = experts * capacity
     vmem = pl.BlockSpec(memory_space=pltpu.VMEM)
     me = lax.axis_index("expert") // 2
-    targets = jnp.stack([partner(me, s, experts) for s in range(experts)]).astype(jnp.int32)
     outgoing, comb = pl.pallas_call(
         functools.partial(route_kernel, experts, capacity),
         out_shape=(
             jax.ShapeDtypeStruct((slots, width), BF16),
             jax.ShapeDtypeStruct((slots, rows), BF16),
         ),
-        in_specs=[pl.BlockSpec(memory_space=pltpu.SMEM), vmem, vmem, vmem],
+        in_specs=[vmem, vmem, vmem],
         out_specs=(vmem, vmem),
+        cost_estimate=pl.CostEstimate(
+            flops=10**12, bytes_accessed=4*10**8, transcendentals=0
+        ),
+        compiler_params=pltpu.CompilerParams(vmem_limit_bytes=4 * MIB),
         name="route",
-    )(targets, routes.T, route_weights.T, tokens)
+    )(routes.T, route_weights.T, tokens)
 
     def trade(x, step):
         pairs = [
@@ -141,9 +117,8 @@
         )
 
     gate, up, down = gate_proj[0], up_proj[0], down_proj[0]
-    mine, gate = lax.optimization_barrier((trade_all(outgoing), fetch(gate, 8)))
+    mine = trade_all(outgoing)
     both = jnp.concatenate([mine, swap(mine, "expert")])
-    both, up = lax.optimization_barrier((both, fetch(up, 8)))
     if tiles == 2:
         received = jnp.concatenate([both, swap(both, "tile")])
     else:
@@ -153,21 +128,19 @@
     partials = pl.pallas_call(
         functools.partial(ffn_kernel, block),
         out_shape=jax.ShapeDtypeStruct((count, width), BF16),
-        in_specs=[vmem, vmem, vmem, pl.BlockSpec(memory_space=pltpu.HBM)],
+        in_specs=[vmem, vmem, vmem, vmem],
         out_specs=vmem,
         scratch_shapes=[
             pltpu.VMEM((count, hidden), BF16),
-            pltpu.VMEM((hidden, width), BF16),
-            pltpu.SemaphoreType.DMA((width // 256,)),
         ],
-        compiler_params=pltpu.CompilerParams(vmem_limit_bytes=20 * MIB),
+        compiler_params=pltpu.CompilerParams(vmem_limit_bytes=8 * MIB),
         cost_estimate=pl.CostEstimate(
             flops=6 * count * width * hidden,
             bytes_accessed=6 * width * hidden,
             transcendentals=count * hidden,
         ),
         name="ffn",
-    )(received, gate, up, pltpu.with_memory_space_constraint(down, pltpu.HBM))
+    )(received, gate, up, down)
     if tiles == 2:
         half = count // 2
         both = add(partials[:half], swap(partials[half:], "tile"))
@@ -183,6 +156,7 @@
         out_shape=jax.ShapeDtypeStruct((rows, width), BF16),
         in_specs=[vmem, vmem],
         out_specs=vmem,
+        compiler_params=pltpu.CompilerParams(vmem_limit_bytes=4 * MIB),
         name="combine",
     )(comb, results)
 

time: 52.4 us -> 43.4 us (0.83)
  Pallas kernels: 22.7 us -> 6.54 us
  waiting for transfers between devices: 13.1 us -> 20.4 us
  local copies, waits for them, and re-layouts: 0.94 us -> 2.39 us
  other arithmetic: 1.61 us -> 0.17 us
    pallas_call x2 -> x0, Pallas kernels: 9.17 us -> none  [fetch(): pl.pallas_call(fetch_kernel, out_shape=pltpu.VMEM(array.shape, array.dtyp...]
    pallas_call x1, Pallas kernels: 9.83 us -> 5.4 us  [shards(): pl.pallas_call(functools.partial(ffn_kernel, block), out_shape=jax.ShapeD...]
    ppermute x4, waiting for transfers between devices: 8.92 us -> 13 us  [swap(): lax.ppermute(x, axis, [(i, i ^ 1) for i in range(lax.axis_size(axis))])]
    ppermute x6, waiting for transfers between devices: 4.21 us -> 7.43 us  [trade(): return lax.ppermute(x, 'expert', pairs)]
    unnamed x0 -> x16, local copies, waits for them, and re-layouts: none -> 2.28 us
    pallas_call x1, Pallas kernels: 1.92 us -> 0.3 us  [shards(): pl.pallas_call(functools.partial(route_kernel, experts, capacity), out_sh...]
    pallas_call x1, Pallas kernels: 1.79 us -> 0.84 us  [shards(): pl.pallas_call(combine_kernel, out_shape=jax.ShapeDtypeStruct((rows, widt...]
    slice x2 -> x1, local copies, waits for them, and re-layouts: 0.9 us -> 0.02 us  [trade_all(): blocks[0]]
  transfers between devices with their start and end apart: 10 -> 10, of which waited for: 5 -> 8; matrix products, arithmetic and copies ran while one was open for 0% -> 0% of each run, Pallas kernels for 18% -> 0%
where the time goes in v2:
time: 43.4 us; the launch traced here: 43.2 us
  waiting for transfers between devices  20.4 us (47%)
  starting transfers between devices  13.6 us (31%)
  Pallas kernels  6.54 us (15%)
  local copies, waits for them, and re-layouts  2.39 us (6%)
    ppermute x4, waiting for transfers between devices, swap(): lax.ppermute(x, axis, [(i, i ^ 1) for i in range(lax.axis_size(axis))])  13 us
    ppermute x6, starting transfers between devices, trade(): return lax.ppermute(x, 'expert', pairs)  10.2 us
    ppermute x6, waiting for transfers between devices, trade(): return lax.ppermute(x, 'expert', pairs)  7.43 us
    pallas_call x1, Pallas kernels, shards(): pl.pallas_call(functools.partial(ffn_kernel, block), out_shape=jax.ShapeD...  5.4 us
    ppermute x4, starting transfers between devices, swap(): lax.ppermute(x, axis, [(i, i ^ 1) for i in range(lax.axis_size(axis))])  3.38 us
    unnamed x16, local copies, waits for them, and re-layouts  2.28 us
  transfers between devices with their start and end apart: 10, of which 8 were waited for; matrix products, arithmetic and copies ran while one was open for 0% of the time, Pallas kernels for 0%

profile of v2, /device:TPU:0, one launch (start us, length us, event | category | flops | bytes accessed | tf_op | source)
XLA Modules:
  0.0 43.2 jit_solution(14142455148944226508)
XLA Ops:
  0.0 0.9 %copy-done.3 = bf16[16,3072]{1,0:T(8,128)(2,1)S(1)} copy-done((bf16[16,3072]{1,0:T(8,128)(2,1)S(1)}, bf16[16,3072]{1,0:T(8,128)(2,1)}, u32[]{:S(2)}) %copy-start.3) | copy-done | bytes 98328
  0.9 0.7 %copy-done.4 = s32[16,2]{0,1:T(2,128)S(1)} copy-done((s32[16,2]{0,1:T(2,128)S(1)}, s32[16,2]{0,1:T(2,128)}, u32[]{:S(2)}) %copy-start.4) | copy-done | bytes 152
  1.6 0.7 %copy-done.5 = bf16[16,2]{0,1:T(2,128)(2,1)S(1)} copy-done((bf16[16,2]{0,1:T(2,128)(2,1)S(1)}, bf16[16,2]{0,1:T(2,128)(2,1)}, u32[]{:S(2)}) %copy-start.5) | copy-done | bytes 88
  2.2 0.3 route.1
  2.6 5.1 %collective-permute-start.2 = (bf16[8,3072]{1,0:T(8,128)(2,1)S(1)}, bf16[8,3072]{1,0:T(8,128)(2,1)S(1)}, u32[]{:S(2)}, u32[]{:S(2)}) collective-permute-start(bf16[8,3072]{1,0:T(8,128)(2,1)S(1)} %get-tuple-element.17), channel_id=1, source_target_pairs={{0,12},{2,14},{4,8},{6,10},{8,4},{10,6},{12,0},{14,2},{1,13},{3,15... | collective-permute-start | bytes 147464 | tf_op jit(solution)/shard_map/ppermute | solution.py:106
  7.7 0.6 %collective-permute-start = (bf16[8,3072]{1,0:T(8,128)(2,1)S(1)}, bf16[8,3072]{1,0:T(8,128)(2,1)S(1)}, u32[]{:S(2)}, u32[]{:S(2)}) collective-permute-start(bf16[8,3072]{1,0:T(8,128)(2,1)S(1)} %get-tuple-element.19), channel_id=1, source_target_pairs={{0,4},{2,6},{4,0},{6,2},{8,12},{10,14},{12,8},{14,10},{1,5},{3,7},... | collective-permute-start | bytes 147464 | tf_op jit(solution)/shard_map/ppermute | solution.py:106
  8.3 1.6 %collective-permute-done.2 = bf16[8,3072]{1,0:T(8,128)(2,1)S(1)} collective-permute-done((bf16[8,3072]{1,0:T(8,128)(2,1)S(1)}, bf16[8,3072]{1,0:T(8,128)(2,1)S(1)}, u32[]{:S(2)}, u32[]{:S(2)}) %collective-permute-start.2) | collective-permute-done | bytes 49184 | tf_op jit(solution)/shard_map/ppermute | solution.py:106
  9.9 2.8 %collective-permute-done.1 = bf16[8,3072]{1,0:T(8,128)(2,1)S(1)} collective-permute-done((bf16[8,3072]{1,0:T(8,128)(2,1)S(1)}, bf16[8,3072]{1,0:T(8,128)(2,1)S(1)}, u32[]{:S(2)}, u32[]{:S(2)}) %collective-permute-start.1) | collective-permute-done | bytes 49184 | tf_op jit(solution)/shard_map/ppermute | solution.py:106
  12.7 1.6 %collective-permute-start.3 = (bf16[32,3072]{1,0:T(8,128)(2,1)S(1)}, bf16[32,3072]{1,0:T(8,128)(2,1)S(1)}, u32[]{:S(2)}, u32[]{:S(2)}) collective-permute-start(bf16[32,3072]{1,0:T(8,128)(2,1)S(1)} %pad_maximum_fusion), channel_id=1, source_target_pairs={{0,2},{2,0},{4,6},{6,4},{8,10},{10,8},{12,14},{14,12},{1,3},{3,1},... | collective-permute-start | bytes 589832 | tf_op jit(solution)/shard_map/ppermute | solution.py:111
  14.3 4.2 %collective-permute-done.3 = bf16[32,3072]{1,0:T(8,128)(2,1)S(1)} collective-permute-done((bf16[32,3072]{1,0:T(8,128)(2,1)S(1)}, bf16[32,3072]{1,0:T(8,128)(2,1)S(1)}, u32[]{:S(2)}, u32[]{:S(2)}) %collective-permute-start.3) | collective-permute-done | bytes 196640 | tf_op jit(solution)/shard_map/ppermute | solution.py:111
  18.5 0.1 collective-permute-start.4
  18.6 1.7 %collective-permute-done.4 = bf16[64,3072]{1,0:T(8,128)(2,1)S(1)} collective-permute-done((bf16[64,3072]{1,0:T(8,128)(2,1)S(1)}, bf16[64,3072]{1,0:T(8,128)(2,1)S(1)}, u32[]{:S(2)}, u32[]{:S(2)}) %collective-permute-start.4) | collective-permute-done | bytes 393248 | tf_op jit(solution)/shard_map/ppermute | solution.py:111
  20.4 5.4 %ffn.1 = bf16[128,3072]{1,0:T(8,128)(2,1)S(1)} custom-call(bf16[128,3072]{1,0:T(8,128)(2,1)S(1)} %constant_dynamic-update-slice_fusion.5.rows_ref, bf16[3072,2048]{1,0:T(8,128)(2,1)S(1)} %bitcast.5, bf16[3072,2048]{1,0:T(8,128)(2,1)S(1)} %bitcast.6, bf16[2048,3072]{1,0:T(8,128)(2,1)S(1)} %bitcast.7), custom_call_target="tpu_custom_call" | custom-call | flops 4831838208 | bytes 37748736 | tf_op jit(solution)/shard_map/ffn/pallas_call | solution.py:128
  25.8 0.2 collective-permute-start.5
  26.0 1.6 %collective-permute-done.5 = bf16[64,3072]{1,0:T(8,128)(2,1)S(1)} collective-permute-done((bf16[64,3072]{1,0:T(8,128)(2,1)S(1)}, bf16[64,3072]{1,0:T(8,128)(2,1)S(1)}, u32[]{:S(2)}, u32[]{:S(2)}) %collective-permute-start.5) | collective-permute-done | bytes 393248 | tf_op jit(solution)/shard_map/ppermute | solution.py:111
  27.6 0.1 add_convert_fusion
  27.7 1.6 %collective-permute-start.6 = (bf16[32,3072]{1,0:T(8,128)(2,1)S(1)}, bf16[32,3072]{1,0:T(8,128)(2,1)S(1)}, u32[]{:S(2)}, u32[]{:S(2)}) collective-permute-start(bf16[32,3072]{1,0:T(8,128)(2,1)S(1)} %slice.59), channel_id=1, source_target_pairs={{0,2},{2,0},{4,6},{6,4},{8,10},{10,8},{12,14},{14,12},{1,3},{3,1},... | collective-permute-start | bytes 589832 | tf_op jit(solution)/shard_map/ppermute | solution.py:111
  29.3 5.5 %collective-permute-done.6 = bf16[32,3072]{1,0:T(8,128)(2,1)S(1)} collective-permute-done((bf16[32,3072]{1,0:T(8,128)(2,1)S(1)}, bf16[32,3072]{1,0:T(8,128)(2,1)S(1)}, u32[]{:S(2)}, u32[]{:S(2)}) %collective-permute-start.6) | collective-permute-done | bytes 196640 | tf_op jit(solution)/shard_map/ppermute | solution.py:111
  34.8 2.1 %collective-permute-start.9 = (bf16[8,3072]{1,0:T(8,128)(2,1)S(1)}, bf16[8,3072]{1,0:T(8,128)(2,1)S(1)}, u32[]{:S(2)}, u32[]{:S(2)}) collective-permute-start(bf16[8,3072]{1,0:T(8,128)(2,1)S(1)} %get-tuple-element.10), channel_id=1, source_target_pairs={{0,12},{2,14},{4,8},{6,10},{8,4},{10,6},{12,0},{14,2},{1,13},{3,15... | collective-permute-start | bytes 147464 | tf_op jit(solution)/shard_map/ppermute | solution.py:106
  36.9 0.1 collective-permute-start.8
  37.1 2.2 %collective-permute-start.7 = (bf16[8,3072]{1,0:T(8,128)(2,1)S(1)}, bf16[8,3072]{1,0:T(8,128)(2,1)S(1)}, u32[]{:S(2)}, u32[]{:S(2)}) collective-permute-start(bf16[8,3072]{1,0:T(8,128)(2,1)S(1)} %get-tuple-element.12), channel_id=1, source_target_pairs={{0,4},{2,6},{4,0},{6,2},{8,12},{10,14},{12,8},{14,10},{1,5},{3,7},... | collective-permute-start | bytes 147464 | tf_op jit(solution)/shard_map/ppermute | solution.py:106
  39.3 1.8 %collective-permute-done.9 = bf16[8,3072]{1,0:T(8,128)(2,1)S(1)} collective-permute-done((bf16[8,3072]{1,0:T(8,128)(2,1)S(1)}, bf16[8,3072]{1,0:T(8,128)(2,1)S(1)}, u32[]{:S(2)}, u32[]{:S(2)}) %collective-permute-start.9) | collective-permute-done | bytes 49184 | tf_op jit(solution)/shard_map/ppermute | solution.py:106
  41.1 1.2 %collective-permute-done.8 = bf16[8,3072]{1,0:T(8,128)(2,1)S(1)} collective-permute-done((bf16[8,3072]{1,0:T(8,128)(2,1)S(1)}, bf16[8,3072]{1,0:T(8,128)(2,1)S(1)}, u32[]{:S(2)}, u32[]{:S(2)}) %collective-permute-start.8) | collective-permute-done | bytes 49184 | tf_op jit(solution)/shard_map/ppermute | solution.py:106
  42.4 0.8 %combine.1 = bf16[16,3072]{1,0:T(8,128)(2,1)} custom-call(bf16[32,16]{1,0:T(8,128)(2,1)S(1)} %get-tuple-element.7.comb_ref, bf16[32,3072]{1,0:T(8,128)(2,1)S(1)} %pad_maximum_fusion.1.results_ref), custom_call_target="tpu_custom_call" | custom-call | tf_op jit(solution)/shard_map/combine/pallas_call | solution.py:154
  (24 shorter events, 0.3 us)
Async XLA Ops:
  0.0 0.9 %copy-start.3 = (bf16[16,3072]{1,0:T(8,128)(2,1)S(1)}, bf16[16,3072]{1,0:T(8,128)(2,1)}, u32[]{:S(2)}) copy-start(bf16[16,3072]{1,0:T(8,128)(2,1)} %tokens_ref.1) | copy-start | bytes 294916
  0.9 0.7 %copy-start.4 = (s32[16,2]{0,1:T(2,128)S(1)}, s32[16,2]{0,1:T(2,128)}, u32[]{:S(2)}) copy-start(s32[16,2]{0,1:T(2,128)} %param.7) | copy-start | bytes 388
  1.6 0.7 %copy-start.5 = (bf16[16,2]{0,1:T(2,128)(2,1)S(1)}, bf16[16,2]{0,1:T(2,128)(2,1)}, u32[]{:S(2)}) copy-start(bf16[16,2]{0,1:T(2,128)(2,1)} %param.8) | copy-start | bytes 196
  2.2 18.1 %copy-start = (bf16[1,3072,2048]{2,1,0:T(8,128)(2,1)S(1)}, bf16[1,3072,2048]{2,1,0:T(8,128)(2,1)}, u32[]{:S(2)}) copy-start(bf16[1,3072,2048]{2,1,0:T(8,128)(2,1)} %param.9) | copy-start | bytes 37748740
  2.2 18.1 %copy-start.1 = (bf16[1,3072,2048]{2,1,0:T(8,128)(2,1)S(1)}, bf16[1,3072,2048]{2,1,0:T(8,128)(2,1)}, u32[]{:S(2)}) copy-start(bf16[1,3072,2048]{2,1,0:T(8,128)(2,1)} %param.10) | copy-start | bytes 37748740
  2.2 18.2 %copy-start.2 = (bf16[1,2048,3072]{2,1,0:T(8,128)(2,1)S(1)}, bf16[1,2048,3072]{2,1,0:T(8,128)(2,1)}, u32[]{:S(2)}) copy-start(bf16[1,2048,3072]{2,1,0:T(8,128)(2,1)} %param.11) | copy-start | bytes 37748740
  2.6 7.3 %collective-permute-start.2 = (bf16[8,3072]{1,0:T(8,128)(2,1)S(1)}, bf16[8,3072]{1,0:T(8,128)(2,1)S(1)}, u32[]{:S(2)}, u32[]{:S(2)}) collective-permute-start(bf16[8,3072]{1,0:T(8,128)(2,1)S(1)} %get-tuple-element.17), channel_id=1, source_target_pairs={{0,12},{2,14},{4,8},{6,10},{8,4},{10,6},{12,0},{14,2},{1,13},{3,15... | collective-permute-start | bytes 147464 | tf_op jit(solution)/shard_map/ppermute | solution.py:106
  7.7 5.0 %collective-permute-start.1 = (bf16[8,3072]{1,0:T(8,128)(2,1)S(1)}, bf16[8,3072]{1,0:T(8,128)(2,1)S(1)}, u32[]{:S(2)}, u32[]{:S(2)}) collective-permute-start(bf16[8,3072]{1,0:T(8,128)(2,1)S(1)} %get-tuple-element.18), channel_id=1, source_target_pairs={{0,8},{2,10},{4,12},{6,14},{8,0},{10,2},{12,4},{14,6},{1,9},{3,11}... | collective-permute-start | bytes 147464 | tf_op jit(solution)/shard_map/ppermute | solution.py:106
  7.7 5.0 %collective-permute-start = (bf16[8,3072]{1,0:T(8,128)(2,1)S(1)}, bf16[8,3072]{1,0:T(8,128)(2,1)S(1)}, u32[]{:S(2)}, u32[]{:S(2)}) collective-permute-start(bf16[8,3072]{1,0:T(8,128)(2,1)S(1)} %get-tuple-element.19), channel_id=1, source_target_pairs={{0,4},{2,6},{4,0},{6,2},{8,12},{10,14},{12,8},{14,10},{1,5},{3,7},... | collective-permute-start | bytes 147464 | tf_op jit(solution)/shard_map/ppermute | solution.py:106
  12.7 5.8 %collective-permute-start.3 = (bf16[32,3072]{1,0:T(8,128)(2,1)S(1)}, bf16[32,3072]{1,0:T(8,128)(2,1)S(1)}, u32[]{:S(2)}, u32[]{:S(2)}) collective-permute-start(bf16[32,3072]{1,0:T(8,128)(2,1)S(1)} %pad_maximum_fusion), channel_id=1, source_target_pairs={{0,2},{2,0},{4,6},{6,4},{8,10},{10,8},{12,14},{14,12},{1,3},{3,1},... | collective-permute-start | bytes 589832 | tf_op jit(solution)/shard_map/ppermute | solution.py:111
  18.5 1.8 %collective-permute-start.4 = (bf16[64,3072]{1,0:T(8,128)(2,1)S(1)}, bf16[64,3072]{1,0:T(8,128)(2,1)S(1)}, u32[]{:S(2)}, u32[]{:S(2)}) collective-permute-start(bf16[64,3072]{1,0:T(8,128)(2,1)S(1)} %get-tuple-element.13), channel_id=1, source_target_pairs={{0,1},{1,0},{2,3},{3,2},{4,5},{5,4},{6,7},{7,6},{8,9},{9,8},{10,11... | collective-permute-start | bytes 1179656 | tf_op jit(solution)/shard_map/ppermute | solution.py:111
  25.8 1.8 %collective-permute-start.5 = (bf16[64,3072]{1,0:T(8,128)(2,1)S(1)}, bf16[64,3072]{1,0:T(8,128)(2,1)S(1)}, u32[]{:S(2)}, u32[]{:S(2)}) collective-permute-start(bf16[64,3072]{1,0:T(8,128)(2,1)S(1)} %slice.57), channel_id=1, source_target_pairs={{0,1},{1,0},{2,3},{3,2},{4,5},{5,4},{6,7},{7,6},{8,9},{9,8},{10,11... | collective-permute-start | bytes 1179656 | tf_op jit(solution)/shard_map/ppermute | solution.py:111
  27.7 7.0 %collective-permute-start.6 = (bf16[32,3072]{1,0:T(8,128)(2,1)S(1)}, bf16[32,3072]{1,0:T(8,128)(2,1)S(1)}, u32[]{:S(2)}, u32[]{:S(2)}) collective-permute-start(bf16[32,3072]{1,0:T(8,128)(2,1)S(1)} %slice.59), channel_id=1, source_target_pairs={{0,2},{2,0},{4,6},{6,4},{8,10},{10,8},{12,14},{14,12},{1,3},{3,1},... | collective-permute-start | bytes 589832 | tf_op jit(solution)/shard_map/ppermute | solution.py:111
  34.8 6.3 %collective-permute-start.9 = (bf16[8,3072]{1,0:T(8,128)(2,1)S(1)}, bf16[8,3072]{1,0:T(8,128)(2,1)S(1)}, u32[]{:S(2)}, u32[]{:S(2)}) collective-permute-start(bf16[8,3072]{1,0:T(8,128)(2,1)S(1)} %get-tuple-element.10), channel_id=1, source_target_pairs={{0,12},{2,14},{4,8},{6,10},{8,4},{10,6},{12,0},{14,2},{1,13},{3,15... | collective-permute-start | bytes 147464 | tf_op jit(solution)/shard_map/ppermute | solution.py:106
  36.9 5.5 %collective-permute-start.8 = (bf16[8,3072]{1,0:T(8,128)(2,1)S(1)}, bf16[8,3072]{1,0:T(8,128)(2,1)S(1)}, u32[]{:S(2)}, u32[]{:S(2)}) collective-permute-start(bf16[8,3072]{1,0:T(8,128)(2,1)S(1)} %get-tuple-element.11), channel_id=1, source_target_pairs={{0,8},{2,10},{4,12},{6,14},{8,0},{10,2},{12,4},{14,6},{1,9},{3,11}... | collective-permute-start | bytes 147464 | tf_op jit(solution)/shard_map/ppermute | solution.py:106
  37.1 5.3 %collective-permute-start.7 = (bf16[8,3072]{1,0:T(8,128)(2,1)S(1)}, bf16[8,3072]{1,0:T(8,128)(2,1)S(1)}, u32[]{:S(2)}, u32[]{:S(2)}) collective-permute-start(bf16[8,3072]{1,0:T(8,128)(2,1)S(1)} %get-tuple-element.12), channel_id=1, source_target_pairs={{0,4},{2,6},{4,0},{6,2},{8,12},{10,14},{12,8},{14,10},{1,5},{3,7},... | collective-permute-start | bytes 147464 | tf_op jit(solution)/shard_map/ppermute | solution.py:106

commit v3 on v2

v3 whole, which is shorter than its diff:
```python
import functools

import jax
import jax.numpy as jnp
from jax import lax
from jax.experimental import pallas as pl
from jax.experimental.pallas import tpu as pltpu
from jax.sharding import PartitionSpec as P

F32 = jnp.float32
BF16 = jnp.bfloat16
MIB = 2**20


def partner(expert, step):
    return expert ^ step


def choose(experts, capacity, routes):
    me = lax.axis_index("expert") // 2
    slots, rows = experts * capacity, routes.shape[1]
    slot = lax.broadcasted_iota(jnp.int32, (slots, rows), 0)
    step = slot // capacity
    place = slot - step * capacity
    expert = jnp.zeros_like(slot)
    for s in range(experts):
        expert = jnp.where(step == s, partner(me, s), expert)
    first, second = routes[0:1, :] == expert, routes[1:2, :] == expert
    named = jnp.where(first | second, 1.0, 0.0)
    before = jnp.where(
        lax.broadcasted_iota(jnp.int32, (rows, rows), 0)
        < lax.broadcasted_iota(jnp.int32, (rows, rows), 1),
        1.0,
        0.0,
    )
    ahead = jnp.dot(named.astype(BF16), before.astype(BF16), preferred_element_type=F32)
    return jnp.where(ahead == place.astype(F32), named, 0.0), first


def route_kernel(experts, capacity, routes_hbm, tokens_hbm, out_ref, routes_ref, tokens_ref, sems):
    copies = [
        pltpu.make_async_copy(routes_hbm, routes_ref, sems.at[0]),
        pltpu.make_async_copy(tokens_hbm, tokens_ref, sems.at[1]),
    ]
    for copy in copies:
        copy.start()
    for copy in copies:
        copy.wait()
    chosen, _ = choose(experts, capacity, routes_ref[...])
    out_ref[...] = jnp.dot(
        chosen.astype(BF16), tokens_ref[...], preferred_element_type=F32
    ).astype(BF16)


def weigh_kernel(experts, capacity, routes_ref, weights_ref, comb_ref):
    chosen, first = choose(experts, capacity, routes_ref[...])
    weights = weights_ref[...].astype(F32)
    weight = jnp.where(first, weights[0:1, :], weights[1:2, :])
    comb_ref[...] = (chosen * weight).astype(BF16)


def ffn_kernel(width, rows_ref, gate_ref, up_ref, down_ref, out_ref, hidden_ref):
    for at in range(0, gate_ref.shape[1], width):
        part = slice(at, at + width)
        gate = jnp.dot(rows_ref[...], gate_ref[:, part], preferred_element_type=F32)
        up = jnp.dot(rows_ref[...], up_ref[:, part], preferred_element_type=F32)
        hidden_ref[:, part] = (gate / (1.0 + jnp.exp(-gate)) * up).astype(BF16)
    for at in range(0, down_ref.shape[1], 256):
        part = slice(at, at + 256)
        out_ref[:, part] = jnp.dot(
            hidden_ref[...], down_ref[:, part], preferred_element_type=F32
        ).astype(BF16)


def combine_kernel(comb_ref, results_ref, out_ref):
    out_ref[...] = lax.dot_general(
        comb_ref[...],
        results_ref[...],
        (((0,), (0,)), ((), ())),
        preferred_element_type=F32,
    ).astype(BF16)


def add(a, b):
    return (a.astype(F32) + b.astype(F32)).astype(BF16)


def shards(tokens, routes, route_weights, gate_proj, up_proj, down_proj):
    groups = lax.axis_size("expert")
    tiles = lax.axis_size("tile")
    experts = groups // 2
    rows, width = tokens.shape
    capacity = max(2, 2 * rows // experts)
    slots = experts * capacity
    vmem = pl.BlockSpec(memory_space=pltpu.VMEM)
    hbm = pl.BlockSpec(memory_space=pltpu.HBM)
    small = pltpu.CompilerParams(vmem_limit_bytes=4 * MIB)
    outgoing = pl.pallas_call(
        functools.partial(route_kernel, experts, capacity),
        out_shape=pltpu.VMEM((slots, width), BF16),
        in_specs=[hbm, hbm],
        out_specs=vmem,
        scratch_shapes=[
            pltpu.VMEM((2, rows), jnp.int32),
            pltpu.VMEM((rows, width), BF16),
            pltpu.SemaphoreType.DMA((2,)),
        ],
        cost_estimate=pl.CostEstimate(
            flops=10**12, bytes_accessed=4 * 10**8, transcendentals=0
        ),
        compiler_params=small,
        name="route",
    )(
        pltpu.with_memory_space_constraint(routes.T, pltpu.HBM),
        pltpu.with_memory_space_constraint(tokens, pltpu.HBM),
    )
    comb = pl.pallas_call(
        functools.partial(weigh_kernel, experts, capacity),
        out_shape=jax.ShapeDtypeStruct((slots, rows), BF16),
        in_specs=[vmem, vmem],
        out_specs=vmem,
        compiler_params=small,
        name="weigh",
    )(routes.T, route_weights.T)

    def trade(x, step):
        pairs = [(g, 2 * partner(g // 2, step) + g % 2) for g in range(groups)]
        return lax.ppermute(x, "expert", pairs)

    def swap(x, axis):
        return lax.ppermute(x, axis, [(i, i ^ 1) for i in range(lax.axis_size(axis))])

    def join(blocks):
        return jnp.concatenate(blocks) if len(blocks) > 1 else blocks[0]

    def cut(block):
        return list(block.reshape(-1, capacity, width))

    steps = list(range(experts - 1, 0, -1))
    sent = cut(outgoing)
    here = {s: trade(sent[s], s) for s in steps}
    here[0] = sent[0]
    there = {}
    for group in [[0, steps[0]]] + [[s] for s in steps[1:]]:
        there.update(zip(group, cut(swap(join([here[s] for s in group]), "expert"))))
    order = [(side, s) for side in (0, 1) for s in range(experts)]
    both = join([side[s] for side in (here, there) for s in range(experts)])
    if tiles == 2:
        received = join([both, swap(both, "tile")])
    else:
        received = lax.all_gather(both, "tile", axis=0, tiled=True)
    gate, up, down = gate_proj[0], up_proj[0], down_proj[0]
    count, hidden = received.shape[0], gate.shape[1]
    block = min(256, hidden)
    partials = pl.pallas_call(
        functools.partial(ffn_kernel, block),
        out_shape=jax.ShapeDtypeStruct((count, width), BF16),
        in_specs=[vmem, vmem, vmem, vmem],
        out_specs=vmem,
        scratch_shapes=[
            pltpu.VMEM((count, hidden), BF16),
        ],
        compiler_params=pltpu.CompilerParams(vmem_limit_bytes=8 * MIB),
        cost_estimate=pl.CostEstimate(
            flops=6 * count * width * hidden,
            bytes_accessed=6 * width * hidden,
            transcendentals=count * hidden,
        ),
        name="ffn",
    )(received, gate, up, down)
    if tiles == 2:
        both = add(partials[: 2 * slots], swap(partials[2 * slots :], "tile"))
    else:
        pieces = lax.all_to_all(
            partials.reshape(tiles, 2 * slots, width), "tile", 0, 0, tiled=True
        )
        both = jnp.sum(pieces.astype(F32), axis=0).astype(BF16)
    summed = dict(zip(order, lax.optimization_barrier(cut(both))))
    results = {}
    for group in [[s] for s in steps[:-1]] + [[steps[-1], 0]]:
        back = cut(swap(join([summed[1, s] for s in group]), "expert"))
        for s, block in zip(group, back):
            total = add(summed[0, s], block)
            results[s] = trade(total, s) if s else total
    results = join([results[s] for s in range(experts)])
    return pl.pallas_call(
        combine_kernel,
        out_shape=jax.ShapeDtypeStruct((rows, width), BF16),
        in_specs=[vmem, vmem],
        out_specs=vmem,
        compiler_params=pltpu.CompilerParams(vmem_limit_bytes=4 * MIB),
        name="combine",
    )(comb, results)


def solution(mesh):
    placed = (
        P(("parts", "expert", "tile"), None),
        P(("parts", "expert", "tile"), None),
        P(("parts", "expert", "tile"), None),
        P("expert", None, "tile"),
        P("expert", None, "tile"),
        P("expert", "tile", None),
    )
    return jax.shard_map(
        shards,
        mesh=mesh,
        in_specs=placed,
        out_specs=P(("parts", "expert", "tile"), None),
        check_vma=False,
    )
```

time: 43.4 us -> 41 us (0.945)
  waiting for transfers between devices: 20.4 us -> 15.2 us
  starting transfers between devices: 13.6 us -> 17.3 us
  local copies, waits for them, and re-layouts: 2.39 us -> 0.19 us
  Pallas kernels: 6.54 us -> 7.76 us
    ppermute x4 -> x8, starting transfers between devices: 3.38 us -> 7.85 us  [swap(): lax.ppermute(x, axis, [(i, i ^ 1) for i in range(lax.axis_size(axis))])]
    ppermute x4 -> x8, waiting for transfers between devices: 13 us -> 9.41 us  [swap(): lax.ppermute(x, axis, [(i, i ^ 1) for i in range(lax.axis_size(axis))])]
    unnamed x16 -> x20, local copies, waits for them, and re-layouts: 2.28 us -> 0.1 us
    ppermute x6, waiting for transfers between devices: 7.43 us -> 5.78 us  [trade(): return lax.ppermute(x, 'expert', pairs)]
    pallas_call x1, Pallas kernels: 0.3 us -> 1.38 us  [shards(): pl.pallas_call(functools.partial(route_kernel, experts, capacity), out_sh...]
    ppermute x6, starting transfers between devices: 10.2 us -> 9.48 us  [trade(): return lax.ppermute(x, 'expert', pairs)]
  transfers between devices with their start and end apart: 10 -> 14, of which waited for: 8 -> 11; matrix products, arithmetic and copies ran while one was open for 0% -> 0% of each run, Pallas kernels for 0% -> 0%
where the time goes in v3:
time: 41 us; the launch traced here: 40.8 us
  starting transfers between devices  17.3 us (42%)
  waiting for transfers between devices  15.2 us (37%)
  Pallas kernels  7.76 us (19%)
    ppermute x6, starting transfers between devices, trade(): return lax.ppermute(x, 'expert', pairs)  9.48 us
    ppermute x8, waiting for transfers between devices, swap(): lax.ppermute(x, axis, [(i, i ^ 1) for i in range(lax.axis_size(axis))])  9.41 us
    ppermute x8, starting transfers between devices, swap(): lax.ppermute(x, axis, [(i, i ^ 1) for i in range(lax.axis_size(axis))])  7.85 us
    ppermute x6, waiting for transfers between devices, trade(): return lax.ppermute(x, 'expert', pairs)  5.78 us
    pallas_call x1, Pallas kernels, shards(): pl.pallas_call(functools.partial(ffn_kernel, block), out_shape=jax.ShapeD...  5.39 us
    pallas_call x1, Pallas kernels, shards(): pl.pallas_call(functools.partial(route_kernel, experts, capacity), out_sh...  1.38 us
    pallas_call x1, Pallas kernels, shards(): pl.pallas_call(combine_kernel, out_shape=jax.ShapeDtypeStruct((rows, widt...  0.84 us
  transfers between devices with their start and end apart: 14, of which 11 were waited for; matrix products, arithmetic and copies ran while one was open for 0% of the time, Pallas kernels for 0%

profile of v3, /device:TPU:0, one launch (start us, length us, event | category | flops | bytes accessed | tf_op | source)
XLA Modules:
  0.0 40.8 jit_solution(14772573817897378749)
XLA Ops:
  0.0 1.4 %route.1 = bf16[32,3072]{1,0:T(8,128)(2,1)S(1)} custom-call(s32[2,16]{1,0:T(2,128)} %bitcast.8, bf16[16,3072]{1,0:T(8,128)(2,1)} %tokens_hbm.1), custom_call_target="tpu_custom_call" | custom-call | flops 999999995904 | bytes 400000000 | tf_op jit(solution)/shard_map/route/pallas_call | solution.py:98
  1.4 5.1 %collective-permute-start.2 = (bf16[8,3072]{1,0:T(8,128)(2,1)S(1)}, bf16[8,3072]{1,0:T(8,128)(2,1)S(1)}, u32[]{:S(2)}, u32[]{:S(2)}) collective-permute-start(bf16[8,3072]{1,0:T(8,128)(2,1)S(1)} %get-tuple-element.31), channel_id=1, source_target_pairs={{0,12},{2,14},{4,8},{6,10},{8,4},{10,6},{12,0},{14,2},{1,13},{3,15... | collective-permute-start | bytes 147464 | tf_op jit(solution)/shard_map/ppermute | solution.py:128
  6.5 0.6 %collective-permute-start.1 = (bf16[8,3072]{1,0:T(8,128)(2,1)S(1)}, bf16[8,3072]{1,0:T(8,128)(2,1)S(1)}, u32[]{:S(2)}, u32[]{:S(2)}) collective-permute-start(bf16[8,3072]{1,0:T(8,128)(2,1)S(1)} %get-tuple-element.32), channel_id=1, source_target_pairs={{0,8},{2,10},{4,12},{6,14},{8,0},{10,2},{12,4},{14,6},{1,9},{3,11}... | collective-permute-start | bytes 147464 | tf_op jit(solution)/shard_map/ppermute | solution.py:128
  7.2 1.6 %collective-permute-done.2 = bf16[8,3072]{1,0:T(8,128)(2,1)S(1)} collective-permute-done((bf16[8,3072]{1,0:T(8,128)(2,1)S(1)}, bf16[8,3072]{1,0:T(8,128)(2,1)S(1)}, u32[]{:S(2)}, u32[]{:S(2)}) %collective-permute-start.2) | collective-permute-done | bytes 49184 | tf_op jit(solution)/shard_map/ppermute | solution.py:128
  8.8 1.6 %collective-permute-start.3 = (bf16[16,3072]{1,0:T(8,128)(2,1)S(1)}, bf16[16,3072]{1,0:T(8,128)(2,1)S(1)}, u32[]{:S(2)}, u32[]{:S(2)}) collective-permute-start(bf16[16,3072]{1,0:T(8,128)(2,1)S(1)} %pad_maximum_fusion.1), channel_id=1, source_target_pairs={{0,2},{2,0},{4,6},{6,4},{8,10},{10,8},{12,14},{14,12},{1,3},{3,1},... | collective-permute-start | bytes 294920 | tf_op jit(solution)/shard_map/ppermute | solution.py:131
  10.4 0.2 collective-permute-done
  10.6 1.5 %collective-permute-start.4 = (bf16[8,3072]{1,0:T(8,128)(2,1)S(1)}, bf16[8,3072]{1,0:T(8,128)(2,1)S(1)}, u32[]{:S(2)}, u32[]{:S(2)}) collective-permute-start(bf16[8,3072]{1,0:T(8,128)(2,1)S(1)} %collective-permute-done), channel_id=1, source_target_pairs={{0,2},{2,0},{4,6},{6,4},{8,10},{10,8},{12,14},{14,12},{1,3},{3,1},... | collective-permute-start | bytes 147464 | tf_op jit(solution)/shard_map/ppermute | solution.py:131
  12.1 1.2 %collective-permute-start.5 = (bf16[8,3072]{1,0:T(8,128)(2,1)S(1)}, bf16[8,3072]{1,0:T(8,128)(2,1)S(1)}, u32[]{:S(2)}, u32[]{:S(2)}) collective-permute-start(bf16[8,3072]{1,0:T(8,128)(2,1)S(1)} %collective-permute-done.1), channel_id=1, source_target_pairs={{0,2},{2,0},{4,6},{6,4},{8,10},{10,8},{12,14},{14,12},{1,3},{3,1},... | collective-permute-start | bytes 147464 | tf_op jit(solution)/shard_map/ppermute | solution.py:131
  13.4 0.7 %collective-permute-done.3 = bf16[16,3072]{1,0:T(8,128)(2,1)S(1)} collective-permute-done((bf16[16,3072]{1,0:T(8,128)(2,1)S(1)}, bf16[16,3072]{1,0:T(8,128)(2,1)S(1)}, u32[]{:S(2)}, u32[]{:S(2)}) %collective-permute-start.3) | collective-permute-done | bytes 98336 | tf_op jit(solution)/shard_map/ppermute | solution.py:131
  14.0 0.7 %collective-permute-done.4 = bf16[8,3072]{1,0:T(8,128)(2,1)S(1)} collective-permute-done((bf16[8,3072]{1,0:T(8,128)(2,1)S(1)}, bf16[8,3072]{1,0:T(8,128)(2,1)S(1)}, u32[]{:S(2)}, u32[]{:S(2)}) %collective-permute-start.4) | collective-permute-done | bytes 49184 | tf_op jit(solution)/shard_map/ppermute | solution.py:131
  14.7 1.5 %collective-permute-done.5 = bf16[8,3072]{1,0:T(8,128)(2,1)S(1)} collective-permute-done((bf16[8,3072]{1,0:T(8,128)(2,1)S(1)}, bf16[8,3072]{1,0:T(8,128)(2,1)S(1)}, u32[]{:S(2)}, u32[]{:S(2)}) %collective-permute-start.5) | collective-permute-done | bytes 49184 | tf_op jit(solution)/shard_map/ppermute | solution.py:131
  16.4 1.7 %collective-permute-done.6 = bf16[64,3072]{1,0:T(8,128)(2,1)S(1)} collective-permute-done((bf16[64,3072]{1,0:T(8,128)(2,1)S(1)}, bf16[64,3072]{1,0:T(8,128)(2,1)S(1)}, u32[]{:S(2)}, u32[]{:S(2)}) %collective-permute-start.6) | collective-permute-done | bytes 393248 | tf_op jit(solution)/shard_map/ppermute | solution.py:131
  18.1 5.4 %ffn.1 = bf16[128,3072]{1,0:T(8,128)(2,1)S(1)} custom-call(bf16[128,3072]{1,0:T(8,128)(2,1)S(1)} %constant_dynamic-update-slice_fusion.6.rows_ref, bf16[3072,2048]{1,0:T(8,128)(2,1)S(1)} %bitcast.5, bf16[3072,2048]{1,0:T(8,128)(2,1)S(1)} %bitcast.6, bf16[2048,3072]{1,0:T(8,128)(2,1)S(1)} %bitcast.7), custom_call_target="tpu_custom_call" | custom-call | flops 4831838208 | bytes 37748736 | tf_op jit(solution)/shard_map/ffn/pallas_call | solution.py:155
  23.8 1.6 %collective-permute-done.7 = bf16[64,3072]{1,0:T(8,128)(2,1)S(1)} collective-permute-done((bf16[64,3072]{1,0:T(8,128)(2,1)S(1)}, bf16[64,3072]{1,0:T(8,128)(2,1)S(1)}, u32[]{:S(2)}, u32[]{:S(2)}) %collective-permute-start.7) | collective-permute-done | bytes 393248 | tf_op jit(solution)/shard_map/ppermute | solution.py:131
  25.5 1.2 %collective-permute-start.10 = (bf16[8,3072]{1,0:T(8,128)(2,1)S(1)}, bf16[8,3072]{1,0:T(8,128)(2,1)S(1)}, u32[]{:S(2)}, u32[]{:S(2)}) collective-permute-start(bf16[8,3072]{1,0:T(8,128)(2,1)S(1)} %get-tuple-element.18), channel_id=1, source_target_pairs={{0,2},{2,0},{4,6},{6,4},{8,10},{10,8},{12,14},{14,12},{1,3},{3,1},... | collective-permute-start | bytes 147464 | tf_op jit(solution)/shard_map/ppermute | solution.py:131
  26.7 0.9 %collective-permute-start.8 = (bf16[16,3072]{1,0:T(8,128)(2,1)S(1)}, bf16[16,3072]{1,0:T(8,128)(2,1)S(1)}, u32[]{:S(2)}, u32[]{:S(2)}) collective-permute-start(bf16[16,3072]{1,0:T(8,128)(2,1)S(1)} %pad_maximum_fusion.2), channel_id=1, source_target_pairs={{0,2},{2,0},{4,6},{6,4},{8,10},{10,8},{12,14},{14,12},{1,3},{3,1},... | collective-permute-start | bytes 294920 | tf_op jit(solution)/shard_map/ppermute | solution.py:131
  27.6 1.2 %collective-permute-start.12 = (bf16[8,3072]{1,0:T(8,128)(2,1)S(1)}, bf16[8,3072]{1,0:T(8,128)(2,1)S(1)}, u32[]{:S(2)}, u32[]{:S(2)}) collective-permute-start(bf16[8,3072]{1,0:T(8,128)(2,1)S(1)} %get-tuple-element.20), channel_id=1, source_target_pairs={{0,2},{2,0},{4,6},{6,4},{8,10},{10,8},{12,14},{14,12},{1,3},{3,1},... | collective-permute-start | bytes 147464 | tf_op jit(solution)/shard_map/ppermute | solution.py:131
  28.8 1.2 %collective-permute-done.10 = bf16[8,3072]{1,0:T(8,128)(2,1)S(1)} collective-permute-done((bf16[8,3072]{1,0:T(8,128)(2,1)S(1)}, bf16[8,3072]{1,0:T(8,128)(2,1)S(1)}, u32[]{:S(2)}, u32[]{:S(2)}) %collective-permute-start.10) | collective-permute-done | bytes 49184 | tf_op jit(solution)/shard_map/ppermute | solution.py:131
  30.1 0.7 %collective-permute-start.11 = (bf16[8,3072]{1,0:T(8,128)(2,1)S(1)}, bf16[8,3072]{1,0:T(8,128)(2,1)S(1)}, u32[]{:S(2)}, u32[]{:S(2)}) collective-permute-start(bf16[8,3072]{1,0:T(8,128)(2,1)S(1)} %add_convert_fusion.2), channel_id=1, source_target_pairs={{0,8},{2,10},{4,12},{6,14},{8,0},{10,2},{12,4},{14,6},{1,9},{3,11}... | collective-permute-start | bytes 147464 | tf_op jit(solution)/shard_map/ppermute | solution.py:128
  30.7 2.1 %collective-permute-done.12 = bf16[8,3072]{1,0:T(8,128)(2,1)S(1)} collective-permute-done((bf16[8,3072]{1,0:T(8,128)(2,1)S(1)}, bf16[8,3072]{1,0:T(8,128)(2,1)S(1)}, u32[]{:S(2)}, u32[]{:S(2)}) %collective-permute-start.12) | collective-permute-done | bytes 49184 | tf_op jit(solution)/shard_map/ppermute | solution.py:131
  32.8 3.0 %collective-permute-start.13 = (bf16[8,3072]{1,0:T(8,128)(2,1)S(1)}, bf16[8,3072]{1,0:T(8,128)(2,1)S(1)}, u32[]{:S(2)}, u32[]{:S(2)}) collective-permute-start(bf16[8,3072]{1,0:T(8,128)(2,1)S(1)} %add_convert_fusion.1), channel_id=1, source_target_pairs={{0,12},{2,14},{4,8},{6,10},{8,4},{10,6},{12,0},{14,2},{1,13},{3,15... | collective-permute-start | bytes 147464 | tf_op jit(solution)/shard_map/ppermute | solution.py:128
  36.1 2.7 %collective-permute-done.13 = bf16[8,3072]{1,0:T(8,128)(2,1)S(1)} collective-permute-done((bf16[8,3072]{1,0:T(8,128)(2,1)S(1)}, bf16[8,3072]{1,0:T(8,128)(2,1)S(1)}, u32[]{:S(2)}, u32[]{:S(2)}) %collective-permute-start.13) | collective-permute-done | bytes 49184 | tf_op jit(solution)/shard_map/ppermute | solution.py:128
  38.8 1.2 %collective-permute-done.9 = bf16[8,3072]{1,0:T(8,128)(2,1)S(1)} collective-permute-done((bf16[8,3072]{1,0:T(8,128)(2,1)S(1)}, bf16[8,3072]{1,0:T(8,128)(2,1)S(1)}, u32[]{:S(2)}, u32[]{:S(2)}) %collective-permute-start.9) | collective-permute-done | bytes 49184 | tf_op jit(solution)/shard_map/ppermute | solution.py:128
  40.0 0.8 %combine.1 = bf16[16,3072]{1,0:T(8,128)(2,1)} custom-call(bf16[32,16]{1,0:T(8,128)(2,1)S(1)} %weigh.1.comb_ref, bf16[32,3072]{1,0:T(8,128)(2,1)S(1)} %pad_maximum_fusion.results_ref), custom_call_target="tpu_custom_call" | custom-call | tf_op jit(solution)/shard_map/combine/pallas_call | solution.py:186
  (39 shorter events, 0.9 us)
Async XLA Ops:
  0.0 18.1 %copy-start = (bf16[1,3072,2048]{2,1,0:T(8,128)(2,1)S(1)}, bf16[1,3072,2048]{2,1,0:T(8,128)(2,1)}, u32[]{:S(2)}) copy-start(bf16[1,3072,2048]{2,1,0:T(8,128)(2,1)} %param.9) | copy-start | bytes 37748740
  0.0 18.1 %copy-start.1 = (bf16[1,3072,2048]{2,1,0:T(8,128)(2,1)S(1)}, bf16[1,3072,2048]{2,1,0:T(8,128)(2,1)}, u32[]{:S(2)}) copy-start(bf16[1,3072,2048]{2,1,0:T(8,128)(2,1)} %param.10) | copy-start | bytes 37748740
  0.0 18.1 %copy-start.2 = (bf16[1,2048,3072]{2,1,0:T(8,128)(2,1)S(1)}, bf16[1,2048,3072]{2,1,0:T(8,128)(2,1)}, u32[]{:S(2)}) copy-start(bf16[1,2048,3072]{2,1,0:T(8,128)(2,1)} %param.11) | copy-start | bytes 37748740
  1.4 7.4 %collective-permute-start.2 = (bf16[8,3072]{1,0:T(8,128)(2,1)S(1)}, bf16[8,3072]{1,0:T(8,128)(2,1)S(1)}, u32[]{:S(2)}, u32[]{:S(2)}) collective-permute-start(bf16[8,3072]{1,0:T(8,128)(2,1)S(1)} %get-tuple-element.31), channel_id=1, source_target_pairs={{0,12},{2,14},{4,8},{6,10},{8,4},{10,6},{12,0},{14,2},{1,13},{3,15... | collective-permute-start | bytes 147464 | tf_op jit(solution)/shard_map/ppermute | solution.py:128
  6.5 4.1 %collective-permute-start = (bf16[8,3072]{1,0:T(8,128)(2,1)S(1)}, bf16[8,3072]{1,0:T(8,128)(2,1)S(1)}, u32[]{:S(2)}, u32[]{:S(2)}) collective-permute-start(bf16[8,3072]{1,0:T(8,128)(2,1)S(1)} %get-tuple-element.33), channel_id=1, source_target_pairs={{0,4},{2,6},{4,0},{6,2},{8,12},{10,14},{12,8},{14,10},{1,5},{3,7},... | collective-permute-start | bytes 147464 | tf_op jit(solution)/shard_map/ppermute | solution.py:128
  6.5 5.6 %collective-permute-start.1 = (bf16[8,3072]{1,0:T(8,128)(2,1)S(1)}, bf16[8,3072]{1,0:T(8,128)(2,1)S(1)}, u32[]{:S(2)}, u32[]{:S(2)}) collective-permute-start(bf16[8,3072]{1,0:T(8,128)(2,1)S(1)} %get-tuple-element.32), channel_id=1, source_target_pairs={{0,8},{2,10},{4,12},{6,14},{8,0},{10,2},{12,4},{14,6},{1,9},{3,11}... | collective-permute-start | bytes 147464 | tf_op jit(solution)/shard_map/ppermute | solution.py:128
  8.8 5.2 %collective-permute-start.3 = (bf16[16,3072]{1,0:T(8,128)(2,1)S(1)}, bf16[16,3072]{1,0:T(8,128)(2,1)S(1)}, u32[]{:S(2)}, u32[]{:S(2)}) collective-permute-start(bf16[16,3072]{1,0:T(8,128)(2,1)S(1)} %pad_maximum_fusion.1), channel_id=1, source_target_pairs={{0,2},{2,0},{4,6},{6,4},{8,10},{10,8},{12,14},{14,12},{1,3},{3,1},... | collective-permute-start | bytes 294920 | tf_op jit(solution)/shard_map/ppermute | solution.py:131
  10.6 4.1 %collective-permute-start.4 = (bf16[8,3072]{1,0:T(8,128)(2,1)S(1)}, bf16[8,3072]{1,0:T(8,128)(2,1)S(1)}, u32[]{:S(2)}, u32[]{:S(2)}) collective-permute-start(bf16[8,3072]{1,0:T(8,128)(2,1)S(1)} %collective-permute-done), channel_id=1, source_target_pairs={{0,2},{2,0},{4,6},{6,4},{8,10},{10,8},{12,14},{14,12},{1,3},{3,1},... | collective-permute-start | bytes 147464 | tf_op jit(solution)/shard_map/ppermute | solution.py:131
  12.1 4.1 %collective-permute-start.5 = (bf16[8,3072]{1,0:T(8,128)(2,1)S(1)}, bf16[8,3072]{1,0:T(8,128)(2,1)S(1)}, u32[]{:S(2)}, u32[]{:S(2)}) collective-permute-start(bf16[8,3072]{1,0:T(8,128)(2,1)S(1)} %collective-permute-done.1), channel_id=1, source_target_pairs={{0,2},{2,0},{4,6},{6,4},{8,10},{10,8},{12,14},{14,12},{1,3},{3,1},... | collective-permute-start | bytes 147464 | tf_op jit(solution)/shard_map/ppermute | solution.py:131
  16.3 1.8 %collective-permute-start.6 = (bf16[64,3072]{1,0:T(8,128)(2,1)S(1)}, bf16[64,3072]{1,0:T(8,128)(2,1)S(1)}, u32[]{:S(2)}, u32[]{:S(2)}) collective-permute-start(bf16[64,3072]{1,0:T(8,128)(2,1)S(1)} %get-tuple-element.37), channel_id=1, source_target_pairs={{0,1},{1,0},{2,3},{3,2},{4,5},{5,4},{6,7},{7,6},{8,9},{9,8},{10,11... | collective-permute-start | bytes 1179656 | tf_op jit(solution)/shard_map/ppermute | solution.py:131
  18.1 17.8 %copy-start.3 = (s32[16,2]{0,1:T(2,128)S(1)}, s32[16,2]{0,1:T(2,128)}, u32[]{:S(2)}) copy-start(s32[16,2]{0,1:T(2,128)} %param.7) | copy-start | bytes 388
  18.1 17.8 %copy-start.4 = (bf16[16,2]{0,1:T(2,128)(2,1)S(1)}, bf16[16,2]{0,1:T(2,128)(2,1)}, u32[]{:S(2)}) copy-start(bf16[16,2]{0,1:T(2,128)(2,1)} %param.8) | copy-start | bytes 196
  23.6 1.8 %collective-permute-start.7 = (bf16[64,3072]{1,0:T(8,128)(2,1)S(1)}, bf16[64,3072]{1,0:T(8,128)(2,1)S(1)}, u32[]{:S(2)}, u32[]{:S(2)}) collective-permute-start(bf16[64,3072]{1,0:T(8,128)(2,1)S(1)} %slice.25), channel_id=1, source_target_pairs={{0,1},{1,0},{2,3},{3,2},{4,5},{5,4},{6,7},{7,6},{8,9},{9,8},{10,11... | collective-permute-start | bytes 1179656 | tf_op jit(solution)/shard_map/ppermute | solution.py:131
  25.5 4.5 %collective-permute-start.10 = (bf16[8,3072]{1,0:T(8,128)(2,1)S(1)}, bf16[8,3072]{1,0:T(8,128)(2,1)S(1)}, u32[]{:S(2)}, u32[]{:S(2)}) collective-permute-start(bf16[8,3072]{1,0:T(8,128)(2,1)S(1)} %get-tuple-element.18), channel_id=1, source_target_pairs={{0,2},{2,0},{4,6},{6,4},{8,10},{10,8},{12,14},{14,12},{1,3},{3,1},... | collective-permute-start | bytes 147464 | tf_op jit(solution)/shard_map/ppermute | solution.py:131
  26.7 9.1 %collective-permute-start.8 = (bf16[16,3072]{1,0:T(8,128)(2,1)S(1)}, bf16[16,3072]{1,0:T(8,128)(2,1)S(1)}, u32[]{:S(2)}, u32[]{:S(2)}) collective-permute-start(bf16[16,3072]{1,0:T(8,128)(2,1)S(1)} %pad_maximum_fusion.2), channel_id=1, source_target_pairs={{0,2},{2,0},{4,6},{6,4},{8,10},{10,8},{12,14},{14,12},{1,3},{3,1},... | collective-permute-start | bytes 294920 | tf_op jit(solution)/shard_map/ppermute | solution.py:131
  27.6 5.2 %collective-permute-start.12 = (bf16[8,3072]{1,0:T(8,128)(2,1)S(1)}, bf16[8,3072]{1,0:T(8,128)(2,1)S(1)}, u32[]{:S(2)}, u32[]{:S(2)}) collective-permute-start(bf16[8,3072]{1,0:T(8,128)(2,1)S(1)} %get-tuple-element.20), channel_id=1, source_target_pairs={{0,2},{2,0},{4,6},{6,4},{8,10},{10,8},{12,14},{14,12},{1,3},{3,1},... | collective-permute-start | bytes 147464 | tf_op jit(solution)/shard_map/ppermute | solution.py:131
  30.1 6.0 %collective-permute-start.11 = (bf16[8,3072]{1,0:T(8,128)(2,1)S(1)}, bf16[8,3072]{1,0:T(8,128)(2,1)S(1)}, u32[]{:S(2)}, u32[]{:S(2)}) collective-permute-start(bf16[8,3072]{1,0:T(8,128)(2,1)S(1)} %add_convert_fusion.2), channel_id=1, source_target_pairs={{0,8},{2,10},{4,12},{6,14},{8,0},{10,2},{12,4},{14,6},{1,9},{3,11}... | collective-permute-start | bytes 147464 | tf_op jit(solution)/shard_map/ppermute | solution.py:128
  32.8 6.0 %collective-permute-start.13 = (bf16[8,3072]{1,0:T(8,128)(2,1)S(1)}, bf16[8,3072]{1,0:T(8,128)(2,1)S(1)}, u32[]{:S(2)}, u32[]{:S(2)}) collective-permute-start(bf16[8,3072]{1,0:T(8,128)(2,1)S(1)} %add_convert_fusion.1), channel_id=1, source_target_pairs={{0,12},{2,14},{4,8},{6,10},{8,4},{10,6},{12,0},{14,2},{1,13},{3,15... | collective-permute-start | bytes 147464 | tf_op jit(solution)/shard_map/ppermute | solution.py:128
  35.8 4.2 %collective-permute-start.9 = (bf16[8,3072]{1,0:T(8,128)(2,1)S(1)}, bf16[8,3072]{1,0:T(8,128)(2,1)S(1)}, u32[]{:S(2)}, u32[]{:S(2)}) collective-permute-start(bf16[8,3072]{1,0:T(8,128)(2,1)S(1)} %get-tuple-element.36), channel_id=1, source_target_pairs={{0,4},{2,6},{4,0},{6,2},{8,12},{10,14},{12,8},{14,10},{1,5},{3,7},... | collective-permute-start | bytes 147464 | tf_op jit(solution)/shard_map/ppermute | solution.py:128

commit v4 on v3

--- a/solution.py
+++ b/solution.py
@@ -16,15 +16,15 @@
     return expert ^ step
 
 
-def choose(experts, capacity, routes):
+def choose(steps, capacity, routes):
     me = lax.axis_index("expert") // 2
-    slots, rows = experts * capacity, routes.shape[1]
+    slots, rows = len(steps) * capacity, routes.shape[1]
     slot = lax.broadcasted_iota(jnp.int32, (slots, rows), 0)
-    step = slot // capacity
-    place = slot - step * capacity
+    block = slot // capacity
+    place = slot - block * capacity
     expert = jnp.zeros_like(slot)
-    for s in range(experts):
-        expert = jnp.where(step == s, partner(me, s), expert)
+    for at, step in enumerate(steps):
+        expert = jnp.where(block == at, partner(me, step), expert)
     first, second = routes[0:1, :] == expert, routes[1:2, :] == expert
     named = jnp.where(first | second, 1.0, 0.0)
     before = jnp.where(
@@ -37,7 +37,7 @@
     return jnp.where(ahead == place.astype(F32), named, 0.0), first
 
 
-def route_kernel(experts, capacity, routes_hbm, tokens_hbm, out_ref, routes_ref, tokens_ref, sems):
+def route_kernel(steps, capacity, routes_hbm, tokens_hbm, out_ref, routes_ref, tokens_ref, sems):
     copies = [
         pltpu.make_async_copy(routes_hbm, routes_ref, sems.at[0]),
         pltpu.make_async_copy(tokens_hbm, tokens_ref, sems.at[1]),
@@ -46,14 +46,14 @@
         copy.start()
     for copy in copies:
         copy.wait()
-    chosen, _ = choose(experts, capacity, routes_ref[...])
+    chosen, _ = choose(steps, capacity, routes_ref[...])
     out_ref[...] = jnp.dot(
         chosen.astype(BF16), tokens_ref[...], preferred_element_type=F32
     ).astype(BF16)
 
 
-def weigh_kernel(experts, capacity, routes_ref, weights_ref, comb_ref):
-    chosen, first = choose(experts, capacity, routes_ref[...])
+def weigh_kernel(steps, capacity, routes_ref, weights_ref, comb_ref):
+    chosen, first = choose(steps, capacity, routes_ref[...])
     weights = weights_ref[...].astype(F32)
     weight = jnp.where(first, weights[0:1, :], weights[1:2, :])
     comb_ref[...] = (chosen * weight).astype(BF16)
@@ -92,11 +92,13 @@
     rows, width = tokens.shape
     capacity = max(2, 2 * rows // experts)
     slots = experts * capacity
+    steps = list(range(experts - 1, 0, -1))
+    blocks = steps + [0]
     vmem = pl.BlockSpec(memory_space=pltpu.VMEM)
     hbm = pl.BlockSpec(memory_space=pltpu.HBM)
     small = pltpu.CompilerParams(vmem_limit_bytes=4 * MIB)
     outgoing = pl.pallas_call(
-        functools.partial(route_kernel, experts, capacity),
+        functools.partial(route_kernel, blocks, capacity),
         out_shape=pltpu.VMEM((slots, width), BF16),
         in_specs=[hbm, hbm],
         out_specs=vmem,
@@ -115,7 +117,7 @@
         pltpu.with_memory_space_constraint(tokens, pltpu.HBM),
     )
     comb = pl.pallas_call(
-        functools.partial(weigh_kernel, experts, capacity),
+        functools.partial(weigh_kernel, blocks, capacity),
         out_shape=jax.ShapeDtypeStruct((slots, rows), BF16),
         in_specs=[vmem, vmem],
         out_specs=vmem,
@@ -136,22 +138,21 @@
     def cut(block):
         return list(block.reshape(-1, capacity, width))
 
-    steps = list(range(experts - 1, 0, -1))
-    sent = cut(outgoing)
+    sent = dict(zip(blocks, cut(outgoing)))
     here = {s: trade(sent[s], s) for s in steps}
     here[0] = sent[0]
     there = {}
     for group in [[0, steps[0]]] + [[s] for s in steps[1:]]:
         there.update(zip(group, cut(swap(join([here[s] for s in group]), "expert"))))
-    order = [(side, s) for side in (0, 1) for s in range(experts)]
-    both = join([side[s] for side in (here, there) for s in range(experts)])
+    order = [(side, s) for side in (0, 1) for s in [0] + steps]
+    both = join([side[s] for side in (here, there) for s in [0] + steps])
     if tiles == 2:
         received = join([both, swap(both, "tile")])
     else:
         received = lax.all_gather(both, "tile", axis=0, tiled=True)
     gate, up, down = gate_proj[0], up_proj[0], down_proj[0]
     count, hidden = received.shape[0], gate.shape[1]
-    block = min(256, hidden)
+    block = min(512, hidden)
     partials = pl.pallas_call(
         functools.partial(ffn_kernel, block),
         out_shape=jax.ShapeDtypeStruct((count, width), BF16),
@@ -177,12 +178,14 @@
         both = jnp.sum(pieces.astype(F32), axis=0).astype(BF16)
     summed = dict(zip(order, lax.optimization_barrier(cut(both))))
     results = {}
-    for group in [[s] for s in steps[:-1]] + [[steps[-1], 0]]:
-        back = cut(swap(join([summed[1, s] for s in group]), "expert"))
-        for s, block in zip(group, back):
-            total = add(summed[0, s], block)
-            results[s] = trade(total, s) if s else total
-    results = join([results[s] for s in range(experts)])
+    for s in blocks:
+        leaving = summed[1, s]
+        if s == 0:
+            leaving, _ = lax.optimization_barrier((leaving, back))
+        back = swap(leaving, "expert")
+        total = add(summed[0, s], back)
+        results[s] = trade(total, s) if s else total
+    results = join([results[s] for s in blocks])
     return pl.pallas_call(
         combine_kernel,
         out_shape=jax.ShapeDtypeStruct((rows, width), BF16),

time: 41 us -> 39.6 us (0.966)
  waiting for transfers between devices: 15.2 us -> 13.5 us
  starting transfers between devices: 17.3 us -> 17.8 us
    ppermute x6, waiting for transfers between devices: 5.78 us -> 3.88 us  [trade(): return lax.ppermute(x, 'expert', pairs)]
    ppermute x8 -> x9, starting transfers between devices: 7.85 us -> 8.1 us  [swap(): lax.ppermute(x, axis, [(i, i ^ 1) for i in range(lax.axis_size(axis))])]
    ppermute x8 -> x9, waiting for transfers between devices: 9.41 us -> 9.63 us  [swap(): lax.ppermute(x, axis, [(i, i ^ 1) for i in range(lax.axis_size(axis))])]
  transfers between devices with their start and end apart: 14 -> 15, of which waited for: 11 -> 11; matrix products, arithmetic and copies ran while one was open for 0% -> 0% of each run, Pallas kernels for 0% -> 0%
where the time goes in v4:
time: 39.6 us; the launch traced here: 39.5 us
  starting transfers between devices  17.8 us (45%)
  waiting for transfers between devices  13.5 us (34%)
  Pallas kernels  7.68 us (19%)
    ppermute x6, starting transfers between devices, trade(): return lax.ppermute(x, 'expert', pairs)  9.69 us
    ppermute x9, waiting for transfers between devices, swap(): lax.ppermute(x, axis, [(i, i ^ 1) for i in range(lax.axis_size(axis))])  9.63 us
    ppermute x9, starting transfers between devices, swap(): lax.ppermute(x, axis, [(i, i ^ 1) for i in range(lax.axis_size(axis))])  8.1 us
    pallas_call x1, Pallas kernels, shards(): pl.pallas_call(functools.partial(ffn_kernel, block), out_shape=jax.ShapeD...  5.32 us
    ppermute x6, waiting for transfers between devices, trade(): return lax.ppermute(x, 'expert', pairs)  3.88 us
    pallas_call x1, Pallas kernels, shards(): pl.pallas_call(functools.partial(route_kernel, blocks, capacity), out_sha...  1.38 us
    pallas_call x1, Pallas kernels, shards(): pl.pallas_call(combine_kernel, out_shape=jax.ShapeDtypeStruct((rows, widt...  0.84 us
  transfers between devices with their start and end apart: 15, of which 11 were waited for; matrix products, arithmetic and copies ran while one was open for 0% of the time, Pallas kernels for 0%

profile of v4, /device:TPU:0, one launch (start us, length us, event | category | flops | bytes accessed | tf_op | source)
XLA Modules:
  0.0 39.5 jit_solution(12108421896479126968)
XLA Ops:
  0.0 1.4 %route.1 = bf16[32,3072]{1,0:T(8,128)(2,1)S(1)} custom-call(s32[2,16]{1,0:T(2,128)} %bitcast.8, bf16[16,3072]{1,0:T(8,128)(2,1)} %tokens_hbm.1), custom_call_target="tpu_custom_call" | custom-call | flops 999999995904 | bytes 400000000 | tf_op jit(solution)/shard_map/route/pallas_call | solution.py:100
  1.4 5.1 %collective-permute-start = (bf16[8,3072]{1,0:T(8,128)(2,1)S(1)}, bf16[8,3072]{1,0:T(8,128)(2,1)S(1)}, u32[]{:S(2)}, u32[]{:S(2)}) collective-permute-start(bf16[8,3072]{1,0:T(8,128)(2,1)S(1)} %get-tuple-element.35), channel_id=1, source_target_pairs={{0,12},{2,14},{4,8},{6,10},{8,4},{10,6},{12,0},{14,2},{1,13},{3,15... | collective-permute-start | bytes 147464 | tf_op jit(solution)/shard_map/ppermute | solution.py:130
  6.6 0.6 %collective-permute-start.2 = (bf16[8,3072]{1,0:T(8,128)(2,1)S(1)}, bf16[8,3072]{1,0:T(8,128)(2,1)S(1)}, u32[]{:S(2)}, u32[]{:S(2)}) collective-permute-start(bf16[8,3072]{1,0:T(8,128)(2,1)S(1)} %get-tuple-element.33), channel_id=1, source_target_pairs={{0,4},{2,6},{4,0},{6,2},{8,12},{10,14},{12,8},{14,10},{1,5},{3,7},... | collective-permute-start | bytes 147464 | tf_op jit(solution)/shard_map/ppermute | solution.py:130
  7.2 1.6 %collective-permute-done = bf16[8,3072]{1,0:T(8,128)(2,1)S(1)} collective-permute-done((bf16[8,3072]{1,0:T(8,128)(2,1)S(1)}, bf16[8,3072]{1,0:T(8,128)(2,1)S(1)}, u32[]{:S(2)}, u32[]{:S(2)}) %collective-permute-start) | collective-permute-done | bytes 49184 | tf_op jit(solution)/shard_map/ppermute | solution.py:130
  8.8 1.9 %collective-permute-start.3 = (bf16[16,3072]{1,0:T(8,128)(2,1)S(1)}, bf16[16,3072]{1,0:T(8,128)(2,1)S(1)}, u32[]{:S(2)}, u32[]{:S(2)}) collective-permute-start(bf16[16,3072]{1,0:T(8,128)(2,1)S(1)} %pad_maximum_fusion.1), channel_id=1, source_target_pairs={{0,2},{2,0},{4,6},{6,4},{8,10},{10,8},{12,14},{14,12},{1,3},{3,1},... | collective-permute-start | bytes 294920 | tf_op jit(solution)/shard_map/ppermute | solution.py:133
  10.6 0.9 %collective-permute-done.1 = bf16[8,3072]{1,0:T(8,128)(2,1)S(1)} collective-permute-done((bf16[8,3072]{1,0:T(8,128)(2,1)S(1)}, bf16[8,3072]{1,0:T(8,128)(2,1)S(1)}, u32[]{:S(2)}, u32[]{:S(2)}) %collective-permute-start.1) | collective-permute-done | bytes 49184 | tf_op jit(solution)/shard_map/ppermute | solution.py:130
  11.5 1.5 %collective-permute-start.4 = (bf16[8,3072]{1,0:T(8,128)(2,1)S(1)}, bf16[8,3072]{1,0:T(8,128)(2,1)S(1)}, u32[]{:S(2)}, u32[]{:S(2)}) collective-permute-start(bf16[8,3072]{1,0:T(8,128)(2,1)S(1)} %collective-permute-done.1), channel_id=1, source_target_pairs={{0,2},{2,0},{4,6},{6,4},{8,10},{10,8},{12,14},{14,12},{1,3},{3,1},... | collective-permute-start | bytes 147464 | tf_op jit(solution)/shard_map/ppermute | solution.py:133
  13.0 0.5 %collective-permute-start.5 = (bf16[8,3072]{1,0:T(8,128)(2,1)S(1)}, bf16[8,3072]{1,0:T(8,128)(2,1)S(1)}, u32[]{:S(2)}, u32[]{:S(2)}) collective-permute-start(bf16[8,3072]{1,0:T(8,128)(2,1)S(1)} %collective-permute-done.2), channel_id=1, source_target_pairs={{0,2},{2,0},{4,6},{6,4},{8,10},{10,8},{12,14},{14,12},{1,3},{3,1},... | collective-permute-start | bytes 147464 | tf_op jit(solution)/shard_map/ppermute | solution.py:133
  13.9 1.7 %collective-permute-done.4 = bf16[8,3072]{1,0:T(8,128)(2,1)S(1)} collective-permute-done((bf16[8,3072]{1,0:T(8,128)(2,1)S(1)}, bf16[8,3072]{1,0:T(8,128)(2,1)S(1)}, u32[]{:S(2)}, u32[]{:S(2)}) %collective-permute-start.4) | collective-permute-done | bytes 49184 | tf_op jit(solution)/shard_map/ppermute | solution.py:133
  15.6 1.5 %collective-permute-done.5 = bf16[8,3072]{1,0:T(8,128)(2,1)S(1)} collective-permute-done((bf16[8,3072]{1,0:T(8,128)(2,1)S(1)}, bf16[8,3072]{1,0:T(8,128)(2,1)S(1)}, u32[]{:S(2)}, u32[]{:S(2)}) %collective-permute-start.5) | collective-permute-done | bytes 49184 | tf_op jit(solution)/shard_map/ppermute | solution.py:133
  17.2 1.7 %collective-permute-done.6 = bf16[64,3072]{1,0:T(8,128)(2,1)S(1)} collective-permute-done((bf16[64,3072]{1,0:T(8,128)(2,1)S(1)}, bf16[64,3072]{1,0:T(8,128)(2,1)S(1)}, u32[]{:S(2)}, u32[]{:S(2)}) %collective-permute-start.6) | collective-permute-done | bytes 393248 | tf_op jit(solution)/shard_map/ppermute | solution.py:133
  19.0 5.3 %ffn.1 = bf16[128,3072]{1,0:T(8,128)(2,1)S(1)} custom-call(bf16[128,3072]{1,0:T(8,128)(2,1)S(1)} %constant_dynamic-update-slice_fusion.7.rows_ref, bf16[3072,2048]{1,0:T(8,128)(2,1)S(1)} %bitcast.5, bf16[3072,2048]{1,0:T(8,128)(2,1)S(1)} %bitcast.6, bf16[2048,3072]{1,0:T(8,128)(2,1)S(1)} %bitcast.7), custom_call_target="tpu_custom_call" | custom-call | flops 4831838208 | bytes 37748736 | tf_op jit(solution)/shard_map/ffn/pallas_call | solution.py:156
  24.6 1.6 %collective-permute-done.7 = bf16[64,3072]{1,0:T(8,128)(2,1)S(1)} collective-permute-done((bf16[64,3072]{1,0:T(8,128)(2,1)S(1)}, bf16[64,3072]{1,0:T(8,128)(2,1)S(1)}, u32[]{:S(2)}, u32[]{:S(2)}) %collective-permute-start.7) | collective-permute-done | bytes 393248 | tf_op jit(solution)/shard_map/ppermute | solution.py:133
  26.3 0.6 %collective-permute-start.8 = (bf16[8,3072]{1,0:T(8,128)(2,1)S(1)}, bf16[8,3072]{1,0:T(8,128)(2,1)S(1)}, u32[]{:S(2)}, u32[]{:S(2)}) collective-permute-start(bf16[8,3072]{1,0:T(8,128)(2,1)S(1)} %get-tuple-element.15), channel_id=1, source_target_pairs={{0,2},{2,0},{4,6},{6,4},{8,10},{10,8},{12,14},{14,12},{1,3},{3,1},... | collective-permute-start | bytes 147464 | tf_op jit(solution)/shard_map/ppermute | solution.py:133
  27.0 1.5 %collective-permute-start.10 = (bf16[8,3072]{1,0:T(8,128)(2,1)S(1)}, bf16[8,3072]{1,0:T(8,128)(2,1)S(1)}, u32[]{:S(2)}, u32[]{:S(2)}) collective-permute-start(bf16[8,3072]{1,0:T(8,128)(2,1)S(1)} %get-tuple-element.17), channel_id=1, source_target_pairs={{0,2},{2,0},{4,6},{6,4},{8,10},{10,8},{12,14},{14,12},{1,3},{3,1},... | collective-permute-start | bytes 147464 | tf_op jit(solution)/shard_map/ppermute | solution.py:133
  28.5 0.5 %collective-permute-start.12 = (bf16[8,3072]{1,0:T(8,128)(2,1)S(1)}, bf16[8,3072]{1,0:T(8,128)(2,1)S(1)}, u32[]{:S(2)}, u32[]{:S(2)}) collective-permute-start(bf16[8,3072]{1,0:T(8,128)(2,1)S(1)} %get-tuple-element.19), channel_id=1, source_target_pairs={{0,2},{2,0},{4,6},{6,4},{8,10},{10,8},{12,14},{14,12},{1,3},{3,1},... | collective-permute-start | bytes 147464 | tf_op jit(solution)/shard_map/ppermute | solution.py:133
  29.1 1.6 %collective-permute-done.8 = bf16[8,3072]{1,0:T(8,128)(2,1)S(1)} collective-permute-done((bf16[8,3072]{1,0:T(8,128)(2,1)S(1)}, bf16[8,3072]{1,0:T(8,128)(2,1)S(1)}, u32[]{:S(2)}, u32[]{:S(2)}) %collective-permute-start.8) | collective-permute-done | bytes 49184 | tf_op jit(solution)/shard_map/ppermute | solution.py:133
  30.7 2.1 %collective-permute-start.9 = (bf16[8,3072]{1,0:T(8,128)(2,1)S(1)}, bf16[8,3072]{1,0:T(8,128)(2,1)S(1)}, u32[]{:S(2)}, u32[]{:S(2)}) collective-permute-start(bf16[8,3072]{1,0:T(8,128)(2,1)S(1)} %add_convert_fusion.4), channel_id=1, source_target_pairs={{0,12},{2,14},{4,8},{6,10},{8,4},{10,6},{12,0},{14,2},{1,13},{3,15... | collective-permute-start | bytes 147464 | tf_op jit(solution)/shard_map/ppermute | solution.py:130
  33.1 1.3 %collective-permute-start.14 = (bf16[8,3072]{1,0:T(8,128)(2,1)S(1)}, bf16[8,3072]{1,0:T(8,128)(2,1)S(1)}, u32[]{:S(2)}, u32[]{:S(2)}) collective-permute-start(bf16[8,3072]{1,0:T(8,128)(2,1)S(1)} %get-tuple-element.22), channel_id=1, source_target_pairs={{0,2},{2,0},{4,6},{6,4},{8,10},{10,8},{12,14},{14,12},{1,3},{3,1},... | collective-permute-start | bytes 147464 | tf_op jit(solution)/shard_map/ppermute | solution.py:133
  34.5 1.5 %collective-permute-start.13 = (bf16[8,3072]{1,0:T(8,128)(2,1)S(1)}, bf16[8,3072]{1,0:T(8,128)(2,1)S(1)}, u32[]{:S(2)}, u32[]{:S(2)}) collective-permute-start(bf16[8,3072]{1,0:T(8,128)(2,1)S(1)} %add_convert_fusion.2), channel_id=1, source_target_pairs={{0,4},{2,6},{4,0},{6,2},{8,12},{10,14},{12,8},{14,10},{1,5},{3,7},... | collective-permute-start | bytes 147464 | tf_op jit(solution)/shard_map/ppermute | solution.py:130
  36.0 1.2 %collective-permute-done.14 = bf16[8,3072]{1,0:T(8,128)(2,1)S(1)} collective-permute-done((bf16[8,3072]{1,0:T(8,128)(2,1)S(1)}, bf16[8,3072]{1,0:T(8,128)(2,1)S(1)}, u32[]{:S(2)}, u32[]{:S(2)}) %collective-permute-start.14) | collective-permute-done | bytes 49184 | tf_op jit(solution)/shard_map/ppermute | solution.py:133
  37.3 0.6 %collective-permute-done.11 = bf16[8,3072]{1,0:T(8,128)(2,1)S(1)} collective-permute-done((bf16[8,3072]{1,0:T(8,128)(2,1)S(1)}, bf16[8,3072]{1,0:T(8,128)(2,1)S(1)}, u32[]{:S(2)}, u32[]{:S(2)}) %collective-permute-start.11) | collective-permute-done | bytes 49184 | tf_op jit(solution)/shard_map/ppermute | solution.py:130
  37.9 0.8 %collective-permute-done.13 = bf16[8,3072]{1,0:T(8,128)(2,1)S(1)} collective-permute-done((bf16[8,3072]{1,0:T(8,128)(2,1)S(1)}, bf16[8,3072]{1,0:T(8,128)(2,1)S(1)}, u32[]{:S(2)}, u32[]{:S(2)}) %collective-permute-start.13) | collective-permute-done | bytes 49184 | tf_op jit(solution)/shard_map/ppermute | solution.py:130
  38.7 0.8 %combine.1 = bf16[16,3072]{1,0:T(8,128)(2,1)} custom-call(bf16[32,16]{1,0:T(8,128)(2,1)S(1)} %weigh.1.comb_ref, bf16[32,3072]{1,0:T(8,128)(2,1)S(1)} %pad_maximum_fusion.results_ref), custom_call_target="tpu_custom_call" | custom-call | tf_op jit(solution)/shard_map/combine/pallas_call | solution.py:189
  (37 shorter events, 1.4 us)
Async XLA Ops:
  0.0 19.0 %copy-start = (bf16[1,3072,2048]{2,1,0:T(8,128)(2,1)S(1)}, bf16[1,3072,2048]{2,1,0:T(8,128)(2,1)}, u32[]{:S(2)}) copy-start(bf16[1,3072,2048]{2,1,0:T(8,128)(2,1)} %param.9) | copy-start | bytes 37748740
  0.0 19.0 %copy-start.1 = (bf16[1,3072,2048]{2,1,0:T(8,128)(2,1)S(1)}, bf16[1,3072,2048]{2,1,0:T(8,128)(2,1)}, u32[]{:S(2)}) copy-start(bf16[1,3072,2048]{2,1,0:T(8,128)(2,1)} %param.10) | copy-start | bytes 37748740
  0.0 19.0 %copy-start.2 = (bf16[1,2048,3072]{2,1,0:T(8,128)(2,1)S(1)}, bf16[1,2048,3072]{2,1,0:T(8,128)(2,1)}, u32[]{:S(2)}) copy-start(bf16[1,2048,3072]{2,1,0:T(8,128)(2,1)} %param.11) | copy-start | bytes 37748740
  1.4 7.4 %collective-permute-start = (bf16[8,3072]{1,0:T(8,128)(2,1)S(1)}, bf16[8,3072]{1,0:T(8,128)(2,1)S(1)}, u32[]{:S(2)}, u32[]{:S(2)}) collective-permute-start(bf16[8,3072]{1,0:T(8,128)(2,1)S(1)} %get-tuple-element.35), channel_id=1, source_target_pairs={{0,12},{2,14},{4,8},{6,10},{8,4},{10,6},{12,0},{14,2},{1,13},{3,15... | collective-permute-start | bytes 147464 | tf_op jit(solution)/shard_map/ppermute | solution.py:130
  6.5 5.0 %collective-permute-start.1 = (bf16[8,3072]{1,0:T(8,128)(2,1)S(1)}, bf16[8,3072]{1,0:T(8,128)(2,1)S(1)}, u32[]{:S(2)}, u32[]{:S(2)}) collective-permute-start(bf16[8,3072]{1,0:T(8,128)(2,1)S(1)} %get-tuple-element.34), channel_id=1, source_target_pairs={{0,8},{2,10},{4,12},{6,14},{8,0},{10,2},{12,4},{14,6},{1,9},{3,11}... | collective-permute-start | bytes 147464 | tf_op jit(solution)/shard_map/ppermute | solution.py:130
  6.6 6.5 %collective-permute-start.2 = (bf16[8,3072]{1,0:T(8,128)(2,1)S(1)}, bf16[8,3072]{1,0:T(8,128)(2,1)S(1)}, u32[]{:S(2)}, u32[]{:S(2)}) collective-permute-start(bf16[8,3072]{1,0:T(8,128)(2,1)S(1)} %get-tuple-element.33), channel_id=1, source_target_pairs={{0,4},{2,6},{4,0},{6,2},{8,12},{10,14},{12,8},{14,10},{1,5},{3,7},... | collective-permute-start | bytes 147464 | tf_op jit(solution)/shard_map/ppermute | solution.py:130
  8.8 5.1 %collective-permute-start.3 = (bf16[16,3072]{1,0:T(8,128)(2,1)S(1)}, bf16[16,3072]{1,0:T(8,128)(2,1)S(1)}, u32[]{:S(2)}, u32[]{:S(2)}) collective-permute-start(bf16[16,3072]{1,0:T(8,128)(2,1)S(1)} %pad_maximum_fusion.1), channel_id=1, source_target_pairs={{0,2},{2,0},{4,6},{6,4},{8,10},{10,8},{12,14},{14,12},{1,3},{3,1},... | collective-permute-start | bytes 294920 | tf_op jit(solution)/shard_map/ppermute | solution.py:133
  11.5 4.1 %collective-permute-start.4 = (bf16[8,3072]{1,0:T(8,128)(2,1)S(1)}, bf16[8,3072]{1,0:T(8,128)(2,1)S(1)}, u32[]{:S(2)}, u32[]{:S(2)}) collective-permute-start(bf16[8,3072]{1,0:T(8,128)(2,1)S(1)} %collective-permute-done.1), channel_id=1, source_target_pairs={{0,2},{2,0},{4,6},{6,4},{8,10},{10,8},{12,14},{14,12},{1,3},{3,1},... | collective-permute-start | bytes 147464 | tf_op jit(solution)/shard_map/ppermute | solution.py:133
  13.0 4.1 %collective-permute-start.5 = (bf16[8,3072]{1,0:T(8,128)(2,1)S(1)}, bf16[8,3072]{1,0:T(8,128)(2,1)S(1)}, u32[]{:S(2)}, u32[]{:S(2)}) collective-permute-start(bf16[8,3072]{1,0:T(8,128)(2,1)S(1)} %collective-permute-done.2), channel_id=1, source_target_pairs={{0,2},{2,0},{4,6},{6,4},{8,10},{10,8},{12,14},{14,12},{1,3},{3,1},... | collective-permute-start | bytes 147464 | tf_op jit(solution)/shard_map/ppermute | solution.py:133
  17.1 1.8 %collective-permute-start.6 = (bf16[64,3072]{1,0:T(8,128)(2,1)S(1)}, bf16[64,3072]{1,0:T(8,128)(2,1)S(1)}, u32[]{:S(2)}, u32[]{:S(2)}) collective-permute-start(bf16[64,3072]{1,0:T(8,128)(2,1)S(1)} %get-tuple-element.39), channel_id=1, source_target_pairs={{0,1},{1,0},{2,3},{3,2},{4,5},{5,4},{6,7},{7,6},{8,9},{9,8},{10,11... | collective-permute-start | bytes 1179656 | tf_op jit(solution)/shard_map/ppermute | solution.py:133
  19.0 7.9 %copy-start.3 = (s32[16,2]{0,1:T(2,128)S(1)}, s32[16,2]{0,1:T(2,128)}, u32[]{:S(2)}) copy-start(s32[16,2]{0,1:T(2,128)} %param.7) | copy-start | bytes 388
  19.0 7.9 %copy-start.4 = (bf16[16,2]{0,1:T(2,128)(2,1)S(1)}, bf16[16,2]{0,1:T(2,128)(2,1)}, u32[]{:S(2)}) copy-start(bf16[16,2]{0,1:T(2,128)(2,1)} %param.8) | copy-start | bytes 196
  24.4 1.8 %collective-permute-start.7 = (bf16[64,3072]{1,0:T(8,128)(2,1)S(1)}, bf16[64,3072]{1,0:T(8,128)(2,1)S(1)}, u32[]{:S(2)}, u32[]{:S(2)}) collective-permute-start(bf16[64,3072]{1,0:T(8,128)(2,1)S(1)} %slice.25), channel_id=1, source_target_pairs={{0,1},{1,0},{2,3},{3,2},{4,5},{5,4},{6,7},{7,6},{8,9},{9,8},{10,11... | collective-permute-start | bytes 1179656 | tf_op jit(solution)/shard_map/ppermute | solution.py:133
  26.3 4.4 %collective-permute-start.8 = (bf16[8,3072]{1,0:T(8,128)(2,1)S(1)}, bf16[8,3072]{1,0:T(8,128)(2,1)S(1)}, u32[]{:S(2)}, u32[]{:S(2)}) collective-permute-start(bf16[8,3072]{1,0:T(8,128)(2,1)S(1)} %get-tuple-element.15), channel_id=1, source_target_pairs={{0,2},{2,0},{4,6},{6,4},{8,10},{10,8},{12,14},{14,12},{1,3},{3,1},... | collective-permute-start | bytes 147464 | tf_op jit(solution)/shard_map/ppermute | solution.py:133
  27.0 5.8 %collective-permute-start.10 = (bf16[8,3072]{1,0:T(8,128)(2,1)S(1)}, bf16[8,3072]{1,0:T(8,128)(2,1)S(1)}, u32[]{:S(2)}, u32[]{:S(2)}) collective-permute-start(bf16[8,3072]{1,0:T(8,128)(2,1)S(1)} %get-tuple-element.17), channel_id=1, source_target_pairs={{0,2},{2,0},{4,6},{6,4},{8,10},{10,8},{12,14},{14,12},{1,3},{3,1},... | collective-permute-start | bytes 147464 | tf_op jit(solution)/shard_map/ppermute | solution.py:133
  28.5 4.6 %collective-permute-start.12 = (bf16[8,3072]{1,0:T(8,128)(2,1)S(1)}, bf16[8,3072]{1,0:T(8,128)(2,1)S(1)}, u32[]{:S(2)}, u32[]{:S(2)}) collective-permute-start(bf16[8,3072]{1,0:T(8,128)(2,1)S(1)} %get-tuple-element.19), channel_id=1, source_target_pairs={{0,2},{2,0},{4,6},{6,4},{8,10},{10,8},{12,14},{14,12},{1,3},{3,1},... | collective-permute-start | bytes 147464 | tf_op jit(solution)/shard_map/ppermute | solution.py:133
  30.7 6.6 %collective-permute-start.9 = (bf16[8,3072]{1,0:T(8,128)(2,1)S(1)}, bf16[8,3072]{1,0:T(8,128)(2,1)S(1)}, u32[]{:S(2)}, u32[]{:S(2)}) collective-permute-start(bf16[8,3072]{1,0:T(8,128)(2,1)S(1)} %add_convert_fusion.4), channel_id=1, source_target_pairs={{0,12},{2,14},{4,8},{6,10},{8,4},{10,6},{12,0},{14,2},{1,13},{3,15... | collective-permute-start | bytes 147464 | tf_op jit(solution)/shard_map/ppermute | solution.py:130
  32.8 5.1 %collective-permute-start.11 = (bf16[8,3072]{1,0:T(8,128)(2,1)S(1)}, bf16[8,3072]{1,0:T(8,128)(2,1)S(1)}, u32[]{:S(2)}, u32[]{:S(2)}) collective-permute-start(bf16[8,3072]{1,0:T(8,128)(2,1)S(1)} %add_convert_fusion.3), channel_id=1, source_target_pairs={{0,8},{2,10},{4,12},{6,14},{8,0},{10,2},{12,4},{14,6},{1,9},{3,11}... | collective-permute-start | bytes 147464 | tf_op jit(solution)/shard_map/ppermute | solution.py:130
  33.1 4.1 %collective-permute-start.14 = (bf16[8,3072]{1,0:T(8,128)(2,1)S(1)}, bf16[8,3072]{1,0:T(8,128)(2,1)S(1)}, u32[]{:S(2)}, u32[]{:S(2)}) collective-permute-start(bf16[8,3072]{1,0:T(8,128)(2,1)S(1)} %get-tuple-element.22), channel_id=1, source_target_pairs={{0,2},{2,0},{4,6},{6,4},{8,10},{10,8},{12,14},{14,12},{1,3},{3,1},... | collective-permute-start | bytes 147464 | tf_op jit(solution)/shard_map/ppermute | solution.py:133
  34.5 4.2 %collective-permute-start.13 = (bf16[8,3072]{1,0:T(8,128)(2,1)S(1)}, bf16[8,3072]{1,0:T(8,128)(2,1)S(1)}, u32[]{:S(2)}, u32[]{:S(2)}) collective-permute-start(bf16[8,3072]{1,0:T(8,128)(2,1)S(1)} %add_convert_fusion.2), channel_id=1, source_target_pairs={{0,4},{2,6},{4,0},{6,2},{8,12},{10,14},{12,8},{14,10},{1,5},{3,7},... | collective-permute-start | bytes 147464 | tf_op jit(solution)/shard_map/ppermute | solution.py:130

commit v5 on v4

--- a/solution.py
+++ b/solution.py
@@ -142,12 +142,14 @@
     here = {s: trade(sent[s], s) for s in steps}
     here[0] = sent[0]
     there = {}
-    for group in [[0, steps[0]]] + [[s] for s in steps[1:]]:
+    for group in [[0]] + [[s] for s in steps]:
         there.update(zip(group, cut(swap(join([here[s] for s in group]), "expert"))))
     order = [(side, s) for side in (0, 1) for s in [0] + steps]
-    both = join([side[s] for side in (here, there) for s in [0] + steps])
+    names = [(side, s) for side in (here, there) for s in [0] + steps]
+    pieces = [join([side[s] for side, s in names[:-2]]), join([side[s] for side, s in names[-2:]])]
+    both = join(pieces)
     if tiles == 2:
-        received = join([both, swap(both, "tile")])
+        received = join(pieces + [swap(piece, "tile") for piece in pieces])
     else:
         received = lax.all_gather(both, "tile", axis=0, tiled=True)
     gate, up, down = gate_proj[0], up_proj[0], down_proj[0]
@@ -170,13 +172,18 @@
         name="ffn",
     )(received, gate, up, down)
     if tiles == 2:
-        both = add(partials[: 2 * slots], swap(partials[2 * slots :], "tile"))
+        kept, left = [dict(zip(order, cut(rows))) for rows in jnp.split(partials, 2)]
+        summed = {}
+        for group in (steps[:-1], [steps[-1], 0]):
+            moved = [key for key in order if key[1] in group]
+            both = add(join([kept[key] for key in moved]), swap(join([left[key] for key in moved]), "tile"))
+            summed.update(zip(moved, lax.optimization_barrier(cut(both))))
     else:
         pieces = lax.all_to_all(
             partials.reshape(tiles, 2 * slots, width), "tile", 0, 0, tiled=True
         )
         both = jnp.sum(pieces.astype(F32), axis=0).astype(BF16)
-    summed = dict(zip(order, lax.optimization_barrier(cut(both))))
+        summed = dict(zip(order, lax.optimization_barrier(cut(both))))
     results = {}
     for s in blocks:
         leaving = summed[1, s]

time: 39.6 us -> 38.9 us (0.982)
  waiting for transfers between devices: 13.5 us -> 10.7 us
  starting transfers between devices: 17.8 us -> 19.7 us
    ppermute x9 -> x12, starting transfers between devices: 8.1 us -> 10.1 us  [swap(): lax.ppermute(x, axis, [(i, i ^ 1) for i in range(lax.axis_size(axis))])]
    ppermute x6, waiting for transfers between devices: 3.88 us -> 2.36 us  [trade(): return lax.ppermute(x, 'expert', pairs)]
    ppermute x9 -> x12, waiting for transfers between devices: 9.63 us -> 8.32 us  [swap(): lax.ppermute(x, axis, [(i, i ^ 1) for i in range(lax.axis_size(axis))])]
  transfers between devices with their start and end apart: 15 -> 18, of which waited for: 11 -> 9; matrix products, arithmetic and copies ran while one was open for 0% -> 1% of each run, Pallas kernels for 0% -> 0%
where the time goes in v5:
time: 38.9 us; the launch traced here: 38.7 us
  starting transfers between devices  19.7 us (51%)
  waiting for transfers between devices  10.7 us (28%)
  Pallas kernels  7.69 us (20%)
    ppermute x12, starting transfers between devices, swap(): lax.ppermute(x, axis, [(i, i ^ 1) for i in range(lax.axis_size(axis))])  10.1 us
    ppermute x6, starting transfers between devices, trade(): return lax.ppermute(x, 'expert', pairs)  9.61 us
    ppermute x12, waiting for transfers between devices, swap(): lax.ppermute(x, axis, [(i, i ^ 1) for i in range(lax.axis_size(axis))])  8.32 us
    pallas_call x1, Pallas kernels, shards(): pl.pallas_call(functools.partial(ffn_kernel, block), out_shape=jax.ShapeD...  5.32 us
    ppermute x6, waiting for transfers between devices, trade(): return lax.ppermute(x, 'expert', pairs)  2.36 us
    pallas_call x1, Pallas kernels, shards(): pl.pallas_call(functools.partial(route_kernel, blocks, capacity), out_sha...  1.38 us
    pallas_call x1, Pallas kernels, shards(): pl.pallas_call(combine_kernel, out_shape=jax.ShapeDtypeStruct((rows, widt...  0.84 us
  transfers between devices with their start and end apart: 18, of which 9 were waited for; matrix products, arithmetic and copies ran while one was open for 1% of the time, Pallas kernels for 0%

profile of v5, /device:TPU:0, one launch (start us, length us, event | category | flops | bytes accessed | tf_op | source)
XLA Modules:
  0.0 38.7 jit_solution(12390152215406052728)
XLA Ops:
  0.0 1.4 %route.1 = bf16[32,3072]{1,0:T(8,128)(2,1)S(1)} custom-call(s32[2,16]{1,0:T(2,128)} %bitcast.8, bf16[16,3072]{1,0:T(8,128)(2,1)} %tokens_hbm.1), custom_call_target="tpu_custom_call" | custom-call | flops 999999995904 | bytes 400000000 | tf_op jit(solution)/shard_map/route/pallas_call | solution.py:100
  1.4 5.1 %collective-permute-start = (bf16[8,3072]{1,0:T(8,128)(2,1)S(1)}, bf16[8,3072]{1,0:T(8,128)(2,1)S(1)}, u32[]{:S(2)}, u32[]{:S(2)}) collective-permute-start(bf16[8,3072]{1,0:T(8,128)(2,1)S(1)} %get-tuple-element.45), channel_id=1, source_target_pairs={{0,12},{2,14},{4,8},{6,10},{8,4},{10,6},{12,0},{14,2},{1,13},{3,15... | collective-permute-start | bytes 147464 | tf_op jit(solution)/shard_map/ppermute | solution.py:130
  6.6 0.6 %collective-permute-start.2 = (bf16[8,3072]{1,0:T(8,128)(2,1)S(1)}, bf16[8,3072]{1,0:T(8,128)(2,1)S(1)}, u32[]{:S(2)}, u32[]{:S(2)}) collective-permute-start(bf16[8,3072]{1,0:T(8,128)(2,1)S(1)} %get-tuple-element.43), channel_id=1, source_target_pairs={{0,4},{2,6},{4,0},{6,2},{8,12},{10,14},{12,8},{14,10},{1,5},{3,7},... | collective-permute-start | bytes 147464 | tf_op jit(solution)/shard_map/ppermute | solution.py:130
  7.2 1.6 %collective-permute-start.3 = (bf16[8,3072]{1,0:T(8,128)(2,1)S(1)}, bf16[8,3072]{1,0:T(8,128)(2,1)S(1)}, u32[]{:S(2)}, u32[]{:S(2)}) collective-permute-start(bf16[8,3072]{1,0:T(8,128)(2,1)S(1)} %get-tuple-element.46), channel_id=1, source_target_pairs={{0,2},{2,0},{4,6},{6,4},{8,10},{10,8},{12,14},{14,12},{1,3},{3,1},... | collective-permute-start | bytes 147464 | tf_op jit(solution)/shard_map/ppermute | solution.py:133
  9.0 1.6 %collective-permute-start.4 = (bf16[8,3072]{1,0:T(8,128)(2,1)S(1)}, bf16[8,3072]{1,0:T(8,128)(2,1)S(1)}, u32[]{:S(2)}, u32[]{:S(2)}) collective-permute-start(bf16[8,3072]{1,0:T(8,128)(2,1)S(1)} %collective-permute-done), channel_id=1, source_target_pairs={{0,2},{2,0},{4,6},{6,4},{8,10},{10,8},{12,14},{14,12},{1,3},{3,1},... | collective-permute-start | bytes 147464 | tf_op jit(solution)/shard_map/ppermute | solution.py:133
  10.6 1.0 %collective-permute-done.1 = bf16[8,3072]{1,0:T(8,128)(2,1)S(1)} collective-permute-done((bf16[8,3072]{1,0:T(8,128)(2,1)S(1)}, bf16[8,3072]{1,0:T(8,128)(2,1)S(1)}, u32[]{:S(2)}, u32[]{:S(2)}) %collective-permute-start.1) | collective-permute-done | bytes 49184 | tf_op jit(solution)/shard_map/ppermute | solution.py:130
  11.6 1.5 %collective-permute-start.5 = (bf16[8,3072]{1,0:T(8,128)(2,1)S(1)}, bf16[8,3072]{1,0:T(8,128)(2,1)S(1)}, u32[]{:S(2)}, u32[]{:S(2)}) collective-permute-start(bf16[8,3072]{1,0:T(8,128)(2,1)S(1)} %collective-permute-done.1), channel_id=1, source_target_pairs={{0,2},{2,0},{4,6},{6,4},{8,10},{10,8},{12,14},{14,12},{1,3},{3,1},... | collective-permute-start | bytes 147464 | tf_op jit(solution)/shard_map/ppermute | solution.py:133
  13.1 0.5 %collective-permute-start.6 = (bf16[8,3072]{1,0:T(8,128)(2,1)S(1)}, bf16[8,3072]{1,0:T(8,128)(2,1)S(1)}, u32[]{:S(2)}, u32[]{:S(2)}) collective-permute-start(bf16[8,3072]{1,0:T(8,128)(2,1)S(1)} %collective-permute-done.2), channel_id=1, source_target_pairs={{0,2},{2,0},{4,6},{6,4},{8,10},{10,8},{12,14},{14,12},{1,3},{3,1},... | collective-permute-start | bytes 147464 | tf_op jit(solution)/shard_map/ppermute | solution.py:133
  13.8 1.9 %collective-permute-done.5 = bf16[8,3072]{1,0:T(8,128)(2,1)S(1)} collective-permute-done((bf16[8,3072]{1,0:T(8,128)(2,1)S(1)}, bf16[8,3072]{1,0:T(8,128)(2,1)S(1)}, u32[]{:S(2)}, u32[]{:S(2)}) %collective-permute-start.5) | collective-permute-done | bytes 49184 | tf_op jit(solution)/shard_map/ppermute | solution.py:133
  15.6 1.5 %collective-permute-done.6 = bf16[8,3072]{1,0:T(8,128)(2,1)S(1)} collective-permute-done((bf16[8,3072]{1,0:T(8,128)(2,1)S(1)}, bf16[8,3072]{1,0:T(8,128)(2,1)S(1)}, u32[]{:S(2)}, u32[]{:S(2)}) %collective-permute-start.6) | collective-permute-done | bytes 49184 | tf_op jit(solution)/shard_map/ppermute | solution.py:133
  17.3 1.2 %collective-permute-done.8 = bf16[16,3072]{1,0:T(8,128)(2,1)S(1)} collective-permute-done((bf16[16,3072]{1,0:T(8,128)(2,1)S(1)}, bf16[16,3072]{1,0:T(8,128)(2,1)S(1)}, u32[]{:S(2)}, u32[]{:S(2)}) %collective-permute-start.8) | collective-permute-done | bytes 98336 | tf_op jit(solution)/shard_map/ppermute | solution.py:133
  18.6 5.3 %ffn.1 = bf16[128,3072]{1,0:T(8,128)(2,1)S(1)} custom-call(bf16[128,3072]{1,0:T(8,128)(2,1)S(1)} %constant_dynamic-update-slice_fusion.6.rows_ref, bf16[3072,2048]{1,0:T(8,128)(2,1)S(1)} %bitcast.5, bf16[3072,2048]{1,0:T(8,128)(2,1)S(1)} %bitcast.6, bf16[2048,3072]{1,0:T(8,128)(2,1)S(1)} %bitcast.7), custom_call_target="tpu_custom_call" | custom-call | flops 4831838208 | bytes 37748736 | tf_op jit(solution)/shard_map/ffn/pallas_call | solution.py:158
  24.7 0.8 %collective-permute-done.9 = bf16[32,3072]{1,0:T(8,128)(2,1)S(1)} collective-permute-done((bf16[32,3072]{1,0:T(8,128)(2,1)S(1)}, bf16[32,3072]{1,0:T(8,128)(2,1)S(1)}, u32[]{:S(2)}, u32[]{:S(2)}) %collective-permute-start.9) | collective-permute-done | bytes 196640 | tf_op jit(solution)/shard_map/ppermute | solution.py:133
  25.6 0.6 %collective-permute-start.10 = (bf16[8,3072]{1,0:T(8,128)(2,1)S(1)}, bf16[8,3072]{1,0:T(8,128)(2,1)S(1)}, u32[]{:S(2)}, u32[]{:S(2)}) collective-permute-start(bf16[8,3072]{1,0:T(8,128)(2,1)S(1)} %get-tuple-element.15), channel_id=1, source_target_pairs={{0,2},{2,0},{4,6},{6,4},{8,10},{10,8},{12,14},{14,12},{1,3},{3,1},... | collective-permute-start | bytes 147464 | tf_op jit(solution)/shard_map/ppermute | solution.py:133
  26.2 1.5 %collective-permute-start.12 = (bf16[8,3072]{1,0:T(8,128)(2,1)S(1)}, bf16[8,3072]{1,0:T(8,128)(2,1)S(1)}, u32[]{:S(2)}, u32[]{:S(2)}) collective-permute-start(bf16[8,3072]{1,0:T(8,128)(2,1)S(1)} %get-tuple-element.17), channel_id=1, source_target_pairs={{0,2},{2,0},{4,6},{6,4},{8,10},{10,8},{12,14},{14,12},{1,3},{3,1},... | collective-permute-start | bytes 147464 | tf_op jit(solution)/shard_map/ppermute | solution.py:133
  27.7 0.6 %collective-permute-start.15 = (bf16[8,3072]{1,0:T(8,128)(2,1)S(1)}, bf16[8,3072]{1,0:T(8,128)(2,1)S(1)}, u32[]{:S(2)}, u32[]{:S(2)}) collective-permute-start(bf16[8,3072]{1,0:T(8,128)(2,1)S(1)} %get-tuple-element.19), channel_id=1, source_target_pairs={{0,2},{2,0},{4,6},{6,4},{8,10},{10,8},{12,14},{14,12},{1,3},{3,1},... | collective-permute-start | bytes 147464 | tf_op jit(solution)/shard_map/ppermute | solution.py:133
  28.3 1.6 %collective-permute-done.10 = bf16[8,3072]{1,0:T(8,128)(2,1)S(1)} collective-permute-done((bf16[8,3072]{1,0:T(8,128)(2,1)S(1)}, bf16[8,3072]{1,0:T(8,128)(2,1)S(1)}, u32[]{:S(2)}, u32[]{:S(2)}) %collective-permute-start.10) | collective-permute-done | bytes 49184 | tf_op jit(solution)/shard_map/ppermute | solution.py:133
  30.0 2.2 %collective-permute-start.11 = (bf16[8,3072]{1,0:T(8,128)(2,1)S(1)}, bf16[8,3072]{1,0:T(8,128)(2,1)S(1)}, u32[]{:S(2)}, u32[]{:S(2)}) collective-permute-start(bf16[8,3072]{1,0:T(8,128)(2,1)S(1)} %add_convert_fusion.5), channel_id=1, source_target_pairs={{0,12},{2,14},{4,8},{6,10},{8,4},{10,6},{12,0},{14,2},{1,13},{3,15... | collective-permute-start | bytes 147464 | tf_op jit(solution)/shard_map/ppermute | solution.py:130
  32.3 1.4 %collective-permute-start.17 = (bf16[8,3072]{1,0:T(8,128)(2,1)S(1)}, bf16[8,3072]{1,0:T(8,128)(2,1)S(1)}, u32[]{:S(2)}, u32[]{:S(2)}) collective-permute-start(bf16[8,3072]{1,0:T(8,128)(2,1)S(1)} %get-tuple-element.22), channel_id=1, source_target_pairs={{0,2},{2,0},{4,6},{6,4},{8,10},{10,8},{12,14},{14,12},{1,3},{3,1},... | collective-permute-start | bytes 147464 | tf_op jit(solution)/shard_map/ppermute | solution.py:133
  33.7 1.5 %collective-permute-start.16 = (bf16[8,3072]{1,0:T(8,128)(2,1)S(1)}, bf16[8,3072]{1,0:T(8,128)(2,1)S(1)}, u32[]{:S(2)}, u32[]{:S(2)}) collective-permute-start(bf16[8,3072]{1,0:T(8,128)(2,1)S(1)} %add_convert_fusion.3), channel_id=1, source_target_pairs={{0,4},{2,6},{4,0},{6,2},{8,12},{10,14},{12,8},{14,10},{1,5},{3,7},... | collective-permute-start | bytes 147464 | tf_op jit(solution)/shard_map/ppermute | solution.py:130
  35.2 1.2 %collective-permute-done.17 = bf16[8,3072]{1,0:T(8,128)(2,1)S(1)} collective-permute-done((bf16[8,3072]{1,0:T(8,128)(2,1)S(1)}, bf16[8,3072]{1,0:T(8,128)(2,1)S(1)}, u32[]{:S(2)}, u32[]{:S(2)}) %collective-permute-start.17) | collective-permute-done | bytes 49184 | tf_op jit(solution)/shard_map/ppermute | solution.py:133
  36.5 0.8 %collective-permute-done.13 = bf16[8,3072]{1,0:T(8,128)(2,1)S(1)} collective-permute-done((bf16[8,3072]{1,0:T(8,128)(2,1)S(1)}, bf16[8,3072]{1,0:T(8,128)(2,1)S(1)}, u32[]{:S(2)}, u32[]{:S(2)}) %collective-permute-start.13) | collective-permute-done | bytes 49184 | tf_op jit(solution)/shard_map/ppermute | solution.py:130
  37.3 0.6 %collective-permute-done.16 = bf16[8,3072]{1,0:T(8,128)(2,1)S(1)} collective-permute-done((bf16[8,3072]{1,0:T(8,128)(2,1)S(1)}, bf16[8,3072]{1,0:T(8,128)(2,1)S(1)}, u32[]{:S(2)}, u32[]{:S(2)}) %collective-permute-start.16) | collective-permute-done | bytes 49184 | tf_op jit(solution)/shard_map/ppermute | solution.py:130
  37.9 0.8 %combine.1 = bf16[16,3072]{1,0:T(8,128)(2,1)} custom-call(bf16[32,16]{1,0:T(8,128)(2,1)S(1)} %weigh.1.comb_ref, bf16[32,3072]{1,0:T(8,128)(2,1)S(1)} %pad_maximum_fusion.2.results_ref), custom_call_target="tpu_custom_call" | custom-call | tf_op jit(solution)/shard_map/combine/pallas_call | solution.py:196
  (50 shorter events, 1.5 us)
Async XLA Ops:
  0.0 8.8 %copy-start.3 = (s32[16,2]{0,1:T(2,128)S(1)}, s32[16,2]{0,1:T(2,128)}, u32[]{:S(2)}) copy-start(s32[16,2]{0,1:T(2,128)} %param.7) | copy-start | bytes 388
  0.0 8.8 %copy-start.4 = (bf16[16,2]{0,1:T(2,128)(2,1)S(1)}, bf16[16,2]{0,1:T(2,128)(2,1)}, u32[]{:S(2)}) copy-start(bf16[16,2]{0,1:T(2,128)(2,1)} %param.8) | copy-start | bytes 196
  0.0 18.5 %copy-start = (bf16[1,3072,2048]{2,1,0:T(8,128)(2,1)S(1)}, bf16[1,3072,2048]{2,1,0:T(8,128)(2,1)}, u32[]{:S(2)}) copy-start(bf16[1,3072,2048]{2,1,0:T(8,128)(2,1)} %param.9) | copy-start | bytes 37748740
  0.0 18.5 %copy-start.1 = (bf16[1,3072,2048]{2,1,0:T(8,128)(2,1)S(1)}, bf16[1,3072,2048]{2,1,0:T(8,128)(2,1)}, u32[]{:S(2)}) copy-start(bf16[1,3072,2048]{2,1,0:T(8,128)(2,1)} %param.10) | copy-start | bytes 37748740
  0.0 18.5 %copy-start.2 = (bf16[1,2048,3072]{2,1,0:T(8,128)(2,1)S(1)}, bf16[1,2048,3072]{2,1,0:T(8,128)(2,1)}, u32[]{:S(2)}) copy-start(bf16[1,2048,3072]{2,1,0:T(8,128)(2,1)} %param.11) | copy-start | bytes 37748740
  1.4 7.6 %collective-permute-start = (bf16[8,3072]{1,0:T(8,128)(2,1)S(1)}, bf16[8,3072]{1,0:T(8,128)(2,1)S(1)}, u32[]{:S(2)}, u32[]{:S(2)}) collective-permute-start(bf16[8,3072]{1,0:T(8,128)(2,1)S(1)} %get-tuple-element.45), channel_id=1, source_target_pairs={{0,12},{2,14},{4,8},{6,10},{8,4},{10,6},{12,0},{14,2},{1,13},{3,15... | collective-permute-start | bytes 147464 | tf_op jit(solution)/shard_map/ppermute | solution.py:130
  6.6 5.0 %collective-permute-start.1 = (bf16[8,3072]{1,0:T(8,128)(2,1)S(1)}, bf16[8,3072]{1,0:T(8,128)(2,1)S(1)}, u32[]{:S(2)}, u32[]{:S(2)}) collective-permute-start(bf16[8,3072]{1,0:T(8,128)(2,1)S(1)} %get-tuple-element.44), channel_id=1, source_target_pairs={{0,8},{2,10},{4,12},{6,14},{8,0},{10,2},{12,4},{14,6},{1,9},{3,11}... | collective-permute-start | bytes 147464 | tf_op jit(solution)/shard_map/ppermute | solution.py:130
  6.6 6.5 %collective-permute-start.2 = (bf16[8,3072]{1,0:T(8,128)(2,1)S(1)}, bf16[8,3072]{1,0:T(8,128)(2,1)S(1)}, u32[]{:S(2)}, u32[]{:S(2)}) collective-permute-start(bf16[8,3072]{1,0:T(8,128)(2,1)S(1)} %get-tuple-element.43), channel_id=1, source_target_pairs={{0,4},{2,6},{4,0},{6,2},{8,12},{10,14},{12,8},{14,10},{1,5},{3,7},... | collective-permute-start | bytes 147464 | tf_op jit(solution)/shard_map/ppermute | solution.py:130
  7.2 6.4 %collective-permute-start.3 = (bf16[8,3072]{1,0:T(8,128)(2,1)S(1)}, bf16[8,3072]{1,0:T(8,128)(2,1)S(1)}, u32[]{:S(2)}, u32[]{:S(2)}) collective-permute-start(bf16[8,3072]{1,0:T(8,128)(2,1)S(1)} %get-tuple-element.46), channel_id=1, source_target_pairs={{0,2},{2,0},{4,6},{6,4},{8,10},{10,8},{12,14},{14,12},{1,3},{3,1},... | collective-permute-start | bytes 147464 | tf_op jit(solution)/shard_map/ppermute | solution.py:133
  9.0 4.7 %collective-permute-start.4 = (bf16[8,3072]{1,0:T(8,128)(2,1)S(1)}, bf16[8,3072]{1,0:T(8,128)(2,1)S(1)}, u32[]{:S(2)}, u32[]{:S(2)}) collective-permute-start(bf16[8,3072]{1,0:T(8,128)(2,1)S(1)} %collective-permute-done), channel_id=1, source_target_pairs={{0,2},{2,0},{4,6},{6,4},{8,10},{10,8},{12,14},{14,12},{1,3},{3,1},... | collective-permute-start | bytes 147464 | tf_op jit(solution)/shard_map/ppermute | solution.py:133
  11.6 4.1 %collective-permute-start.5 = (bf16[8,3072]{1,0:T(8,128)(2,1)S(1)}, bf16[8,3072]{1,0:T(8,128)(2,1)S(1)}, u32[]{:S(2)}, u32[]{:S(2)}) collective-permute-start(bf16[8,3072]{1,0:T(8,128)(2,1)S(1)} %collective-permute-done.1), channel_id=1, source_target_pairs={{0,2},{2,0},{4,6},{6,4},{8,10},{10,8},{12,14},{14,12},{1,3},{3,1},... | collective-permute-start | bytes 147464 | tf_op jit(solution)/shard_map/ppermute | solution.py:133
  13.1 4.1 %collective-permute-start.6 = (bf16[8,3072]{1,0:T(8,128)(2,1)S(1)}, bf16[8,3072]{1,0:T(8,128)(2,1)S(1)}, u32[]{:S(2)}, u32[]{:S(2)}) collective-permute-start(bf16[8,3072]{1,0:T(8,128)(2,1)S(1)} %collective-permute-done.2), channel_id=1, source_target_pairs={{0,2},{2,0},{4,6},{6,4},{8,10},{10,8},{12,14},{14,12},{1,3},{3,1},... | collective-permute-start | bytes 147464 | tf_op jit(solution)/shard_map/ppermute | solution.py:133
  13.7 3.6 %collective-permute-start.7 = (bf16[48,3072]{1,0:T(8,128)(2,1)S(1)}, bf16[48,3072]{1,0:T(8,128)(2,1)S(1)}, u32[]{:S(2)}, u32[]{:S(2)}) collective-permute-start(bf16[48,3072]{1,0:T(8,128)(2,1)S(1)} %get-tuple-element.47), channel_id=1, source_target_pairs={{0,1},{1,0},{2,3},{3,2},{4,5},{5,4},{6,7},{7,6},{8,9},{9,8},{10,11... | collective-permute-start | bytes 884744 | tf_op jit(solution)/shard_map/ppermute | solution.py:133
  17.2 1.4 %collective-permute-start.8 = (bf16[16,3072]{1,0:T(8,128)(2,1)S(1)}, bf16[16,3072]{1,0:T(8,128)(2,1)S(1)}, u32[]{:S(2)}, u32[]{:S(2)}) collective-permute-start(bf16[16,3072]{1,0:T(8,128)(2,1)S(1)} %pad_maximum_fusion.3), channel_id=1, source_target_pairs={{0,1},{1,0},{2,3},{3,2},{4,5},{5,4},{6,7},{7,6},{8,9},{9,8},{10,11... | collective-permute-start | bytes 294920 | tf_op jit(solution)/shard_map/ppermute | solution.py:133
  24.0 1.5 %collective-permute-start.9 = (bf16[32,3072]{1,0:T(8,128)(2,1)S(1)}, bf16[32,3072]{1,0:T(8,128)(2,1)S(1)}, u32[]{:S(2)}, u32[]{:S(2)}) collective-permute-start(bf16[32,3072]{1,0:T(8,128)(2,1)S(1)} %pad_maximum_fusion), channel_id=1, source_target_pairs={{0,1},{1,0},{2,3},{3,2},{4,5},{5,4},{6,7},{7,6},{8,9},{9,8},{10,11... | collective-permute-start | bytes 589832 | tf_op jit(solution)/shard_map/ppermute | solution.py:133
  24.2 3.5 %collective-permute-start.14 = (bf16[32,3072]{1,0:T(8,128)(2,1)S(1)}, bf16[32,3072]{1,0:T(8,128)(2,1)S(1)}, u32[]{:S(2)}, u32[]{:S(2)}) collective-permute-start(bf16[32,3072]{1,0:T(8,128)(2,1)S(1)} %pad_maximum_fusion.1), channel_id=1, source_target_pairs={{0,1},{1,0},{2,3},{3,2},{4,5},{5,4},{6,7},{7,6},{8,9},{9,8},{10,11... | collective-permute-start | bytes 589832 | tf_op jit(solution)/shard_map/ppermute | solution.py:133
  25.6 4.4 %collective-permute-start.10 = (bf16[8,3072]{1,0:T(8,128)(2,1)S(1)}, bf16[8,3072]{1,0:T(8,128)(2,1)S(1)}, u32[]{:S(2)}, u32[]{:S(2)}) collective-permute-start(bf16[8,3072]{1,0:T(8,128)(2,1)S(1)} %get-tuple-element.15), channel_id=1, source_target_pairs={{0,2},{2,0},{4,6},{6,4},{8,10},{10,8},{12,14},{14,12},{1,3},{3,1},... | collective-permute-start | bytes 147464 | tf_op jit(solution)/shard_map/ppermute | solution.py:133
  26.2 6.0 %collective-permute-start.12 = (bf16[8,3072]{1,0:T(8,128)(2,1)S(1)}, bf16[8,3072]{1,0:T(8,128)(2,1)S(1)}, u32[]{:S(2)}, u32[]{:S(2)}) collective-permute-start(bf16[8,3072]{1,0:T(8,128)(2,1)S(1)} %get-tuple-element.17), channel_id=1, source_target_pairs={{0,2},{2,0},{4,6},{6,4},{8,10},{10,8},{12,14},{14,12},{1,3},{3,1},... | collective-permute-start | bytes 147464 | tf_op jit(solution)/shard_map/ppermute | solution.py:133
  27.7 4.6 %collective-permute-start.15 = (bf16[8,3072]{1,0:T(8,128)(2,1)S(1)}, bf16[8,3072]{1,0:T(8,128)(2,1)S(1)}, u32[]{:S(2)}, u32[]{:S(2)}) collective-permute-start(bf16[8,3072]{1,0:T(8,128)(2,1)S(1)} %get-tuple-element.19), channel_id=1, source_target_pairs={{0,2},{2,0},{4,6},{6,4},{8,10},{10,8},{12,14},{14,12},{1,3},{3,1},... | collective-permute-start | bytes 147464 | tf_op jit(solution)/shard_map/ppermute | solution.py:133
  30.0 6.5 %collective-permute-start.11 = (bf16[8,3072]{1,0:T(8,128)(2,1)S(1)}, bf16[8,3072]{1,0:T(8,128)(2,1)S(1)}, u32[]{:S(2)}, u32[]{:S(2)}) collective-permute-start(bf16[8,3072]{1,0:T(8,128)(2,1)S(1)} %add_convert_fusion.5), channel_id=1, source_target_pairs={{0,12},{2,14},{4,8},{6,10},{8,4},{10,6},{12,0},{14,2},{1,13},{3,15... | collective-permute-start | bytes 147464 | tf_op jit(solution)/shard_map/ppermute | solution.py:130
  32.2 5.1 %collective-permute-start.13 = (bf16[8,3072]{1,0:T(8,128)(2,1)S(1)}, bf16[8,3072]{1,0:T(8,128)(2,1)S(1)}, u32[]{:S(2)}, u32[]{:S(2)}) collective-permute-start(bf16[8,3072]{1,0:T(8,128)(2,1)S(1)} %add_convert_fusion.4), channel_id=1, source_target_pairs={{0,8},{2,10},{4,12},{6,14},{8,0},{10,2},{12,4},{14,6},{1,9},{3,11}... | collective-permute-start | bytes 147464 | tf_op jit(solution)/shard_map/ppermute | solution.py:130
  32.3 4.1 %collective-permute-start.17 = (bf16[8,3072]{1,0:T(8,128)(2,1)S(1)}, bf16[8,3072]{1,0:T(8,128)(2,1)S(1)}, u32[]{:S(2)}, u32[]{:S(2)}) collective-permute-start(bf16[8,3072]{1,0:T(8,128)(2,1)S(1)} %get-tuple-element.22), channel_id=1, source_target_pairs={{0,2},{2,0},{4,6},{6,4},{8,10},{10,8},{12,14},{14,12},{1,3},{3,1},... | collective-permute-start | bytes 147464 | tf_op jit(solution)/shard_map/ppermute | solution.py:133
  33.7 4.2 %collective-permute-start.16 = (bf16[8,3072]{1,0:T(8,128)(2,1)S(1)}, bf16[8,3072]{1,0:T(8,128)(2,1)S(1)}, u32[]{:S(2)}, u32[]{:S(2)}) collective-permute-start(bf16[8,3072]{1,0:T(8,128)(2,1)S(1)} %add_convert_fusion.3), channel_id=1, source_target_pairs={{0,4},{2,6},{4,0},{6,2},{8,12},{10,14},{12,8},{14,10},{1,5},{3,7},... | collective-permute-start | bytes 147464 | tf_op jit(solution)/shard_map/ppermute | solution.py:130

commit v6 on v5

--- a/solution.py
+++ b/solution.py
@@ -44,9 +44,9 @@
     ]
     for copy in copies:
         copy.start()
-    for copy in copies:
-        copy.wait()
+    copies[0].wait()
     chosen, _ = choose(steps, capacity, routes_ref[...])
+    copies[1].wait()
     out_ref[...] = jnp.dot(
         chosen.astype(BF16), tokens_ref[...], preferred_element_type=F32
     ).astype(BF16)
@@ -146,7 +146,7 @@
         there.update(zip(group, cut(swap(join([here[s] for s in group]), "expert"))))
     order = [(side, s) for side in (0, 1) for s in [0] + steps]
     names = [(side, s) for side in (here, there) for s in [0] + steps]
-    pieces = [join([side[s] for side, s in names[:-2]]), join([side[s] for side, s in names[-2:]])]
+    pieces = [join([side[s] for side, s in names[:-1]]), join([side[s] for side, s in names[-1:]])]
     both = join(pieces)
     if tiles == 2:
         received = join(pieces + [swap(piece, "tile") for piece in pieces])
@@ -185,13 +185,11 @@
         both = jnp.sum(pieces.astype(F32), axis=0).astype(BF16)
         summed = dict(zip(order, lax.optimization_barrier(cut(both))))
     results = {}
-    for s in blocks:
-        leaving = summed[1, s]
-        if s == 0:
-            leaving, _ = lax.optimization_barrier((leaving, back))
-        back = swap(leaving, "expert")
-        total = add(summed[0, s], back)
-        results[s] = trade(total, s) if s else total
+    for group in [[s] for s in steps[:-1]] + [[steps[-1], 0]]:
+        back = swap(join([summed[1, s] for s in group]), "expert")
+        for s, block in zip(group, cut(back)):
+            total = add(summed[0, s], block)
+            results[s] = trade(total, s) if s else total
     results = join([results[s] for s in blocks])
     return pl.pallas_call(
         combine_kernel,

time: 38.9 us -> 38.2 us (0.982)
  starting transfers between devices: 19.7 us -> 19 us
    ppermute x6, waiting for transfers between devices: 2.36 us -> 3.71 us  [trade(): return lax.ppermute(x, 'expert', pairs)]
    ppermute x12 -> x11, starting transfers between devices: 10.1 us -> 8.85 us  [swap(): lax.ppermute(x, axis, [(i, i ^ 1) for i in range(lax.axis_size(axis))])]
    ppermute x12 -> x11, waiting for transfers between devices: 8.32 us -> 7.21 us  [swap(): lax.ppermute(x, axis, [(i, i ^ 1) for i in range(lax.axis_size(axis))])]
    ppermute x6, starting transfers between devices: 9.61 us -> 10.1 us  [trade(): return lax.ppermute(x, 'expert', pairs)]
  transfers between devices with their start and end apart: 18 -> 17, of which waited for: 9 -> 10; matrix products, arithmetic and copies ran while one was open for 1% -> 1% of each run, Pallas kernels for 0% -> 0%
where the time goes in v6:
time: 38.2 us; the launch traced here: 38.1 us
  starting transfers between devices  19 us (50%)
  waiting for transfers between devices  10.9 us (29%)
  Pallas kernels  7.56 us (20%)
    ppermute x6, starting transfers between devices, trade(): return lax.ppermute(x, 'expert', pairs)  10.1 us
    ppermute x11, starting transfers between devices, swap(): lax.ppermute(x, axis, [(i, i ^ 1) for i in range(lax.axis_size(axis))])  8.85 us
    ppermute x11, waiting for transfers between devices, swap(): lax.ppermute(x, axis, [(i, i ^ 1) for i in range(lax.axis_size(axis))])  7.21 us
    pallas_call x1, Pallas kernels, shards(): pl.pallas_call(functools.partial(ffn_kernel, block), out_shape=jax.ShapeD...  5.32 us
    ppermute x6, waiting for transfers between devices, trade(): return lax.ppermute(x, 'expert', pairs)  3.71 us
    pallas_call x1, Pallas kernels, shards(): pl.pallas_call(functools.partial(route_kernel, blocks, capacity), out_sha...  1.26 us
    pallas_call x1, Pallas kernels, shards(): pl.pallas_call(combine_kernel, out_shape=jax.ShapeDtypeStruct((rows, widt...  0.84 us
  transfers between devices with their start and end apart: 17, of which 10 were waited for; matrix products, arithmetic and copies ran while one was open for 1% of the time, Pallas kernels for 0%

profile of v6, /device:TPU:0, one launch (start us, length us, event | category | flops | bytes accessed | tf_op | source)
XLA Modules:
  0.0 38.1 jit_solution(15420309143321230907)
XLA Ops:
  0.0 1.3 %route.1 = bf16[32,3072]{1,0:T(8,128)(2,1)S(1)} custom-call(s32[2,16]{1,0:T(2,128)} %bitcast.8, bf16[16,3072]{1,0:T(8,128)(2,1)} %tokens_hbm.1), custom_call_target="tpu_custom_call" | custom-call | flops 999999995904 | bytes 400000000 | tf_op jit(solution)/shard_map/route/pallas_call | solution.py:100
  1.3 5.1 %collective-permute-start = (bf16[8,3072]{1,0:T(8,128)(2,1)S(1)}, bf16[8,3072]{1,0:T(8,128)(2,1)S(1)}, u32[]{:S(2)}, u32[]{:S(2)}) collective-permute-start(bf16[8,3072]{1,0:T(8,128)(2,1)S(1)} %get-tuple-element.43), channel_id=1, source_target_pairs={{0,12},{2,14},{4,8},{6,10},{8,4},{10,6},{12,0},{14,2},{1,13},{3,15... | collective-permute-start | bytes 147464 | tf_op jit(solution)/shard_map/ppermute | solution.py:130
  6.4 0.6 %collective-permute-start.2 = (bf16[8,3072]{1,0:T(8,128)(2,1)S(1)}, bf16[8,3072]{1,0:T(8,128)(2,1)S(1)}, u32[]{:S(2)}, u32[]{:S(2)}) collective-permute-start(bf16[8,3072]{1,0:T(8,128)(2,1)S(1)} %get-tuple-element.41), channel_id=1, source_target_pairs={{0,4},{2,6},{4,0},{6,2},{8,12},{10,14},{12,8},{14,10},{1,5},{3,7},... | collective-permute-start | bytes 147464 | tf_op jit(solution)/shard_map/ppermute | solution.py:130
  7.1 1.6 %collective-permute-start.3 = (bf16[8,3072]{1,0:T(8,128)(2,1)S(1)}, bf16[8,3072]{1,0:T(8,128)(2,1)S(1)}, u32[]{:S(2)}, u32[]{:S(2)}) collective-permute-start(bf16[8,3072]{1,0:T(8,128)(2,1)S(1)} %get-tuple-element.44), channel_id=1, source_target_pairs={{0,2},{2,0},{4,6},{6,4},{8,10},{10,8},{12,14},{14,12},{1,3},{3,1},... | collective-permute-start | bytes 147464 | tf_op jit(solution)/shard_map/ppermute | solution.py:133
  8.7 1.7 %collective-permute-start.4 = (bf16[8,3072]{1,0:T(8,128)(2,1)S(1)}, bf16[8,3072]{1,0:T(8,128)(2,1)S(1)}, u32[]{:S(2)}, u32[]{:S(2)}) collective-permute-start(bf16[8,3072]{1,0:T(8,128)(2,1)S(1)} %collective-permute-done), channel_id=1, source_target_pairs={{0,2},{2,0},{4,6},{6,4},{8,10},{10,8},{12,14},{14,12},{1,3},{3,1},... | collective-permute-start | bytes 147464 | tf_op jit(solution)/shard_map/ppermute | solution.py:133
  10.5 1.0 %collective-permute-done.1 = bf16[8,3072]{1,0:T(8,128)(2,1)S(1)} collective-permute-done((bf16[8,3072]{1,0:T(8,128)(2,1)S(1)}, bf16[8,3072]{1,0:T(8,128)(2,1)S(1)}, u32[]{:S(2)}, u32[]{:S(2)}) %collective-permute-start.1) | collective-permute-done | bytes 49184 | tf_op jit(solution)/shard_map/ppermute | solution.py:130
  11.4 1.5 %collective-permute-start.5 = (bf16[8,3072]{1,0:T(8,128)(2,1)S(1)}, bf16[8,3072]{1,0:T(8,128)(2,1)S(1)}, u32[]{:S(2)}, u32[]{:S(2)}) collective-permute-start(bf16[8,3072]{1,0:T(8,128)(2,1)S(1)} %collective-permute-done.1), channel_id=1, source_target_pairs={{0,2},{2,0},{4,6},{6,4},{8,10},{10,8},{12,14},{14,12},{1,3},{3,1},... | collective-permute-start | bytes 147464 | tf_op jit(solution)/shard_map/ppermute | solution.py:133
  12.9 0.5 %collective-permute-start.6 = (bf16[8,3072]{1,0:T(8,128)(2,1)S(1)}, bf16[8,3072]{1,0:T(8,128)(2,1)S(1)}, u32[]{:S(2)}, u32[]{:S(2)}) collective-permute-start(bf16[8,3072]{1,0:T(8,128)(2,1)S(1)} %collective-permute-done.2), channel_id=1, source_target_pairs={{0,2},{2,0},{4,6},{6,4},{8,10},{10,8},{12,14},{14,12},{1,3},{3,1},... | collective-permute-start | bytes 147464 | tf_op jit(solution)/shard_map/ppermute | solution.py:133
  13.5 2.0 %collective-permute-done.5 = bf16[8,3072]{1,0:T(8,128)(2,1)S(1)} collective-permute-done((bf16[8,3072]{1,0:T(8,128)(2,1)S(1)}, bf16[8,3072]{1,0:T(8,128)(2,1)S(1)}, u32[]{:S(2)}, u32[]{:S(2)}) %collective-permute-start.5) | collective-permute-done | bytes 49184 | tf_op jit(solution)/shard_map/ppermute | solution.py:133
  15.6 1.4 %collective-permute-done.6 = bf16[8,3072]{1,0:T(8,128)(2,1)S(1)} collective-permute-done((bf16[8,3072]{1,0:T(8,128)(2,1)S(1)}, bf16[8,3072]{1,0:T(8,128)(2,1)S(1)}, u32[]{:S(2)}, u32[]{:S(2)}) %collective-permute-start.6) | collective-permute-done | bytes 49184 | tf_op jit(solution)/shard_map/ppermute | solution.py:133
  17.3 1.0 %collective-permute-done.8 = bf16[8,3072]{1,0:T(8,128)(2,1)S(1)} collective-permute-done((bf16[8,3072]{1,0:T(8,128)(2,1)S(1)}, bf16[8,3072]{1,0:T(8,128)(2,1)S(1)}, u32[]{:S(2)}, u32[]{:S(2)}) %collective-permute-start.8) | collective-permute-done | bytes 49184 | tf_op jit(solution)/shard_map/ppermute | solution.py:133
  18.3 5.3 %ffn.1 = bf16[128,3072]{1,0:T(8,128)(2,1)S(1)} custom-call(bf16[128,3072]{1,0:T(8,128)(2,1)S(1)} %constant_dynamic-update-slice_fusion.7.rows_ref, bf16[3072,2048]{1,0:T(8,128)(2,1)S(1)} %bitcast.5, bf16[3072,2048]{1,0:T(8,128)(2,1)S(1)} %bitcast.6, bf16[2048,3072]{1,0:T(8,128)(2,1)S(1)} %bitcast.7), custom_call_target="tpu_custom_call" | custom-call | flops 4831838208 | bytes 37748736 | tf_op jit(solution)/shard_map/ffn/pallas_call | solution.py:158
  23.9 0.4 %collective-permute-start.14 = (bf16[32,3072]{1,0:T(8,128)(2,1)S(1)}, bf16[32,3072]{1,0:T(8,128)(2,1)S(1)}, u32[]{:S(2)}, u32[]{:S(2)}) collective-permute-start(bf16[32,3072]{1,0:T(8,128)(2,1)S(1)} %pad_maximum_fusion.1), channel_id=1, source_target_pairs={{0,1},{1,0},{2,3},{3,2},{4,5},{5,4},{6,7},{7,6},{8,9},{9,8},{10,11... | collective-permute-start | bytes 589832 | tf_op jit(solution)/shard_map/ppermute | solution.py:133
  24.4 0.8 %collective-permute-done.9 = bf16[32,3072]{1,0:T(8,128)(2,1)S(1)} collective-permute-done((bf16[32,3072]{1,0:T(8,128)(2,1)S(1)}, bf16[32,3072]{1,0:T(8,128)(2,1)S(1)}, u32[]{:S(2)}, u32[]{:S(2)}) %collective-permute-start.9) | collective-permute-done | bytes 196640 | tf_op jit(solution)/shard_map/ppermute | solution.py:133
  25.3 0.6 %collective-permute-start.10 = (bf16[8,3072]{1,0:T(8,128)(2,1)S(1)}, bf16[8,3072]{1,0:T(8,128)(2,1)S(1)}, u32[]{:S(2)}, u32[]{:S(2)}) collective-permute-start(bf16[8,3072]{1,0:T(8,128)(2,1)S(1)} %get-tuple-element.14), channel_id=1, source_target_pairs={{0,2},{2,0},{4,6},{6,4},{8,10},{10,8},{12,14},{14,12},{1,3},{3,1},... | collective-permute-start | bytes 147464 | tf_op jit(solution)/shard_map/ppermute | solution.py:133
  25.9 1.5 %collective-permute-start.12 = (bf16[8,3072]{1,0:T(8,128)(2,1)S(1)}, bf16[8,3072]{1,0:T(8,128)(2,1)S(1)}, u32[]{:S(2)}, u32[]{:S(2)}) collective-permute-start(bf16[8,3072]{1,0:T(8,128)(2,1)S(1)} %get-tuple-element.16), channel_id=1, source_target_pairs={{0,2},{2,0},{4,6},{6,4},{8,10},{10,8},{12,14},{14,12},{1,3},{3,1},... | collective-permute-start | bytes 147464 | tf_op jit(solution)/shard_map/ppermute | solution.py:133
  27.5 0.6 %collective-permute-start.15 = (bf16[16,3072]{1,0:T(8,128)(2,1)S(1)}, bf16[16,3072]{1,0:T(8,128)(2,1)S(1)}, u32[]{:S(2)}, u32[]{:S(2)}) collective-permute-start(bf16[16,3072]{1,0:T(8,128)(2,1)S(1)} %pad_maximum_fusion.3), channel_id=1, source_target_pairs={{0,2},{2,0},{4,6},{6,4},{8,10},{10,8},{12,14},{14,12},{1,3},{3,1},... | collective-permute-start | bytes 294920 | tf_op jit(solution)/shard_map/ppermute | solution.py:133
  28.1 1.6 %collective-permute-done.10 = bf16[8,3072]{1,0:T(8,128)(2,1)S(1)} collective-permute-done((bf16[8,3072]{1,0:T(8,128)(2,1)S(1)}, bf16[8,3072]{1,0:T(8,128)(2,1)S(1)}, u32[]{:S(2)}, u32[]{:S(2)}) %collective-permute-start.10) | collective-permute-done | bytes 49184 | tf_op jit(solution)/shard_map/ppermute | solution.py:133
  29.7 2.2 %collective-permute-start.11 = (bf16[8,3072]{1,0:T(8,128)(2,1)S(1)}, bf16[8,3072]{1,0:T(8,128)(2,1)S(1)}, u32[]{:S(2)}, u32[]{:S(2)}) collective-permute-start(bf16[8,3072]{1,0:T(8,128)(2,1)S(1)} %add_convert_fusion.5), channel_id=1, source_target_pairs={{0,12},{2,14},{4,8},{6,10},{8,4},{10,6},{12,0},{14,2},{1,13},{3,15... | collective-permute-start | bytes 147464 | tf_op jit(solution)/shard_map/ppermute | solution.py:130
  31.9 0.2 collective-permute-start.13
  32.3 2.0 %collective-permute-start.16 = (bf16[8,3072]{1,0:T(8,128)(2,1)S(1)}, bf16[8,3072]{1,0:T(8,128)(2,1)S(1)}, u32[]{:S(2)}, u32[]{:S(2)}) collective-permute-start(bf16[8,3072]{1,0:T(8,128)(2,1)S(1)} %get-tuple-element.45), channel_id=1, source_target_pairs={{0,4},{2,6},{4,0},{6,2},{8,12},{10,14},{12,8},{14,10},{1,5},{3,7},... | collective-permute-start | bytes 147464 | tf_op jit(solution)/shard_map/ppermute | solution.py:130
  34.5 1.6 %collective-permute-done.11 = bf16[8,3072]{1,0:T(8,128)(2,1)S(1)} collective-permute-done((bf16[8,3072]{1,0:T(8,128)(2,1)S(1)}, bf16[8,3072]{1,0:T(8,128)(2,1)S(1)}, u32[]{:S(2)}, u32[]{:S(2)}) %collective-permute-start.11) | collective-permute-done | bytes 49184 | tf_op jit(solution)/shard_map/ppermute | solution.py:130
  36.1 1.1 %collective-permute-done.13 = bf16[8,3072]{1,0:T(8,128)(2,1)S(1)} collective-permute-done((bf16[8,3072]{1,0:T(8,128)(2,1)S(1)}, bf16[8,3072]{1,0:T(8,128)(2,1)S(1)}, u32[]{:S(2)}, u32[]{:S(2)}) %collective-permute-start.13) | collective-permute-done | bytes 49184 | tf_op jit(solution)/shard_map/ppermute | solution.py:130
  37.3 0.8 %combine.1 = bf16[16,3072]{1,0:T(8,128)(2,1)} custom-call(bf16[32,16]{1,0:T(8,128)(2,1)S(1)} %weigh.1.comb_ref, bf16[32,3072]{1,0:T(8,128)(2,1)S(1)} %pad_maximum_fusion.2.results_ref), custom_call_target="tpu_custom_call" | custom-call | tf_op jit(solution)/shard_map/combine/pallas_call | solution.py:194
  (47 shorter events, 1.3 us)
Async XLA Ops:
  0.0 18.2 %copy-start = (bf16[1,3072,2048]{2,1,0:T(8,128)(2,1)S(1)}, bf16[1,3072,2048]{2,1,0:T(8,128)(2,1)}, u32[]{:S(2)}) copy-start(bf16[1,3072,2048]{2,1,0:T(8,128)(2,1)} %param.9) | copy-start | bytes 37748740
  0.0 18.2 %copy-start.1 = (bf16[1,3072,2048]{2,1,0:T(8,128)(2,1)S(1)}, bf16[1,3072,2048]{2,1,0:T(8,128)(2,1)}, u32[]{:S(2)}) copy-start(bf16[1,3072,2048]{2,1,0:T(8,128)(2,1)} %param.10) | copy-start | bytes 37748740
  0.0 18.2 %copy-start.2 = (bf16[1,2048,3072]{2,1,0:T(8,128)(2,1)S(1)}, bf16[1,2048,3072]{2,1,0:T(8,128)(2,1)}, u32[]{:S(2)}) copy-start(bf16[1,2048,3072]{2,1,0:T(8,128)(2,1)} %param.11) | copy-start | bytes 37748740
  1.3 7.4 %collective-permute-start = (bf16[8,3072]{1,0:T(8,128)(2,1)S(1)}, bf16[8,3072]{1,0:T(8,128)(2,1)S(1)}, u32[]{:S(2)}, u32[]{:S(2)}) collective-permute-start(bf16[8,3072]{1,0:T(8,128)(2,1)S(1)} %get-tuple-element.43), channel_id=1, source_target_pairs={{0,12},{2,14},{4,8},{6,10},{8,4},{10,6},{12,0},{14,2},{1,13},{3,15... | collective-permute-start | bytes 147464 | tf_op jit(solution)/shard_map/ppermute | solution.py:130
  6.4 5.0 %collective-permute-start.1 = (bf16[8,3072]{1,0:T(8,128)(2,1)S(1)}, bf16[8,3072]{1,0:T(8,128)(2,1)S(1)}, u32[]{:S(2)}, u32[]{:S(2)}) collective-permute-start(bf16[8,3072]{1,0:T(8,128)(2,1)S(1)} %get-tuple-element.42), channel_id=1, source_target_pairs={{0,8},{2,10},{4,12},{6,14},{8,0},{10,2},{12,4},{14,6},{1,9},{3,11}... | collective-permute-start | bytes 147464 | tf_op jit(solution)/shard_map/ppermute | solution.py:130
  6.4 6.5 %collective-permute-start.2 = (bf16[8,3072]{1,0:T(8,128)(2,1)S(1)}, bf16[8,3072]{1,0:T(8,128)(2,1)S(1)}, u32[]{:S(2)}, u32[]{:S(2)}) collective-permute-start(bf16[8,3072]{1,0:T(8,128)(2,1)S(1)} %get-tuple-element.41), channel_id=1, source_target_pairs={{0,4},{2,6},{4,0},{6,2},{8,12},{10,14},{12,8},{14,10},{1,5},{3,7},... | collective-permute-start | bytes 147464 | tf_op jit(solution)/shard_map/ppermute | solution.py:130
  7.1 6.4 %collective-permute-start.3 = (bf16[8,3072]{1,0:T(8,128)(2,1)S(1)}, bf16[8,3072]{1,0:T(8,128)(2,1)S(1)}, u32[]{:S(2)}, u32[]{:S(2)}) collective-permute-start(bf16[8,3072]{1,0:T(8,128)(2,1)S(1)} %get-tuple-element.44), channel_id=1, source_target_pairs={{0,2},{2,0},{4,6},{6,4},{8,10},{10,8},{12,14},{14,12},{1,3},{3,1},... | collective-permute-start | bytes 147464 | tf_op jit(solution)/shard_map/ppermute | solution.py:133
  8.7 4.8 %collective-permute-start.4 = (bf16[8,3072]{1,0:T(8,128)(2,1)S(1)}, bf16[8,3072]{1,0:T(8,128)(2,1)S(1)}, u32[]{:S(2)}, u32[]{:S(2)}) collective-permute-start(bf16[8,3072]{1,0:T(8,128)(2,1)S(1)} %collective-permute-done), channel_id=1, source_target_pairs={{0,2},{2,0},{4,6},{6,4},{8,10},{10,8},{12,14},{14,12},{1,3},{3,1},... | collective-permute-start | bytes 147464 | tf_op jit(solution)/shard_map/ppermute | solution.py:133
  11.4 4.1 %collective-permute-start.5 = (bf16[8,3072]{1,0:T(8,128)(2,1)S(1)}, bf16[8,3072]{1,0:T(8,128)(2,1)S(1)}, u32[]{:S(2)}, u32[]{:S(2)}) collective-permute-start(bf16[8,3072]{1,0:T(8,128)(2,1)S(1)} %collective-permute-done.1), channel_id=1, source_target_pairs={{0,2},{2,0},{4,6},{6,4},{8,10},{10,8},{12,14},{14,12},{1,3},{3,1},... | collective-permute-start | bytes 147464 | tf_op jit(solution)/shard_map/ppermute | solution.py:133
  12.9 4.1 %collective-permute-start.6 = (bf16[8,3072]{1,0:T(8,128)(2,1)S(1)}, bf16[8,3072]{1,0:T(8,128)(2,1)S(1)}, u32[]{:S(2)}, u32[]{:S(2)}) collective-permute-start(bf16[8,3072]{1,0:T(8,128)(2,1)S(1)} %collective-permute-done.2), channel_id=1, source_target_pairs={{0,2},{2,0},{4,6},{6,4},{8,10},{10,8},{12,14},{14,12},{1,3},{3,1},... | collective-permute-start | bytes 147464 | tf_op jit(solution)/shard_map/ppermute | solution.py:133
  15.5 1.7 %collective-permute-start.7 = (bf16[56,3072]{1,0:T(8,128)(2,1)S(1)}, bf16[56,3072]{1,0:T(8,128)(2,1)S(1)}, u32[]{:S(2)}, u32[]{:S(2)}) collective-permute-start(bf16[56,3072]{1,0:T(8,128)(2,1)S(1)} %get-tuple-element.47), channel_id=1, source_target_pairs={{0,1},{1,0},{2,3},{3,2},{4,5},{5,4},{6,7},{7,6},{8,9},{9,8},{10,11... | collective-permute-start | bytes 1032200 | tf_op jit(solution)/shard_map/ppermute | solution.py:133
  17.0 1.2 %collective-permute-start.8 = (bf16[8,3072]{1,0:T(8,128)(2,1)S(1)}, bf16[8,3072]{1,0:T(8,128)(2,1)S(1)}, u32[]{:S(2)}, u32[]{:S(2)}) collective-permute-start(bf16[8,3072]{1,0:T(8,128)(2,1)S(1)} %collective-permute-done.6), channel_id=1, source_target_pairs={{0,1},{1,0},{2,3},{3,2},{4,5},{5,4},{6,7},{7,6},{8,9},{9,8},{10,11... | collective-permute-start | bytes 147464 | tf_op jit(solution)/shard_map/ppermute | solution.py:133
  18.3 16.1 %copy-start.3 = (s32[16,2]{0,1:T(2,128)S(1)}, s32[16,2]{0,1:T(2,128)}, u32[]{:S(2)}) copy-start(s32[16,2]{0,1:T(2,128)} %param.7) | copy-start | bytes 388
  18.3 16.1 %copy-start.4 = (bf16[16,2]{0,1:T(2,128)(2,1)S(1)}, bf16[16,2]{0,1:T(2,128)(2,1)}, u32[]{:S(2)}) copy-start(bf16[16,2]{0,1:T(2,128)(2,1)} %param.8) | copy-start | bytes 196
  23.7 1.5 %collective-permute-start.9 = (bf16[32,3072]{1,0:T(8,128)(2,1)S(1)}, bf16[32,3072]{1,0:T(8,128)(2,1)S(1)}, u32[]{:S(2)}, u32[]{:S(2)}) collective-permute-start(bf16[32,3072]{1,0:T(8,128)(2,1)S(1)} %pad_maximum_fusion), channel_id=1, source_target_pairs={{0,1},{1,0},{2,3},{3,2},{4,5},{5,4},{6,7},{7,6},{8,9},{9,8},{10,11... | collective-permute-start | bytes 589832 | tf_op jit(solution)/shard_map/ppermute | solution.py:133
  23.9 3.4 %collective-permute-start.14 = (bf16[32,3072]{1,0:T(8,128)(2,1)S(1)}, bf16[32,3072]{1,0:T(8,128)(2,1)S(1)}, u32[]{:S(2)}, u32[]{:S(2)}) collective-permute-start(bf16[32,3072]{1,0:T(8,128)(2,1)S(1)} %pad_maximum_fusion.1), channel_id=1, source_target_pairs={{0,1},{1,0},{2,3},{3,2},{4,5},{5,4},{6,7},{7,6},{8,9},{9,8},{10,11... | collective-permute-start | bytes 589832 | tf_op jit(solution)/shard_map/ppermute | solution.py:133
  25.3 4.4 %collective-permute-start.10 = (bf16[8,3072]{1,0:T(8,128)(2,1)S(1)}, bf16[8,3072]{1,0:T(8,128)(2,1)S(1)}, u32[]{:S(2)}, u32[]{:S(2)}) collective-permute-start(bf16[8,3072]{1,0:T(8,128)(2,1)S(1)} %get-tuple-element.14), channel_id=1, source_target_pairs={{0,2},{2,0},{4,6},{6,4},{8,10},{10,8},{12,14},{14,12},{1,3},{3,1},... | collective-permute-start | bytes 147464 | tf_op jit(solution)/shard_map/ppermute | solution.py:133
  25.9 6.0 %collective-permute-start.12 = (bf16[8,3072]{1,0:T(8,128)(2,1)S(1)}, bf16[8,3072]{1,0:T(8,128)(2,1)S(1)}, u32[]{:S(2)}, u32[]{:S(2)}) collective-permute-start(bf16[8,3072]{1,0:T(8,128)(2,1)S(1)} %get-tuple-element.16), channel_id=1, source_target_pairs={{0,2},{2,0},{4,6},{6,4},{8,10},{10,8},{12,14},{14,12},{1,3},{3,1},... | collective-permute-start | bytes 147464 | tf_op jit(solution)/shard_map/ppermute | solution.py:133
  27.5 4.8 %collective-permute-start.15 = (bf16[16,3072]{1,0:T(8,128)(2,1)S(1)}, bf16[16,3072]{1,0:T(8,128)(2,1)S(1)}, u32[]{:S(2)}, u32[]{:S(2)}) collective-permute-start(bf16[16,3072]{1,0:T(8,128)(2,1)S(1)} %pad_maximum_fusion.3), channel_id=1, source_target_pairs={{0,2},{2,0},{4,6},{6,4},{8,10},{10,8},{12,14},{14,12},{1,3},{3,1},... | collective-permute-start | bytes 294920 | tf_op jit(solution)/shard_map/ppermute | solution.py:133
  29.7 6.4 %collective-permute-start.11 = (bf16[8,3072]{1,0:T(8,128)(2,1)S(1)}, bf16[8,3072]{1,0:T(8,128)(2,1)S(1)}, u32[]{:S(2)}, u32[]{:S(2)}) collective-permute-start(bf16[8,3072]{1,0:T(8,128)(2,1)S(1)} %add_convert_fusion.5), channel_id=1, source_target_pairs={{0,12},{2,14},{4,8},{6,10},{8,4},{10,6},{12,0},{14,2},{1,13},{3,15... | collective-permute-start | bytes 147464 | tf_op jit(solution)/shard_map/ppermute | solution.py:130
  31.9 5.3 %collective-permute-start.13 = (bf16[8,3072]{1,0:T(8,128)(2,1)S(1)}, bf16[8,3072]{1,0:T(8,128)(2,1)S(1)}, u32[]{:S(2)}, u32[]{:S(2)}) collective-permute-start(bf16[8,3072]{1,0:T(8,128)(2,1)S(1)} %add_convert_fusion.4), channel_id=1, source_target_pairs={{0,8},{2,10},{4,12},{6,14},{8,0},{10,2},{12,4},{14,6},{1,9},{3,11}... | collective-permute-start | bytes 147464 | tf_op jit(solution)/shard_map/ppermute | solution.py:130
  32.3 4.9 %collective-permute-start.16 = (bf16[8,3072]{1,0:T(8,128)(2,1)S(1)}, bf16[8,3072]{1,0:T(8,128)(2,1)S(1)}, u32[]{:S(2)}, u32[]{:S(2)}) collective-permute-start(bf16[8,3072]{1,0:T(8,128)(2,1)S(1)} %get-tuple-element.45), channel_id=1, source_target_pairs={{0,4},{2,6},{4,0},{6,2},{8,12},{10,14},{12,8},{14,10},{1,5},{3,7},... | collective-permute-start | bytes 147464 | tf_op jit(solution)/shard_map/ppermute | solution.py:130

commit v7 on v6

--- a/solution.py
+++ b/solution.py
@@ -141,11 +141,12 @@
     sent = dict(zip(blocks, cut(outgoing)))
     here = {s: trade(sent[s], s) for s in steps}
     here[0] = sent[0]
+    arrival = [0, steps[-1]] + steps[:-1]
     there = {}
-    for group in [[0]] + [[s] for s in steps]:
-        there.update(zip(group, cut(swap(join([here[s] for s in group]), "expert"))))
-    order = [(side, s) for side in (0, 1) for s in [0] + steps]
-    names = [(side, s) for side in (here, there) for s in [0] + steps]
+    for s in arrival:
+        there[s] = swap(here[s], "expert")
+    order = [(side, s) for side in (0, 1) for s in arrival]
+    names = [(side, s) for side in (here, there) for s in arrival]
     pieces = [join([side[s] for side, s in names[:-1]]), join([side[s] for side, s in names[-1:]])]
     both = join(pieces)
     if tiles == 2:

time: 38.2 us -> 38 us (level)
  waiting for transfers between devices: 10.9 us -> 10 us
  starting transfers between devices: 19 us -> 19.6 us
    ppermute x11, waiting for transfers between devices: 7.21 us -> 5.12 us  [swap(): lax.ppermute(x, axis, [(i, i ^ 1) for i in range(lax.axis_size(axis))])]
    ppermute x6, waiting for transfers between devices: 3.71 us -> 4.91 us  [trade(): return lax.ppermute(x, 'expert', pairs)]
    ppermute x11, starting transfers between devices: 8.85 us -> 9.35 us  [swap(): lax.ppermute(x, axis, [(i, i ^ 1) for i in range(lax.axis_size(axis))])]
  transfers between devices with their start and end apart: 17 -> 17, of which waited for: 10 -> 9; matrix products, arithmetic and copies ran while one was open for 1% -> 1% of each run, Pallas kernels for 0% -> 0%
where the time goes in v7:
time: 38 us; the launch traced here: 37.8 us
  starting transfers between devices  19.6 us (52%)
  waiting for transfers between devices  10 us (26%)
  Pallas kernels  7.56 us (20%)
    ppermute x6, starting transfers between devices, trade(): return lax.ppermute(x, 'expert', pairs)  10.3 us
    ppermute x11, starting transfers between devices, swap(): lax.ppermute(x, axis, [(i, i ^ 1) for i in range(lax.axis_size(axis))])  9.35 us
    pallas_call x1, Pallas kernels, shards(): pl.pallas_call(functools.partial(ffn_kernel, block), out_shape=jax.ShapeD...  5.32 us
    ppermute x11, waiting for transfers between devices, swap(): lax.ppermute(x, axis, [(i, i ^ 1) for i in range(lax.axis_size(axis))])  5.12 us
    ppermute x6, waiting for transfers between devices, trade(): return lax.ppermute(x, 'expert', pairs)  4.91 us
    pallas_call x1, Pallas kernels, shards(): pl.pallas_call(functools.partial(route_kernel, blocks, capacity), out_sha...  1.26 us
    pallas_call x1, Pallas kernels, shards(): pl.pallas_call(combine_kernel, out_shape=jax.ShapeDtypeStruct((rows, widt...  0.84 us
  transfers between devices with their start and end apart: 17, of which 9 were waited for; matrix products, arithmetic and copies ran while one was open for 1% of the time, Pallas kernels for 0%

profile of v7, /device:TPU:0, one launch (start us, length us, event | category | flops | bytes accessed | tf_op | source)
XLA Modules:
  0.0 37.8 jit_solution(11929347210549727990)
XLA Ops:
  0.0 1.3 %route.1 = bf16[32,3072]{1,0:T(8,128)(2,1)S(1)} custom-call(s32[2,16]{1,0:T(2,128)} %bitcast.8, bf16[16,3072]{1,0:T(8,128)(2,1)} %tokens_hbm.1), custom_call_target="tpu_custom_call" | custom-call | flops 999999995904 | bytes 400000000 | tf_op jit(solution)/shard_map/route/pallas_call | solution.py:100
  1.3 3.1 %collective-permute-start = (bf16[8,3072]{1,0:T(8,128)(2,1)S(1)}, bf16[8,3072]{1,0:T(8,128)(2,1)S(1)}, u32[]{:S(2)}, u32[]{:S(2)}) collective-permute-start(bf16[8,3072]{1,0:T(8,128)(2,1)S(1)} %get-tuple-element.41), channel_id=1, source_target_pairs={{0,4},{2,6},{4,0},{6,2},{8,12},{10,14},{12,8},{14,10},{1,5},{3,7},... | collective-permute-start | bytes 147464 | tf_op jit(solution)/shard_map/ppermute | solution.py:130
  4.4 2.5 %collective-permute-start.1 = (bf16[8,3072]{1,0:T(8,128)(2,1)S(1)}, bf16[8,3072]{1,0:T(8,128)(2,1)S(1)}, u32[]{:S(2)}, u32[]{:S(2)}) collective-permute-start(bf16[8,3072]{1,0:T(8,128)(2,1)S(1)} %get-tuple-element.40), channel_id=1, source_target_pairs={{0,12},{2,14},{4,8},{6,10},{8,4},{10,6},{12,0},{14,2},{1,13},{3,15... | collective-permute-start | bytes 147464 | tf_op jit(solution)/shard_map/ppermute | solution.py:130
  7.0 1.5 %collective-permute-start.3 = (bf16[8,3072]{1,0:T(8,128)(2,1)S(1)}, bf16[8,3072]{1,0:T(8,128)(2,1)S(1)}, u32[]{:S(2)}, u32[]{:S(2)}) collective-permute-start(bf16[8,3072]{1,0:T(8,128)(2,1)S(1)} %get-tuple-element.42), channel_id=1, source_target_pairs={{0,2},{2,0},{4,6},{6,4},{8,10},{10,8},{12,14},{14,12},{1,3},{3,1},... | collective-permute-start | bytes 147464 | tf_op jit(solution)/shard_map/ppermute | solution.py:133
  8.5 0.5 %collective-permute-start.4 = (bf16[8,3072]{1,0:T(8,128)(2,1)S(1)}, bf16[8,3072]{1,0:T(8,128)(2,1)S(1)}, u32[]{:S(2)}, u32[]{:S(2)}) collective-permute-start(bf16[8,3072]{1,0:T(8,128)(2,1)S(1)} %collective-permute-done), channel_id=1, source_target_pairs={{0,2},{2,0},{4,6},{6,4},{8,10},{10,8},{12,14},{14,12},{1,3},{3,1},... | collective-permute-start | bytes 147464 | tf_op jit(solution)/shard_map/ppermute | solution.py:133
  9.0 1.9 %collective-permute-done.1 = bf16[8,3072]{1,0:T(8,128)(2,1)S(1)} collective-permute-done((bf16[8,3072]{1,0:T(8,128)(2,1)S(1)}, bf16[8,3072]{1,0:T(8,128)(2,1)S(1)}, u32[]{:S(2)}, u32[]{:S(2)}) %collective-permute-start.1) | collective-permute-done | bytes 49184 | tf_op jit(solution)/shard_map/ppermute | solution.py:130
  10.9 1.5 %collective-permute-start.5 = (bf16[8,3072]{1,0:T(8,128)(2,1)S(1)}, bf16[8,3072]{1,0:T(8,128)(2,1)S(1)}, u32[]{:S(2)}, u32[]{:S(2)}) collective-permute-start(bf16[8,3072]{1,0:T(8,128)(2,1)S(1)} %collective-permute-done.1), channel_id=1, source_target_pairs={{0,2},{2,0},{4,6},{6,4},{8,10},{10,8},{12,14},{14,12},{1,3},{3,1},... | collective-permute-start | bytes 147464 | tf_op jit(solution)/shard_map/ppermute | solution.py:133
  12.4 1.5 %collective-permute-start.6 = (bf16[8,3072]{1,0:T(8,128)(2,1)S(1)}, bf16[8,3072]{1,0:T(8,128)(2,1)S(1)}, u32[]{:S(2)}, u32[]{:S(2)}) collective-permute-start(bf16[8,3072]{1,0:T(8,128)(2,1)S(1)} %collective-permute-done.2), channel_id=1, source_target_pairs={{0,2},{2,0},{4,6},{6,4},{8,10},{10,8},{12,14},{14,12},{1,3},{3,1},... | collective-permute-start | bytes 147464 | tf_op jit(solution)/shard_map/ppermute | solution.py:133
  14.0 1.0 %collective-permute-done.5 = bf16[8,3072]{1,0:T(8,128)(2,1)S(1)} collective-permute-done((bf16[8,3072]{1,0:T(8,128)(2,1)S(1)}, bf16[8,3072]{1,0:T(8,128)(2,1)S(1)}, u32[]{:S(2)}, u32[]{:S(2)}) %collective-permute-start.5) | collective-permute-done | bytes 49184 | tf_op jit(solution)/shard_map/ppermute | solution.py:133
  15.1 1.4 %collective-permute-done.6 = bf16[8,3072]{1,0:T(8,128)(2,1)S(1)} collective-permute-done((bf16[8,3072]{1,0:T(8,128)(2,1)S(1)}, bf16[8,3072]{1,0:T(8,128)(2,1)S(1)}, u32[]{:S(2)}, u32[]{:S(2)}) %collective-permute-start.6) | collective-permute-done | bytes 49184 | tf_op jit(solution)/shard_map/ppermute | solution.py:133
  16.8 1.0 %collective-permute-done.8 = bf16[8,3072]{1,0:T(8,128)(2,1)S(1)} collective-permute-done((bf16[8,3072]{1,0:T(8,128)(2,1)S(1)}, bf16[8,3072]{1,0:T(8,128)(2,1)S(1)}, u32[]{:S(2)}, u32[]{:S(2)}) %collective-permute-start.8) | collective-permute-done | bytes 49184 | tf_op jit(solution)/shard_map/ppermute | solution.py:133
  17.8 5.3 %ffn.1 = bf16[128,3072]{1,0:T(8,128)(2,1)S(1)} custom-call(bf16[128,3072]{1,0:T(8,128)(2,1)S(1)} %constant_dynamic-update-slice_fusion.7.rows_ref, bf16[3072,2048]{1,0:T(8,128)(2,1)S(1)} %bitcast.5, bf16[3072,2048]{1,0:T(8,128)(2,1)S(1)} %bitcast.6, bf16[2048,3072]{1,0:T(8,128)(2,1)S(1)} %bitcast.7), custom_call_target="tpu_custom_call" | custom-call | flops 4831838208 | bytes 37748736 | tf_op jit(solution)/shard_map/ffn/pallas_call | solution.py:159
  23.4 0.4 %collective-permute-start.14 = (bf16[32,3072]{1,0:T(8,128)(2,1)S(1)}, bf16[32,3072]{1,0:T(8,128)(2,1)S(1)}, u32[]{:S(2)}, u32[]{:S(2)}) collective-permute-start(bf16[32,3072]{1,0:T(8,128)(2,1)S(1)} %pad_maximum_fusion.1), channel_id=1, source_target_pairs={{0,1},{1,0},{2,3},{3,2},{4,5},{5,4},{6,7},{7,6},{8,9},{9,8},{10,11... | collective-permute-start | bytes 589832 | tf_op jit(solution)/shard_map/ppermute | solution.py:133
  23.8 0.8 %collective-permute-done.9 = bf16[32,3072]{1,0:T(8,128)(2,1)S(1)} collective-permute-done((bf16[32,3072]{1,0:T(8,128)(2,1)S(1)}, bf16[32,3072]{1,0:T(8,128)(2,1)S(1)}, u32[]{:S(2)}, u32[]{:S(2)}) %collective-permute-start.9) | collective-permute-done | bytes 196640 | tf_op jit(solution)/shard_map/ppermute | solution.py:133
  24.8 1.5 %collective-permute-start.10 = (bf16[8,3072]{1,0:T(8,128)(2,1)S(1)}, bf16[8,3072]{1,0:T(8,128)(2,1)S(1)}, u32[]{:S(2)}, u32[]{:S(2)}) collective-permute-start(bf16[8,3072]{1,0:T(8,128)(2,1)S(1)} %get-tuple-element.14), channel_id=1, source_target_pairs={{0,2},{2,0},{4,6},{6,4},{8,10},{10,8},{12,14},{14,12},{1,3},{3,1},... | collective-permute-start | bytes 147464 | tf_op jit(solution)/shard_map/ppermute | solution.py:133
  26.3 0.5 %collective-permute-start.12 = (bf16[8,3072]{1,0:T(8,128)(2,1)S(1)}, bf16[8,3072]{1,0:T(8,128)(2,1)S(1)}, u32[]{:S(2)}, u32[]{:S(2)}) collective-permute-start(bf16[8,3072]{1,0:T(8,128)(2,1)S(1)} %get-tuple-element.16), channel_id=1, source_target_pairs={{0,2},{2,0},{4,6},{6,4},{8,10},{10,8},{12,14},{14,12},{1,3},{3,1},... | collective-permute-start | bytes 147464 | tf_op jit(solution)/shard_map/ppermute | solution.py:133
  27.0 1.5 %collective-permute-start.15 = (bf16[16,3072]{1,0:T(8,128)(2,1)S(1)}, bf16[16,3072]{1,0:T(8,128)(2,1)S(1)}, u32[]{:S(2)}, u32[]{:S(2)}) collective-permute-start(bf16[16,3072]{1,0:T(8,128)(2,1)S(1)} %pad_maximum_fusion.3), channel_id=1, source_target_pairs={{0,2},{2,0},{4,6},{6,4},{8,10},{10,8},{12,14},{14,12},{1,3},{3,1},... | collective-permute-start | bytes 294920 | tf_op jit(solution)/shard_map/ppermute | solution.py:133
  28.5 0.6 %collective-permute-done.10 = bf16[8,3072]{1,0:T(8,128)(2,1)S(1)} collective-permute-done((bf16[8,3072]{1,0:T(8,128)(2,1)S(1)}, bf16[8,3072]{1,0:T(8,128)(2,1)S(1)}, u32[]{:S(2)}, u32[]{:S(2)}) %collective-permute-start.10) | collective-permute-done | bytes 49184 | tf_op jit(solution)/shard_map/ppermute | solution.py:133
  29.2 2.2 %collective-permute-start.11 = (bf16[8,3072]{1,0:T(8,128)(2,1)S(1)}, bf16[8,3072]{1,0:T(8,128)(2,1)S(1)}, u32[]{:S(2)}, u32[]{:S(2)}) collective-permute-start(bf16[8,3072]{1,0:T(8,128)(2,1)S(1)} %add_convert_fusion.5), channel_id=1, source_target_pairs={{0,12},{2,14},{4,8},{6,10},{8,4},{10,6},{12,0},{14,2},{1,13},{3,15... | collective-permute-start | bytes 147464 | tf_op jit(solution)/shard_map/ppermute | solution.py:130
  31.3 1.1 %collective-permute-start.13 = (bf16[8,3072]{1,0:T(8,128)(2,1)S(1)}, bf16[8,3072]{1,0:T(8,128)(2,1)S(1)}, u32[]{:S(2)}, u32[]{:S(2)}) collective-permute-start(bf16[8,3072]{1,0:T(8,128)(2,1)S(1)} %add_convert_fusion.4), channel_id=1, source_target_pairs={{0,8},{2,10},{4,12},{6,14},{8,0},{10,2},{12,4},{14,6},{1,9},{3,11}... | collective-permute-start | bytes 147464 | tf_op jit(solution)/shard_map/ppermute | solution.py:130
  32.5 1.3 %collective-permute-start.16 = (bf16[8,3072]{1,0:T(8,128)(2,1)S(1)}, bf16[8,3072]{1,0:T(8,128)(2,1)S(1)}, u32[]{:S(2)}, u32[]{:S(2)}) collective-permute-start(bf16[8,3072]{1,0:T(8,128)(2,1)S(1)} %get-tuple-element.43), channel_id=1, source_target_pairs={{0,4},{2,6},{4,0},{6,2},{8,12},{10,14},{12,8},{14,10},{1,5},{3,7},... | collective-permute-start | bytes 147464 | tf_op jit(solution)/shard_map/ppermute | solution.py:130
  33.9 1.2 %collective-permute-done.11 = bf16[8,3072]{1,0:T(8,128)(2,1)S(1)} collective-permute-done((bf16[8,3072]{1,0:T(8,128)(2,1)S(1)}, bf16[8,3072]{1,0:T(8,128)(2,1)S(1)}, u32[]{:S(2)}, u32[]{:S(2)}) %collective-permute-start.11) | collective-permute-done | bytes 49184 | tf_op jit(solution)/shard_map/ppermute | solution.py:130
  35.2 1.8 %collective-permute-done.13 = bf16[8,3072]{1,0:T(8,128)(2,1)S(1)} collective-permute-done((bf16[8,3072]{1,0:T(8,128)(2,1)S(1)}, bf16[8,3072]{1,0:T(8,128)(2,1)S(1)}, u32[]{:S(2)}, u32[]{:S(2)}) %collective-permute-start.13) | collective-permute-done | bytes 49184 | tf_op jit(solution)/shard_map/ppermute | solution.py:130
  37.0 0.8 %combine.1 = bf16[16,3072]{1,0:T(8,128)(2,1)} custom-call(bf16[32,16]{1,0:T(8,128)(2,1)S(1)} %weigh.1.comb_ref, bf16[32,3072]{1,0:T(8,128)(2,1)S(1)} %pad_maximum_fusion.2.results_ref), custom_call_target="tpu_custom_call" | custom-call | tf_op jit(solution)/shard_map/combine/pallas_call | solution.py:195
  (46 shorter events, 1.2 us)
Async XLA Ops:
  0.0 17.7 %copy-start = (bf16[1,3072,2048]{2,1,0:T(8,128)(2,1)S(1)}, bf16[1,3072,2048]{2,1,0:T(8,128)(2,1)}, u32[]{:S(2)}) copy-start(bf16[1,3072,2048]{2,1,0:T(8,128)(2,1)} %param.9) | copy-start | bytes 37748740
  0.0 17.7 %copy-start.1 = (bf16[1,3072,2048]{2,1,0:T(8,128)(2,1)S(1)}, bf16[1,3072,2048]{2,1,0:T(8,128)(2,1)}, u32[]{:S(2)}) copy-start(bf16[1,3072,2048]{2,1,0:T(8,128)(2,1)} %param.10) | copy-start | bytes 37748740
  0.0 17.7 %copy-start.2 = (bf16[1,2048,3072]{2,1,0:T(8,128)(2,1)S(1)}, bf16[1,2048,3072]{2,1,0:T(8,128)(2,1)}, u32[]{:S(2)}) copy-start(bf16[1,2048,3072]{2,1,0:T(8,128)(2,1)} %param.11) | copy-start | bytes 37748740
  1.3 7.2 %collective-permute-start = (bf16[8,3072]{1,0:T(8,128)(2,1)S(1)}, bf16[8,3072]{1,0:T(8,128)(2,1)S(1)}, u32[]{:S(2)}, u32[]{:S(2)}) collective-permute-start(bf16[8,3072]{1,0:T(8,128)(2,1)S(1)} %get-tuple-element.41), channel_id=1, source_target_pairs={{0,4},{2,6},{4,0},{6,2},{8,12},{10,14},{12,8},{14,10},{1,5},{3,7},... | collective-permute-start | bytes 147464 | tf_op jit(solution)/shard_map/ppermute | solution.py:130
  4.4 6.5 %collective-permute-start.1 = (bf16[8,3072]{1,0:T(8,128)(2,1)S(1)}, bf16[8,3072]{1,0:T(8,128)(2,1)S(1)}, u32[]{:S(2)}, u32[]{:S(2)}) collective-permute-start(bf16[8,3072]{1,0:T(8,128)(2,1)S(1)} %get-tuple-element.40), channel_id=1, source_target_pairs={{0,12},{2,14},{4,8},{6,10},{8,4},{10,6},{12,0},{14,2},{1,13},{3,15... | collective-permute-start | bytes 147464 | tf_op jit(solution)/shard_map/ppermute | solution.py:130
  6.9 5.5 %collective-permute-start.2 = (bf16[8,3072]{1,0:T(8,128)(2,1)S(1)}, bf16[8,3072]{1,0:T(8,128)(2,1)S(1)}, u32[]{:S(2)}, u32[]{:S(2)}) collective-permute-start(bf16[8,3072]{1,0:T(8,128)(2,1)S(1)} %get-tuple-element.39), channel_id=1, source_target_pairs={{0,8},{2,10},{4,12},{6,14},{8,0},{10,2},{12,4},{14,6},{1,9},{3,11}... | collective-permute-start | bytes 147464 | tf_op jit(solution)/shard_map/ppermute | solution.py:130
  7.0 6.9 %collective-permute-start.3 = (bf16[8,3072]{1,0:T(8,128)(2,1)S(1)}, bf16[8,3072]{1,0:T(8,128)(2,1)S(1)}, u32[]{:S(2)}, u32[]{:S(2)}) collective-permute-start(bf16[8,3072]{1,0:T(8,128)(2,1)S(1)} %get-tuple-element.42), channel_id=1, source_target_pairs={{0,2},{2,0},{4,6},{6,4},{8,10},{10,8},{12,14},{14,12},{1,3},{3,1},... | collective-permute-start | bytes 147464 | tf_op jit(solution)/shard_map/ppermute | solution.py:133
  8.5 5.5 %collective-permute-start.4 = (bf16[8,3072]{1,0:T(8,128)(2,1)S(1)}, bf16[8,3072]{1,0:T(8,128)(2,1)S(1)}, u32[]{:S(2)}, u32[]{:S(2)}) collective-permute-start(bf16[8,3072]{1,0:T(8,128)(2,1)S(1)} %collective-permute-done), channel_id=1, source_target_pairs={{0,2},{2,0},{4,6},{6,4},{8,10},{10,8},{12,14},{14,12},{1,3},{3,1},... | collective-permute-start | bytes 147464 | tf_op jit(solution)/shard_map/ppermute | solution.py:133
  10.9 4.1 %collective-permute-start.5 = (bf16[8,3072]{1,0:T(8,128)(2,1)S(1)}, bf16[8,3072]{1,0:T(8,128)(2,1)S(1)}, u32[]{:S(2)}, u32[]{:S(2)}) collective-permute-start(bf16[8,3072]{1,0:T(8,128)(2,1)S(1)} %collective-permute-done.1), channel_id=1, source_target_pairs={{0,2},{2,0},{4,6},{6,4},{8,10},{10,8},{12,14},{14,12},{1,3},{3,1},... | collective-permute-start | bytes 147464 | tf_op jit(solution)/shard_map/ppermute | solution.py:133
  12.4 4.1 %collective-permute-start.6 = (bf16[8,3072]{1,0:T(8,128)(2,1)S(1)}, bf16[8,3072]{1,0:T(8,128)(2,1)S(1)}, u32[]{:S(2)}, u32[]{:S(2)}) collective-permute-start(bf16[8,3072]{1,0:T(8,128)(2,1)S(1)} %collective-permute-done.2), channel_id=1, source_target_pairs={{0,2},{2,0},{4,6},{6,4},{8,10},{10,8},{12,14},{14,12},{1,3},{3,1},... | collective-permute-start | bytes 147464 | tf_op jit(solution)/shard_map/ppermute | solution.py:133
  15.0 1.7 %collective-permute-start.7 = (bf16[56,3072]{1,0:T(8,128)(2,1)S(1)}, bf16[56,3072]{1,0:T(8,128)(2,1)S(1)}, u32[]{:S(2)}, u32[]{:S(2)}) collective-permute-start(bf16[56,3072]{1,0:T(8,128)(2,1)S(1)} %get-tuple-element.45), channel_id=1, source_target_pairs={{0,1},{1,0},{2,3},{3,2},{4,5},{5,4},{6,7},{7,6},{8,9},{9,8},{10,11... | collective-permute-start | bytes 1032200 | tf_op jit(solution)/shard_map/ppermute | solution.py:133
  16.5 1.2 %collective-permute-start.8 = (bf16[8,3072]{1,0:T(8,128)(2,1)S(1)}, bf16[8,3072]{1,0:T(8,128)(2,1)S(1)}, u32[]{:S(2)}, u32[]{:S(2)}) collective-permute-start(bf16[8,3072]{1,0:T(8,128)(2,1)S(1)} %collective-permute-done.6), channel_id=1, source_target_pairs={{0,1},{1,0},{2,3},{3,2},{4,5},{5,4},{6,7},{7,6},{8,9},{9,8},{10,11... | collective-permute-start | bytes 147464 | tf_op jit(solution)/shard_map/ppermute | solution.py:133
  17.7 16.1 %copy-start.3 = (s32[16,2]{0,1:T(2,128)S(1)}, s32[16,2]{0,1:T(2,128)}, u32[]{:S(2)}) copy-start(s32[16,2]{0,1:T(2,128)} %param.7) | copy-start | bytes 388
  17.8 16.1 %copy-start.4 = (bf16[16,2]{0,1:T(2,128)(2,1)S(1)}, bf16[16,2]{0,1:T(2,128)(2,1)}, u32[]{:S(2)}) copy-start(bf16[16,2]{0,1:T(2,128)(2,1)} %param.8) | copy-start | bytes 196
  23.2 1.5 %collective-permute-start.9 = (bf16[32,3072]{1,0:T(8,128)(2,1)S(1)}, bf16[32,3072]{1,0:T(8,128)(2,1)S(1)}, u32[]{:S(2)}, u32[]{:S(2)}) collective-permute-start(bf16[32,3072]{1,0:T(8,128)(2,1)S(1)} %pad_maximum_fusion), channel_id=1, source_target_pairs={{0,1},{1,0},{2,3},{3,2},{4,5},{5,4},{6,7},{7,6},{8,9},{9,8},{10,11... | collective-permute-start | bytes 589832 | tf_op jit(solution)/shard_map/ppermute | solution.py:133
  23.4 3.4 %collective-permute-start.14 = (bf16[32,3072]{1,0:T(8,128)(2,1)S(1)}, bf16[32,3072]{1,0:T(8,128)(2,1)S(1)}, u32[]{:S(2)}, u32[]{:S(2)}) collective-permute-start(bf16[32,3072]{1,0:T(8,128)(2,1)S(1)} %pad_maximum_fusion.1), channel_id=1, source_target_pairs={{0,1},{1,0},{2,3},{3,2},{4,5},{5,4},{6,7},{7,6},{8,9},{9,8},{10,11... | collective-permute-start | bytes 589832 | tf_op jit(solution)/shard_map/ppermute | solution.py:133
  24.8 4.4 %collective-permute-start.10 = (bf16[8,3072]{1,0:T(8,128)(2,1)S(1)}, bf16[8,3072]{1,0:T(8,128)(2,1)S(1)}, u32[]{:S(2)}, u32[]{:S(2)}) collective-permute-start(bf16[8,3072]{1,0:T(8,128)(2,1)S(1)} %get-tuple-element.14), channel_id=1, source_target_pairs={{0,2},{2,0},{4,6},{6,4},{8,10},{10,8},{12,14},{14,12},{1,3},{3,1},... | collective-permute-start | bytes 147464 | tf_op jit(solution)/shard_map/ppermute | solution.py:133
  26.3 5.0 %collective-permute-start.12 = (bf16[8,3072]{1,0:T(8,128)(2,1)S(1)}, bf16[8,3072]{1,0:T(8,128)(2,1)S(1)}, u32[]{:S(2)}, u32[]{:S(2)}) collective-permute-start(bf16[8,3072]{1,0:T(8,128)(2,1)S(1)} %get-tuple-element.16), channel_id=1, source_target_pairs={{0,2},{2,0},{4,6},{6,4},{8,10},{10,8},{12,14},{14,12},{1,3},{3,1},... | collective-permute-start | bytes 147464 | tf_op jit(solution)/shard_map/ppermute | solution.py:133
  27.0 5.5 %collective-permute-start.15 = (bf16[16,3072]{1,0:T(8,128)(2,1)S(1)}, bf16[16,3072]{1,0:T(8,128)(2,1)S(1)}, u32[]{:S(2)}, u32[]{:S(2)}) collective-permute-start(bf16[16,3072]{1,0:T(8,128)(2,1)S(1)} %pad_maximum_fusion.3), channel_id=1, source_target_pairs={{0,2},{2,0},{4,6},{6,4},{8,10},{10,8},{12,14},{14,12},{1,3},{3,1},... | collective-permute-start | bytes 294920 | tf_op jit(solution)/shard_map/ppermute | solution.py:133
  29.2 6.0 %collective-permute-start.11 = (bf16[8,3072]{1,0:T(8,128)(2,1)S(1)}, bf16[8,3072]{1,0:T(8,128)(2,1)S(1)}, u32[]{:S(2)}, u32[]{:S(2)}) collective-permute-start(bf16[8,3072]{1,0:T(8,128)(2,1)S(1)} %add_convert_fusion.5), channel_id=1, source_target_pairs={{0,12},{2,14},{4,8},{6,10},{8,4},{10,6},{12,0},{14,2},{1,13},{3,15... | collective-permute-start | bytes 147464 | tf_op jit(solution)/shard_map/ppermute | solution.py:130
  31.3 5.6 %collective-permute-start.13 = (bf16[8,3072]{1,0:T(8,128)(2,1)S(1)}, bf16[8,3072]{1,0:T(8,128)(2,1)S(1)}, u32[]{:S(2)}, u32[]{:S(2)}) collective-permute-start(bf16[8,3072]{1,0:T(8,128)(2,1)S(1)} %add_convert_fusion.4), channel_id=1, source_target_pairs={{0,8},{2,10},{4,12},{6,14},{8,0},{10,2},{12,4},{14,6},{1,9},{3,11}... | collective-permute-start | bytes 147464 | tf_op jit(solution)/shard_map/ppermute | solution.py:130
  32.5 4.5 %collective-permute-start.16 = (bf16[8,3072]{1,0:T(8,128)(2,1)S(1)}, bf16[8,3072]{1,0:T(8,128)(2,1)S(1)}, u32[]{:S(2)}, u32[]{:S(2)}) collective-permute-start(bf16[8,3072]{1,0:T(8,128)(2,1)S(1)} %get-tuple-element.43), channel_id=1, source_target_pairs={{0,4},{2,6},{4,0},{6,2},{8,12},{10,14},{12,8},{14,10},{1,5},{3,7},... | collective-permute-start | bytes 147464 | tf_op jit(solution)/shard_map/ppermute | solution.py:130

commit v8 on v7

--- a/solution.py
+++ b/solution.py
@@ -186,7 +186,7 @@
         both = jnp.sum(pieces.astype(F32), axis=0).astype(BF16)
         summed = dict(zip(order, lax.optimization_barrier(cut(both))))
     results = {}
-    for group in [[s] for s in steps[:-1]] + [[steps[-1], 0]]:
+    for group in [[s] for s in blocks]:
         back = swap(join([summed[1, s] for s in group]), "expert")
         for s, block in zip(group, cut(back)):
             total = add(summed[0, s], block)

time: 38 us -> 38 us (level)
  starting transfers between devices: 19.6 us -> 20.2 us
  waiting for transfers between devices: 10 us -> 9.48 us
    ppermute x11 -> x12, waiting for transfers between devices: 5.12 us -> 4.43 us  [swap(): lax.ppermute(x, axis, [(i, i ^ 1) for i in range(lax.axis_size(axis))])]
    ppermute x11 -> x12, starting transfers between devices: 9.35 us -> 9.9 us  [swap(): lax.ppermute(x, axis, [(i, i ^ 1) for i in range(lax.axis_size(axis))])]
  transfers between devices with their start and end apart: 17 -> 18, of which waited for: 9 -> 9; matrix products, arithmetic and copies ran while one was open for 1% -> 1% of each run, Pallas kernels for 0% -> 0%
where the time goes in v8:
time: 38 us; the launch traced here: 37.8 us
  starting transfers between devices  20.2 us (53%)
  waiting for transfers between devices  9.48 us (25%)
  Pallas kernels  7.56 us (20%)
    ppermute x6, starting transfers between devices, trade(): return lax.ppermute(x, 'expert', pairs)  10.3 us
    ppermute x12, starting transfers between devices, swap(): lax.ppermute(x, axis, [(i, i ^ 1) for i in range(lax.axis_size(axis))])  9.9 us
    pallas_call x1, Pallas kernels, shards(): pl.pallas_call(functools.partial(ffn_kernel, block), out_shape=jax.ShapeD...  5.32 us
    ppermute x6, waiting for transfers between devices, trade(): return lax.ppermute(x, 'expert', pairs)  5.05 us
    ppermute x12, waiting for transfers between devices, swap(): lax.ppermute(x, axis, [(i, i ^ 1) for i in range(lax.axis_size(axis))])  4.43 us
    pallas_call x1, Pallas kernels, shards(): pl.pallas_call(functools.partial(route_kernel, blocks, capacity), out_sha...  1.25 us
    pallas_call x1, Pallas kernels, shards(): pl.pallas_call(combine_kernel, out_shape=jax.ShapeDtypeStruct((rows, widt...  0.84 us
  transfers between devices with their start and end apart: 18, of which 9 were waited for; matrix products, arithmetic and copies ran while one was open for 1% of the time, Pallas kernels for 0%

profile of v8, /device:TPU:0, one launch (start us, length us, event | category | flops | bytes accessed | tf_op | source)
XLA Modules:
  0.0 37.8 jit_solution(818163111746729563)
XLA Ops:
  0.0 1.3 %route.1 = bf16[32,3072]{1,0:T(8,128)(2,1)S(1)} custom-call(s32[2,16]{1,0:T(2,128)} %bitcast.8, bf16[16,3072]{1,0:T(8,128)(2,1)} %tokens_hbm.1), custom_call_target="tpu_custom_call" | custom-call | flops 999999995904 | bytes 400000000 | tf_op jit(solution)/shard_map/route/pallas_call | solution.py:100
  1.3 3.1 %collective-permute-start = (bf16[8,3072]{1,0:T(8,128)(2,1)S(1)}, bf16[8,3072]{1,0:T(8,128)(2,1)S(1)}, u32[]{:S(2)}, u32[]{:S(2)}) collective-permute-start(bf16[8,3072]{1,0:T(8,128)(2,1)S(1)} %get-tuple-element.41), channel_id=1, source_target_pairs={{0,4},{2,6},{4,0},{6,2},{8,12},{10,14},{12,8},{14,10},{1,5},{3,7},... | collective-permute-start | bytes 147464 | tf_op jit(solution)/shard_map/ppermute | solution.py:130
  4.4 2.5 %collective-permute-start.1 = (bf16[8,3072]{1,0:T(8,128)(2,1)S(1)}, bf16[8,3072]{1,0:T(8,128)(2,1)S(1)}, u32[]{:S(2)}, u32[]{:S(2)}) collective-permute-start(bf16[8,3072]{1,0:T(8,128)(2,1)S(1)} %get-tuple-element.40), channel_id=1, source_target_pairs={{0,12},{2,14},{4,8},{6,10},{8,4},{10,6},{12,0},{14,2},{1,13},{3,15... | collective-permute-start | bytes 147464 | tf_op jit(solution)/shard_map/ppermute | solution.py:130
  7.0 1.5 %collective-permute-start.3 = (bf16[8,3072]{1,0:T(8,128)(2,1)S(1)}, bf16[8,3072]{1,0:T(8,128)(2,1)S(1)}, u32[]{:S(2)}, u32[]{:S(2)}) collective-permute-start(bf16[8,3072]{1,0:T(8,128)(2,1)S(1)} %get-tuple-element.42), channel_id=1, source_target_pairs={{0,2},{2,0},{4,6},{6,4},{8,10},{10,8},{12,14},{14,12},{1,3},{3,1},... | collective-permute-start | bytes 147464 | tf_op jit(solution)/shard_map/ppermute | solution.py:133
  8.5 0.5 %collective-permute-start.4 = (bf16[8,3072]{1,0:T(8,128)(2,1)S(1)}, bf16[8,3072]{1,0:T(8,128)(2,1)S(1)}, u32[]{:S(2)}, u32[]{:S(2)}) collective-permute-start(bf16[8,3072]{1,0:T(8,128)(2,1)S(1)} %collective-permute-done), channel_id=1, source_target_pairs={{0,2},{2,0},{4,6},{6,4},{8,10},{10,8},{12,14},{14,12},{1,3},{3,1},... | collective-permute-start | bytes 147464 | tf_op jit(solution)/shard_map/ppermute | solution.py:133
  9.0 1.9 %collective-permute-done.1 = bf16[8,3072]{1,0:T(8,128)(2,1)S(1)} collective-permute-done((bf16[8,3072]{1,0:T(8,128)(2,1)S(1)}, bf16[8,3072]{1,0:T(8,128)(2,1)S(1)}, u32[]{:S(2)}, u32[]{:S(2)}) %collective-permute-start.1) | collective-permute-done | bytes 49184 | tf_op jit(solution)/shard_map/ppermute | solution.py:130
  10.9 1.5 %collective-permute-start.5 = (bf16[8,3072]{1,0:T(8,128)(2,1)S(1)}, bf16[8,3072]{1,0:T(8,128)(2,1)S(1)}, u32[]{:S(2)}, u32[]{:S(2)}) collective-permute-start(bf16[8,3072]{1,0:T(8,128)(2,1)S(1)} %collective-permute-done.1), channel_id=1, source_target_pairs={{0,2},{2,0},{4,6},{6,4},{8,10},{10,8},{12,14},{14,12},{1,3},{3,1},... | collective-permute-start | bytes 147464 | tf_op jit(solution)/shard_map/ppermute | solution.py:133
  12.4 1.5 %collective-permute-start.6 = (bf16[8,3072]{1,0:T(8,128)(2,1)S(1)}, bf16[8,3072]{1,0:T(8,128)(2,1)S(1)}, u32[]{:S(2)}, u32[]{:S(2)}) collective-permute-start(bf16[8,3072]{1,0:T(8,128)(2,1)S(1)} %collective-permute-done.2), channel_id=1, source_target_pairs={{0,2},{2,0},{4,6},{6,4},{8,10},{10,8},{12,14},{14,12},{1,3},{3,1},... | collective-permute-start | bytes 147464 | tf_op jit(solution)/shard_map/ppermute | solution.py:133
  14.0 1.0 %collective-permute-done.5 = bf16[8,3072]{1,0:T(8,128)(2,1)S(1)} collective-permute-done((bf16[8,3072]{1,0:T(8,128)(2,1)S(1)}, bf16[8,3072]{1,0:T(8,128)(2,1)S(1)}, u32[]{:S(2)}, u32[]{:S(2)}) %collective-permute-start.5) | collective-permute-done | bytes 49184 | tf_op jit(solution)/shard_map/ppermute | solution.py:133
  15.3 1.2 %collective-permute-done.6 = bf16[8,3072]{1,0:T(8,128)(2,1)S(1)} collective-permute-done((bf16[8,3072]{1,0:T(8,128)(2,1)S(1)}, bf16[8,3072]{1,0:T(8,128)(2,1)S(1)}, u32[]{:S(2)}, u32[]{:S(2)}) %collective-permute-start.6) | collective-permute-done | bytes 49184 | tf_op jit(solution)/shard_map/ppermute | solution.py:133
  16.8 1.0 %collective-permute-done.8 = bf16[8,3072]{1,0:T(8,128)(2,1)S(1)} collective-permute-done((bf16[8,3072]{1,0:T(8,128)(2,1)S(1)}, bf16[8,3072]{1,0:T(8,128)(2,1)S(1)}, u32[]{:S(2)}, u32[]{:S(2)}) %collective-permute-start.8) | collective-permute-done | bytes 49184 | tf_op jit(solution)/shard_map/ppermute | solution.py:133
  17.8 5.3 %ffn.1 = bf16[128,3072]{1,0:T(8,128)(2,1)S(1)} custom-call(bf16[128,3072]{1,0:T(8,128)(2,1)S(1)} %constant_dynamic-update-slice_fusion.7.rows_ref, bf16[3072,2048]{1,0:T(8,128)(2,1)S(1)} %bitcast.5, bf16[3072,2048]{1,0:T(8,128)(2,1)S(1)} %bitcast.6, bf16[2048,3072]{1,0:T(8,128)(2,1)S(1)} %bitcast.7), custom_call_target="tpu_custom_call" | custom-call | flops 4831838208 | bytes 37748736 | tf_op jit(solution)/shard_map/ffn/pallas_call | solution.py:159
  23.4 0.4 %collective-permute-start.14 = (bf16[32,3072]{1,0:T(8,128)(2,1)S(1)}, bf16[32,3072]{1,0:T(8,128)(2,1)S(1)}, u32[]{:S(2)}, u32[]{:S(2)}) collective-permute-start(bf16[32,3072]{1,0:T(8,128)(2,1)S(1)} %pad_maximum_fusion.1), channel_id=1, source_target_pairs={{0,1},{1,0},{2,3},{3,2},{4,5},{5,4},{6,7},{7,6},{8,9},{9,8},{10,11... | collective-permute-start | bytes 589832 | tf_op jit(solution)/shard_map/ppermute | solution.py:133
  23.8 0.8 %collective-permute-done.9 = bf16[32,3072]{1,0:T(8,128)(2,1)S(1)} collective-permute-done((bf16[32,3072]{1,0:T(8,128)(2,1)S(1)}, bf16[32,3072]{1,0:T(8,128)(2,1)S(1)}, u32[]{:S(2)}, u32[]{:S(2)}) %collective-permute-start.9) | collective-permute-done | bytes 196640 | tf_op jit(solution)/shard_map/ppermute | solution.py:133
  24.8 1.5 %collective-permute-start.10 = (bf16[8,3072]{1,0:T(8,128)(2,1)S(1)}, bf16[8,3072]{1,0:T(8,128)(2,1)S(1)}, u32[]{:S(2)}, u32[]{:S(2)}) collective-permute-start(bf16[8,3072]{1,0:T(8,128)(2,1)S(1)} %get-tuple-element.14), channel_id=1, source_target_pairs={{0,2},{2,0},{4,6},{6,4},{8,10},{10,8},{12,14},{14,12},{1,3},{3,1},... | collective-permute-start | bytes 147464 | tf_op jit(solution)/shard_map/ppermute | solution.py:133
  26.3 0.5 %collective-permute-start.12 = (bf16[8,3072]{1,0:T(8,128)(2,1)S(1)}, bf16[8,3072]{1,0:T(8,128)(2,1)S(1)}, u32[]{:S(2)}, u32[]{:S(2)}) collective-permute-start(bf16[8,3072]{1,0:T(8,128)(2,1)S(1)} %get-tuple-element.16), channel_id=1, source_target_pairs={{0,2},{2,0},{4,6},{6,4},{8,10},{10,8},{12,14},{14,12},{1,3},{3,1},... | collective-permute-start | bytes 147464 | tf_op jit(solution)/shard_map/ppermute | solution.py:133
  26.9 1.5 %collective-permute-start.15 = (bf16[8,3072]{1,0:T(8,128)(2,1)S(1)}, bf16[8,3072]{1,0:T(8,128)(2,1)S(1)}, u32[]{:S(2)}, u32[]{:S(2)}) collective-permute-start(bf16[8,3072]{1,0:T(8,128)(2,1)S(1)} %get-tuple-element.18), channel_id=1, source_target_pairs={{0,2},{2,0},{4,6},{6,4},{8,10},{10,8},{12,14},{14,12},{1,3},{3,1},... | collective-permute-start | bytes 147464 | tf_op jit(solution)/shard_map/ppermute | solution.py:133
  28.5 0.5 %collective-permute-start.17 = (bf16[8,3072]{1,0:T(8,128)(2,1)S(1)}, bf16[8,3072]{1,0:T(8,128)(2,1)S(1)}, u32[]{:S(2)}, u32[]{:S(2)}) collective-permute-start(bf16[8,3072]{1,0:T(8,128)(2,1)S(1)} %get-tuple-element.20), channel_id=1, source_target_pairs={{0,2},{2,0},{4,6},{6,4},{8,10},{10,8},{12,14},{14,12},{1,3},{3,1},... | collective-permute-start | bytes 147464 | tf_op jit(solution)/shard_map/ppermute | solution.py:133
  29.2 2.1 %collective-permute-start.11 = (bf16[8,3072]{1,0:T(8,128)(2,1)S(1)}, bf16[8,3072]{1,0:T(8,128)(2,1)S(1)}, u32[]{:S(2)}, u32[]{:S(2)}) collective-permute-start(bf16[8,3072]{1,0:T(8,128)(2,1)S(1)} %add_convert_fusion.5), channel_id=1, source_target_pairs={{0,12},{2,14},{4,8},{6,10},{8,4},{10,6},{12,0},{14,2},{1,13},{3,15... | collective-permute-start | bytes 147464 | tf_op jit(solution)/shard_map/ppermute | solution.py:130
  31.3 1.1 %collective-permute-start.13 = (bf16[8,3072]{1,0:T(8,128)(2,1)S(1)}, bf16[8,3072]{1,0:T(8,128)(2,1)S(1)}, u32[]{:S(2)}, u32[]{:S(2)}) collective-permute-start(bf16[8,3072]{1,0:T(8,128)(2,1)S(1)} %add_convert_fusion.4), channel_id=1, source_target_pairs={{0,8},{2,10},{4,12},{6,14},{8,0},{10,2},{12,4},{14,6},{1,9},{3,11}... | collective-permute-start | bytes 147464 | tf_op jit(solution)/shard_map/ppermute | solution.py:130
  32.5 1.3 %collective-permute-start.16 = (bf16[8,3072]{1,0:T(8,128)(2,1)S(1)}, bf16[8,3072]{1,0:T(8,128)(2,1)S(1)}, u32[]{:S(2)}, u32[]{:S(2)}) collective-permute-start(bf16[8,3072]{1,0:T(8,128)(2,1)S(1)} %add_convert_fusion.3), channel_id=1, source_target_pairs={{0,4},{2,6},{4,0},{6,2},{8,12},{10,14},{12,8},{14,10},{1,5},{3,7},... | collective-permute-start | bytes 147464 | tf_op jit(solution)/shard_map/ppermute | solution.py:130
  33.8 1.6 %collective-permute-done.11 = bf16[8,3072]{1,0:T(8,128)(2,1)S(1)} collective-permute-done((bf16[8,3072]{1,0:T(8,128)(2,1)S(1)}, bf16[8,3072]{1,0:T(8,128)(2,1)S(1)}, u32[]{:S(2)}, u32[]{:S(2)}) %collective-permute-start.11) | collective-permute-done | bytes 49184 | tf_op jit(solution)/shard_map/ppermute | solution.py:130
  35.4 1.6 %collective-permute-done.13 = bf16[8,3072]{1,0:T(8,128)(2,1)S(1)} collective-permute-done((bf16[8,3072]{1,0:T(8,128)(2,1)S(1)}, bf16[8,3072]{1,0:T(8,128)(2,1)S(1)}, u32[]{:S(2)}, u32[]{:S(2)}) %collective-permute-start.13) | collective-permute-done | bytes 49184 | tf_op jit(solution)/shard_map/ppermute | solution.py:130
  37.0 0.8 %combine.1 = bf16[16,3072]{1,0:T(8,128)(2,1)} custom-call(bf16[32,16]{1,0:T(8,128)(2,1)S(1)} %weigh.1.comb_ref, bf16[32,3072]{1,0:T(8,128)(2,1)S(1)} %pad_maximum_fusion.2.results_ref), custom_call_target="tpu_custom_call" | custom-call | tf_op jit(solution)/shard_map/combine/pallas_call | solution.py:195
  (48 shorter events, 1.3 us)
Async XLA Ops:
  0.0 15.1 %copy-start.3 = (s32[16,2]{0,1:T(2,128)S(1)}, s32[16,2]{0,1:T(2,128)}, u32[]{:S(2)}) copy-start(s32[16,2]{0,1:T(2,128)} %param.7) | copy-start | bytes 388
  0.0 15.1 %copy-start.4 = (bf16[16,2]{0,1:T(2,128)(2,1)S(1)}, bf16[16,2]{0,1:T(2,128)(2,1)}, u32[]{:S(2)}) copy-start(bf16[16,2]{0,1:T(2,128)(2,1)} %param.8) | copy-start | bytes 196
  0.0 17.7 %copy-start = (bf16[1,3072,2048]{2,1,0:T(8,128)(2,1)S(1)}, bf16[1,3072,2048]{2,1,0:T(8,128)(2,1)}, u32[]{:S(2)}) copy-start(bf16[1,3072,2048]{2,1,0:T(8,128)(2,1)} %param.9) | copy-start | bytes 37748740
  0.0 17.7 %copy-start.1 = (bf16[1,3072,2048]{2,1,0:T(8,128)(2,1)S(1)}, bf16[1,3072,2048]{2,1,0:T(8,128)(2,1)}, u32[]{:S(2)}) copy-start(bf16[1,3072,2048]{2,1,0:T(8,128)(2,1)} %param.10) | copy-start | bytes 37748740
  0.0 17.8 %copy-start.2 = (bf16[1,2048,3072]{2,1,0:T(8,128)(2,1)S(1)}, bf16[1,2048,3072]{2,1,0:T(8,128)(2,1)}, u32[]{:S(2)}) copy-start(bf16[1,2048,3072]{2,1,0:T(8,128)(2,1)} %param.11) | copy-start | bytes 37748740
  1.3 7.2 %collective-permute-start = (bf16[8,3072]{1,0:T(8,128)(2,1)S(1)}, bf16[8,3072]{1,0:T(8,128)(2,1)S(1)}, u32[]{:S(2)}, u32[]{:S(2)}) collective-permute-start(bf16[8,3072]{1,0:T(8,128)(2,1)S(1)} %get-tuple-element.41), channel_id=1, source_target_pairs={{0,4},{2,6},{4,0},{6,2},{8,12},{10,14},{12,8},{14,10},{1,5},{3,7},... | collective-permute-start | bytes 147464 | tf_op jit(solution)/shard_map/ppermute | solution.py:130
  4.4 6.5 %collective-permute-start.1 = (bf16[8,3072]{1,0:T(8,128)(2,1)S(1)}, bf16[8,3072]{1,0:T(8,128)(2,1)S(1)}, u32[]{:S(2)}, u32[]{:S(2)}) collective-permute-start(bf16[8,3072]{1,0:T(8,128)(2,1)S(1)} %get-tuple-element.40), channel_id=1, source_target_pairs={{0,12},{2,14},{4,8},{6,10},{8,4},{10,6},{12,0},{14,2},{1,13},{3,15... | collective-permute-start | bytes 147464 | tf_op jit(solution)/shard_map/ppermute | solution.py:130
  6.9 5.5 %collective-permute-start.2 = (bf16[8,3072]{1,0:T(8,128)(2,1)S(1)}, bf16[8,3072]{1,0:T(8,128)(2,1)S(1)}, u32[]{:S(2)}, u32[]{:S(2)}) collective-permute-start(bf16[8,3072]{1,0:T(8,128)(2,1)S(1)} %get-tuple-element.39), channel_id=1, source_target_pairs={{0,8},{2,10},{4,12},{6,14},{8,0},{10,2},{12,4},{14,6},{1,9},{3,11}... | collective-permute-start | bytes 147464 | tf_op jit(solution)/shard_map/ppermute | solution.py:130
  7.0 6.9 %collective-permute-start.3 = (bf16[8,3072]{1,0:T(8,128)(2,1)S(1)}, bf16[8,3072]{1,0:T(8,128)(2,1)S(1)}, u32[]{:S(2)}, u32[]{:S(2)}) collective-permute-start(bf16[8,3072]{1,0:T(8,128)(2,1)S(1)} %get-tuple-element.42), channel_id=1, source_target_pairs={{0,2},{2,0},{4,6},{6,4},{8,10},{10,8},{12,14},{14,12},{1,3},{3,1},... | collective-permute-start | bytes 147464 | tf_op jit(solution)/shard_map/ppermute | solution.py:133
  8.5 5.5 %collective-permute-start.4 = (bf16[8,3072]{1,0:T(8,128)(2,1)S(1)}, bf16[8,3072]{1,0:T(8,128)(2,1)S(1)}, u32[]{:S(2)}, u32[]{:S(2)}) collective-permute-start(bf16[8,3072]{1,0:T(8,128)(2,1)S(1)} %collective-permute-done), channel_id=1, source_target_pairs={{0,2},{2,0},{4,6},{6,4},{8,10},{10,8},{12,14},{14,12},{1,3},{3,1},... | collective-permute-start | bytes 147464 | tf_op jit(solution)/shard_map/ppermute | solution.py:133
  10.9 4.1 %collective-permute-start.5 = (bf16[8,3072]{1,0:T(8,128)(2,1)S(1)}, bf16[8,3072]{1,0:T(8,128)(2,1)S(1)}, u32[]{:S(2)}, u32[]{:S(2)}) collective-permute-start(bf16[8,3072]{1,0:T(8,128)(2,1)S(1)} %collective-permute-done.1), channel_id=1, source_target_pairs={{0,2},{2,0},{4,6},{6,4},{8,10},{10,8},{12,14},{14,12},{1,3},{3,1},... | collective-permute-start | bytes 147464 | tf_op jit(solution)/shard_map/ppermute | solution.py:133
  12.4 4.1 %collective-permute-start.6 = (bf16[8,3072]{1,0:T(8,128)(2,1)S(1)}, bf16[8,3072]{1,0:T(8,128)(2,1)S(1)}, u32[]{:S(2)}, u32[]{:S(2)}) collective-permute-start(bf16[8,3072]{1,0:T(8,128)(2,1)S(1)} %collective-permute-done.2), channel_id=1, source_target_pairs={{0,2},{2,0},{4,6},{6,4},{8,10},{10,8},{12,14},{14,12},{1,3},{3,1},... | collective-permute-start | bytes 147464 | tf_op jit(solution)/shard_map/ppermute | solution.py:133
  15.0 1.7 %collective-permute-start.7 = (bf16[56,3072]{1,0:T(8,128)(2,1)S(1)}, bf16[56,3072]{1,0:T(8,128)(2,1)S(1)}, u32[]{:S(2)}, u32[]{:S(2)}) collective-permute-start(bf16[56,3072]{1,0:T(8,128)(2,1)S(1)} %get-tuple-element.43), channel_id=1, source_target_pairs={{0,1},{1,0},{2,3},{3,2},{4,5},{5,4},{6,7},{7,6},{8,9},{9,8},{10,11... | collective-permute-start | bytes 1032200 | tf_op jit(solution)/shard_map/ppermute | solution.py:133
  16.5 1.2 %collective-permute-start.8 = (bf16[8,3072]{1,0:T(8,128)(2,1)S(1)}, bf16[8,3072]{1,0:T(8,128)(2,1)S(1)}, u32[]{:S(2)}, u32[]{:S(2)}) collective-permute-start(bf16[8,3072]{1,0:T(8,128)(2,1)S(1)} %collective-permute-done.6), channel_id=1, source_target_pairs={{0,1},{1,0},{2,3},{3,2},{4,5},{5,4},{6,7},{7,6},{8,9},{9,8},{10,11... | collective-permute-start | bytes 147464 | tf_op jit(solution)/shard_map/ppermute | solution.py:133
  23.2 1.5 %collective-permute-start.9 = (bf16[32,3072]{1,0:T(8,128)(2,1)S(1)}, bf16[32,3072]{1,0:T(8,128)(2,1)S(1)}, u32[]{:S(2)}, u32[]{:S(2)}) collective-permute-start(bf16[32,3072]{1,0:T(8,128)(2,1)S(1)} %pad_maximum_fusion), channel_id=1, source_target_pairs={{0,1},{1,0},{2,3},{3,2},{4,5},{5,4},{6,7},{7,6},{8,9},{9,8},{10,11... | collective-permute-start | bytes 589832 | tf_op jit(solution)/shard_map/ppermute | solution.py:133
  23.4 3.4 %collective-permute-start.14 = (bf16[32,3072]{1,0:T(8,128)(2,1)S(1)}, bf16[32,3072]{1,0:T(8,128)(2,1)S(1)}, u32[]{:S(2)}, u32[]{:S(2)}) collective-permute-start(bf16[32,3072]{1,0:T(8,128)(2,1)S(1)} %pad_maximum_fusion.1), channel_id=1, source_target_pairs={{0,1},{1,0},{2,3},{3,2},{4,5},{5,4},{6,7},{7,6},{8,9},{9,8},{10,11... | collective-permute-start | bytes 589832 | tf_op jit(solution)/shard_map/ppermute | solution.py:133
  24.8 4.4 %collective-permute-start.10 = (bf16[8,3072]{1,0:T(8,128)(2,1)S(1)}, bf16[8,3072]{1,0:T(8,128)(2,1)S(1)}, u32[]{:S(2)}, u32[]{:S(2)}) collective-permute-start(bf16[8,3072]{1,0:T(8,128)(2,1)S(1)} %get-tuple-element.14), channel_id=1, source_target_pairs={{0,2},{2,0},{4,6},{6,4},{8,10},{10,8},{12,14},{14,12},{1,3},{3,1},... | collective-permute-start | bytes 147464 | tf_op jit(solution)/shard_map/ppermute | solution.py:133
  26.3 5.0 %collective-permute-start.12 = (bf16[8,3072]{1,0:T(8,128)(2,1)S(1)}, bf16[8,3072]{1,0:T(8,128)(2,1)S(1)}, u32[]{:S(2)}, u32[]{:S(2)}) collective-permute-start(bf16[8,3072]{1,0:T(8,128)(2,1)S(1)} %get-tuple-element.16), channel_id=1, source_target_pairs={{0,2},{2,0},{4,6},{6,4},{8,10},{10,8},{12,14},{14,12},{1,3},{3,1},... | collective-permute-start | bytes 147464 | tf_op jit(solution)/shard_map/ppermute | solution.py:133
  26.9 5.5 %collective-permute-start.15 = (bf16[8,3072]{1,0:T(8,128)(2,1)S(1)}, bf16[8,3072]{1,0:T(8,128)(2,1)S(1)}, u32[]{:S(2)}, u32[]{:S(2)}) collective-permute-start(bf16[8,3072]{1,0:T(8,128)(2,1)S(1)} %get-tuple-element.18), channel_id=1, source_target_pairs={{0,2},{2,0},{4,6},{6,4},{8,10},{10,8},{12,14},{14,12},{1,3},{3,1},... | collective-permute-start | bytes 147464 | tf_op jit(solution)/shard_map/ppermute | solution.py:133
  28.5 5.3 %collective-permute-start.17 = (bf16[8,3072]{1,0:T(8,128)(2,1)S(1)}, bf16[8,3072]{1,0:T(8,128)(2,1)S(1)}, u32[]{:S(2)}, u32[]{:S(2)}) collective-permute-start(bf16[8,3072]{1,0:T(8,128)(2,1)S(1)} %get-tuple-element.20), channel_id=1, source_target_pairs={{0,2},{2,0},{4,6},{6,4},{8,10},{10,8},{12,14},{14,12},{1,3},{3,1},... | collective-permute-start | bytes 147464 | tf_op jit(solution)/shard_map/ppermute | solution.py:133
  29.2 6.2 %collective-permute-start.11 = (bf16[8,3072]{1,0:T(8,128)(2,1)S(1)}, bf16[8,3072]{1,0:T(8,128)(2,1)S(1)}, u32[]{:S(2)}, u32[]{:S(2)}) collective-permute-start(bf16[8,3072]{1,0:T(8,128)(2,1)S(1)} %add_convert_fusion.5), channel_id=1, source_target_pairs={{0,12},{2,14},{4,8},{6,10},{8,4},{10,6},{12,0},{14,2},{1,13},{3,15... | collective-permute-start | bytes 147464 | tf_op jit(solution)/shard_map/ppermute | solution.py:130
  31.3 5.6 %collective-permute-start.13 = (bf16[8,3072]{1,0:T(8,128)(2,1)S(1)}, bf16[8,3072]{1,0:T(8,128)(2,1)S(1)}, u32[]{:S(2)}, u32[]{:S(2)}) collective-permute-start(bf16[8,3072]{1,0:T(8,128)(2,1)S(1)} %add_convert_fusion.4), channel_id=1, source_target_pairs={{0,8},{2,10},{4,12},{6,14},{8,0},{10,2},{12,4},{14,6},{1,9},{3,11}... | collective-permute-start | bytes 147464 | tf_op jit(solution)/shard_map/ppermute | solution.py:130
  32.5 4.5 %collective-permute-start.16 = (bf16[8,3072]{1,0:T(8,128)(2,1)S(1)}, bf16[8,3072]{1,0:T(8,128)(2,1)S(1)}, u32[]{:S(2)}, u32[]{:S(2)}) collective-permute-start(bf16[8,3072]{1,0:T(8,128)(2,1)S(1)} %add_convert_fusion.3), channel_id=1, source_target_pairs={{0,4},{2,6},{4,0},{6,2},{8,12},{10,14},{12,8},{14,10},{1,5},{3,7},... | collective-permute-start | bytes 147464 | tf_op jit(solution)/shard_map/ppermute | solution.py:130
